TPU v7x, 32 devices: a whole 2x2x4 slice. The times are simulated.
32 devices in a mesh: groups: 2 (over y), ex: 16 (over z, x, core).
Axes of the slice: x: 2, y: 2, z: 4, core: 2. Of those that a mesh axis runs over, the one named last changes fastest.
Arguments:
- gradient_mantissas: bfloat16 [4096, 4096], P(('groups', 'ex')), parts along dimension 0, may hold values from -6 to 6
- gradient_exponents: int32 [4096, 32], P(('groups', 'ex')), parts along dimension 0, may hold values from -2 to 2
- routes: int32 [4096, 8], P(('groups', 'ex')), parts along dimension 0, may hold values from 0 to 15, all different within a row; in each aligned block of 128 rows (0 to 127, 128 to 255, ...) at most 80 rows name the same one
- routing_weight: bfloat16 [4096, 8], P(('groups', 'ex')), parts along dimension 0, may hold values from 0.019897461 to 0.5
- stored_hidden_rows: bfloat16 [32, 16, 80, 768], P(('groups', 'ex')), parts along dimension 0, may hold values from -0.29882812 to 0.29882812
- frozen_down_weight: bfloat16 [16, 768, 4096], P('ex'), may hold values from -0.21875 to 0.21875
- adapter_first_factor: bfloat16 [768, 32], replicated, may hold values from -0.21875 to 0.21875
- adapter_second_factor: bfloat16 [32, 4096], replicated, may hold values from -0.44921875 to 0.44921875
- expert_adapter_gate: float32 [16], replicated, may hold values from 0.25 to 1
Outputs:
- hidden_gradient: bfloat16 [32, 16, 80, 768], P(('groups', 'ex')), parts along dimension 0
- routing_gradient: float32 [4096, 8], P(('groups', 'ex')), parts along dimension 0
- first_factor_gradient: float32 [1536, 32], P('groups'), parts along dimension 0
- second_factor_gradient: float32 [64, 4096], P('groups'), parts along dimension 0
- gate_grad: float32 [32], P('groups'), parts along dimension 0
There are 2 independent parts, one for each index of `groups`. A program takes and returns all parts, laid end to end along the dimension named above; an argument that names none is the same for every part. Nothing has to cross between parts.
Inputs may be any that keep to these rules, and one draw needn't show every extreme that they name: `routes`: each token names 8 different experts; the 128 tokens of one device name one expert at most 80 times.
All inputs are finite; a program needn't handle non-finite values.
Results may differ from a plain program's by a relative error of at most 0.0052.
Values may be sent and summed in bfloat16 or wider, within the bound.
No kernel may reach another device: no remote copies, remote signals or barrier semaphores. Data moves between devices by JAX's collectives and lax.ppermute only.
A program may use at most 128 MiB of HBM per device.

v0:
```python
import jax
import jax.numpy as jnp
from jax import lax
from jax.sharding import PartitionSpec as P


def block_scale(gradient_exponents):
    scaling = jnp.zeros(gradient_exponents.shape, jnp.float32)
    for exponent in range(-2, 3):
        scaling = scaling + jnp.where(
            gradient_exponents == exponent, jnp.float32(2.0**exponent), jnp.float32(0.0)
        )
    return scaling


def expand_grad(gradient_mantissas, gradient_exponents):
    blocks = gradient_exponents.shape[1]
    scaling = block_scale(gradient_exponents)
    widened = (
        gradient_mantissas.astype(jnp.float32).reshape(gradient_mantissas.shape[0], blocks, -1)
        * scaling[:, :, None]
    )
    return widened.reshape(gradient_mantissas.shape).astype(jnp.bfloat16)


def slot_table(route_block, experts, capacity):
    flat_routes = route_block.reshape(-1)
    onehot = (flat_routes[:, None] == jnp.arange(experts, dtype=jnp.int32)[None, :]).astype(
        jnp.int32
    )
    running = jnp.cumsum(onehot, axis=0) - 1
    slot_index = jnp.sum(running * onehot, axis=1)
    return flat_routes * capacity + slot_index


def reduced_projection(current_row_block, adapter_second_factor):
    return lax.dot_general(
        current_row_block,
        adapter_second_factor,
        (((1,), (1,)), ((), ())),
        preferred_element_type=jnp.float32,
    ).astype(jnp.bfloat16)


def per_expert_terms(
    current_row_block,
    routing_share,
    reduced_input,
    stored_rows,
    expert_down_matrix,
    adapter_first_factor,
    expert_gate_value,
):
    contract_dimensions = (((1,), (1,)), ((), ()))
    base_term = lax.dot_general(
        current_row_block,
        expert_down_matrix,
        contract_dimensions,
        preferred_element_type=jnp.float32,
    )
    adapter_side_term = lax.dot_general(
        reduced_input, adapter_first_factor, contract_dimensions, preferred_element_type=jnp.float32
    )
    combined = base_term + expert_gate_value * adapter_side_term
    share_col = routing_share.astype(jnp.float32)[:, None]
    hidden_gradient = (share_col * combined).astype(jnp.bfloat16)
    weight_grad = jnp.sum(stored_rows.astype(jnp.float32) * combined, axis=1)
    low_float = reduced_input.astype(jnp.float32)
    rows_dims = (((0,), (0,)), ((), ()))
    pushed = (expert_gate_value * share_col * low_float).astype(jnp.bfloat16)
    a_grad = lax.dot_general(stored_rows, pushed, rows_dims, preferred_element_type=jnp.float32)
    reduced_rank_rows = jnp.dot(
        stored_rows, adapter_first_factor, preferred_element_type=jnp.float32
    )
    pulled = (expert_gate_value * share_col * reduced_rank_rows).astype(jnp.bfloat16)
    b_grad = lax.dot_general(
        pulled, current_row_block, rows_dims, preferred_element_type=jnp.float32
    )
    gate_term = jnp.sum(
        routing_share.astype(jnp.float32) * jnp.sum(reduced_rank_rows * low_float, axis=1)
    )
    return (hidden_gradient, weight_grad, a_grad, b_grad, gate_term)


def body(
    gradient_mantissas,
    gradient_exponents,
    routes,
    routing_weight,
    stored_hidden_rows,
    frozen_down_weight,
    adapter_first_factor,
    adapter_second_factor,
    expert_adapter_gate,
):
    experts = expert_adapter_gate.shape[0]
    sources = stored_hidden_rows.shape[1]
    capacity = stored_hidden_rows.shape[2]
    hidden_width = stored_hidden_rows.shape[3]
    tok_count, top_count = routes.shape
    slots_all = experts * capacity
    grad_out = expand_grad(gradient_mantissas, gradient_exponents)
    dest = slot_table(routes, experts, capacity)
    token_ids = jnp.arange(tok_count * top_count, dtype=jnp.int32) // top_count
    token_of = jnp.zeros((slots_all,), jnp.int32).at[dest].set(token_ids)
    share_send = (
        jnp.zeros((slots_all,), jnp.bfloat16)
        .at[dest]
        .set(routing_weight.reshape(-1))
        .reshape(experts, capacity)
    )
    row_send = grad_out[token_of].reshape(experts, capacity, -1)
    received_rows = sources * capacity
    token_low = reduced_projection(grad_out, adapter_second_factor)
    low_send = token_low[token_of].reshape(experts, capacity, -1)
    row_recv, share_recv, low_recv = (
        lax.all_to_all(row_send, "ex", split_axis=0, concat_axis=0, tiled=True),
        lax.all_to_all(share_send, "ex", split_axis=0, concat_axis=0, tiled=True),
        lax.all_to_all(low_send, "ex", split_axis=0, concat_axis=0, tiled=True),
    )
    current_row_block = row_recv.reshape(received_rows, -1)
    reduced_input = low_recv.reshape(received_rows, -1)
    routing_share = share_recv.reshape(received_rows)
    stored_rows = stored_hidden_rows.reshape(received_rows, hidden_width)
    expert_down_matrix = frozen_down_weight[0]
    own_index = lax.axis_index("ex")
    expert_gate_value = lax.dynamic_index_in_dim(expert_adapter_gate, own_index, 0, keepdims=False)
    hidden_gradient, weight_grad, a_grad, b_grad, gate_term = per_expert_terms(
        current_row_block,
        routing_share,
        reduced_input,
        stored_rows,
        expert_down_matrix,
        adapter_first_factor,
        expert_gate_value,
    )
    returned = lax.all_to_all(
        weight_grad.reshape(sources, capacity), "ex", split_axis=0, concat_axis=0, tiled=True
    )
    routing_gradient = returned.reshape(-1)[dest].reshape(tok_count, top_count)
    own_gate = (jnp.arange(experts, dtype=jnp.int32) == own_index).astype(jnp.float32) * gate_term
    a_total, b_total, gate_total = lax.psum((a_grad, b_grad, own_gate), "ex")
    hidden_out = hidden_gradient.reshape(1, sources, capacity, hidden_width)
    return (hidden_out, routing_gradient, a_total, b_total, gate_total)


def solution(mesh):
    return jax.shard_map(
        body,
        mesh=mesh,
        in_specs=(
            P(("groups", "ex"), None),
            P(("groups", "ex"), None),
            P(("groups", "ex"), None),
            P(("groups", "ex"), None),
            P(("groups", "ex"), None, None, None),
            P("ex", None, None),
            P(),
            P(),
            P(),
        ),
        out_specs=(
            P(("groups", "ex"), None, None, None),
            P(("groups", "ex"), None),
            P("groups", None),
            P("groups", None),
            P("groups"),
        ),
        check_vma=False,
    )
```

profile of v0, /device:TPU:0, one launch (start us, length us, event | category | flops | bytes accessed | tf_op | source)
XLA Modules:
  0.0 398.2 jit_solution(6745933920017200718)
XLA Ops:
  7.2 0.9 copy.41
  8.3 0.7 broadcast_multiply_fusion.1
  9.0 4.5 %reduce-window.6 = s32[16,8,128]{2,1,0:T(8,128)S(1)} reduce-window(s32[16,8,128]{2,1,0:T(8,128)S(1)} %fusion.10, s32[]{:T(128)} %constant.21.clone.1), window={size=1x1x128 pad=0_0x0_0x127_0}, to_apply=%region_0.1 | reduce-window | flops 2080768 | bytes 131076 | tf_op jit(solution)/shard_map/reduce-window
  14.1 0.8 copy.45
  15.1 7.6 %scatter_custom_fusion = bf16[1280]{0:T(1024)(128)(2,1)S(1)} fusion(s32[1024]{0:T(1024)S(1)} %bitcast.61, bf16[1024]{0:T(1024)(128)(2,1)S(1)} %reshape.165, bf16[]{:T(256)} %constant.19.clone.1), kind=kCustom, calls=%fused_computation.47 | custom fusion | bytes 2562 | tf_op jit(solution)/shard_map/scatter | solution.py:109
  22.6 0.7 all_to_all.24
  23.3 7.4 %all-to-all-start = ((bf16[16,1,80]{2,1,0:T(2,128)(2,1)}), bf16[16,1,80]{2,1,0:T(2,128)(2,1)S(1)}, u32[]{:S(2)}, u32[]{:S(2)}) async-start(bf16[16,1,80]{2,1,0:T(2,128)(2,1)} %all_to_all.24), calls=%async_computation | async-start | bytes 16384 | tf_op jit(solution)/shard_map/all_to_all | solution.py:118
  30.7 4.3 %scatter_custom_fusion.1 = s32[1280]{0:T(1024)S(1)} fusion(s32[1024]{0:T(1024)S(1)} %bitcast.62, s32[1024]{0:T(1024)S(1)} %add_select_fusion, s32[]{:T(128)} %constant.21.clone.1), kind=kCustom, calls=%fused_computation.42 | custom fusion | bytes 5124 | tf_op jit(solution)/shard_map/scatter | solution.py:105
  35.0 0.7 select_add_fusion
  36.5 1.8 fusion.5
  39.0 2.8 gather_fusion.1
  41.8 0.8 copy.49
  42.6 6.0 %all-to-all-start.2 = ((bf16[16,80,32]{1,2,0:T(8,128)(2,1)}), bf16[16,80,32]{1,2,0:T(8,128)(2,1)S(1)}, u32[]{:S(2)}, u32[]{:S(2)}) async-start(bf16[16,80,32]{1,2,0:T(8,128)(2,1)} %copy.49), calls=%async_computation.2 | async-start | bytes 262144 | tf_op jit(solution)/shard_map/all_to_all | solution.py:119
  48.6 8.2 %gather_fusion = bf16[1280,4096]{1,0:T(8,128)(2,1)} fusion(bf16[128,4096]{1,0:T(8,128)(2,1)S(1)} %fusion.5, s32[2048]{0:T(1024)S(1)} %pad_clamp_fusion), kind=kCustom, calls=%fused_computation | custom fusion | bytes 20976640 | tf_op jit(solution)/shard_map/gather | solution.py:112
  56.8 6.2 %all-to-all-start.1 = ((bf16[16,80,4096]{2,1,0:T(8,128)(2,1)}), bf16[16,80,4096]{2,1,0:T(8,128)(2,1)}, u32[]{:S(2)}, u32[]{:S(2)}) async-start(bf16[16,80,4096]{2,1,0:T(8,128)(2,1)} %bitcast.52), calls=%async_computation.1 | async-start | bytes 20971520 | tf_op jit(solution)/shard_map/all_to_all | solution.py:117
  64.1 0.7 multiply_reduce_fusion.1
  65.0 1.3 fusion.11
  66.6 0.7 compare_select_fusion.2
  67.9 1.1 convolution_bitcast_fusion
  69.0 3.2 convolution_multiply_fusion
  72.2 178.1 %all-to-all-done.1 = bf16[16,80,4096]{2,1,0:T(8,128)(2,1)} async-done(((bf16[16,80,4096]{2,1,0:T(8,128)(2,1)}), bf16[16,80,4096]{2,1,0:T(8,128)(2,1)}, u32[]{:S(2)}, u32[]{:S(2)}) %all-to-all-start.1) | async-done | bytes 10485792 | tf_op jit(solution)/shard_map/all_to_all | solution.py:117
  250.3 6.7 %fusion.6 = f32[32,4096]{1,0:T(8,128)} fusion(bf16[1280,4096]{1,0:T(8,128)(2,1)} %bitcast.5, f32[1280,32]{0,1:T(8,128)S(1)} %get-tuple-element.28, f32[1280]{0:T(1024)S(1)} %broadcast_multiply_fusion), kind=kOutput, calls=%fused_computation.18 | convolution fusion | flops 335626240 | bytes 11179008 | tf_op jit(solution)/shard_map/dot_general | solution.py:76
  257.0 14.8 %multiply_reduce_fusion = (f32[1280]{0:T(1024)S(1)}, bf16[1280,768]{1,0:T(8,128)(2,1)}) fusion(bf16[1,16,80,768]{3,2,1,0:T(8,128)(2,1)S(1)} %copy-done.1, f32[1280]{0:T(1024)S(1)} %reshape.136, f32[1280,768]{1,0:T(8,128)} %convolution_multiply_fusion, bf16[1280,4096]{1,0:T(8,128)(2,1)} %bitcast.5, bf16[1,768,4096]{2,1,0:T(8,128)(2,1)} %param.14), kind=kOutput, calls=%fused_computation.9 | convolution fusion | flops 8058960896 | bytes 24651776 | tf_op jit(solution)/shard_map/dot_general | solution.py:55
  271.7 0.7 all_to_all.22
  272.4 44.9 %all-to-all-start.3 = ((f32[16,1,80]{2,1,0:T(1,128)}), f32[16,1,80]{2,1,0:T(1,128)S(1)}, u32[]{:S(2)}, u32[]{:S(2)}) async-start(f32[16,1,80]{2,1,0:T(1,128)} %all_to_all.22), calls=%async_computation.3 | async-start | bytes 16384 | tf_op jit(solution)/shard_map/all_to_all | solution.py:137
  317.4 34.4 %psum.23 = f32[16]{0:T(128)} all-reduce(f32[16]{0:T(128)S(1)} %compare_select_fusion.2), channel_id=1, replica_groups=mesh['groups'=2,'ex'=16] {'ex'}, use_global_device_ids=true, to_apply=%region_10.11 | all-reduce | flops 16 | bytes 128 | tf_op jit(solution)/shard_map/psum | solution.py:142
  352.2 0.7 reduce.10
  353.0 6.1 %gather_fusion.2 = f32[1024]{0:T(1024)S(1)} fusion(f32[1280]{0:T(1024)S(1)} %reshape.134, s32[1024]{0:T(1024)S(1)} %broadcast_clamp_fusion), kind=kCustom, calls=%fused_computation.2 | custom fusion | bytes 12288 | tf_op jit(solution)/shard_map/gather | solution.py:140
  359.2 0.7 copy.52
  359.9 28.1 %all-reduce.3.cloned.1.call-done = (f32[768,32]{0,1:T(8,128)}, f32[32,4096]{1,0:T(8,128)}) async-done(((f32[768,32]{0,1:T(8,128)}, f32[32,4096]{1,0:T(8,128)}), (f32[768,32]{0,1:T(8,128)}, f32[32,4096]{1,0:T(8,128)})) %all-reduce.3.cloned.1.call-update) | async-done | bytes 622608 | tf_op jit(solution)/shard_map/psum | solution.py:142
  388.0 1.5 copy.59
  389.5 1.9 copy.60
  (49 shorter events, 5.1 us)
Async XLA Ops:
  7.2 31.2 %copy-start = (bf16[32,4096]{1,0:T(8,128)(2,1)S(1)}, bf16[32,4096]{1,0:T(8,128)(2,1)}, u32[]{:S(2)}) copy-start(bf16[32,4096]{1,0:T(8,128)(2,1)} %param.16) | copy-start | bytes 786436
  7.2 29.3 %copy-start.2 = (bf16[128,4096]{1,0:T(8,128)(2,1)S(1)}, bf16[128,4096]{1,0:T(8,128)(2,1)}, u32[]{:S(2)}) copy-start(bf16[128,4096]{1,0:T(8,128)(2,1)} %param.9) | copy-start | bytes 3145732
  23.3 19.2 %all-to-all-start = ((bf16[16,1,80]{2,1,0:T(2,128)(2,1)}), bf16[16,1,80]{2,1,0:T(2,128)(2,1)S(1)}, u32[]{:S(2)}, u32[]{:S(2)}) async-start(bf16[16,1,80]{2,1,0:T(2,128)(2,1)} %all_to_all.24), calls=%async_computation | async-start | bytes 16384 | tf_op jit(solution)/shard_map/all_to_all | solution.py:118
  42.6 14.2 %all-to-all-start.2 = ((bf16[16,80,32]{1,2,0:T(8,128)(2,1)}), bf16[16,80,32]{1,2,0:T(8,128)(2,1)S(1)}, u32[]{:S(2)}, u32[]{:S(2)}) async-start(bf16[16,80,32]{1,2,0:T(8,128)(2,1)} %copy.49), calls=%async_computation.2 | async-start | bytes 262144 | tf_op jit(solution)/shard_map/all_to_all | solution.py:119
  56.8 6.5 %copy-start.4 = (f32[16]{0:T(128)S(1)}, f32[16]{0:T(128)}, u32[]{:S(2)}) copy-start(f32[16]{0:T(128)} %param.17) | copy-start | bytes 196
  56.8 7.3 %copy-start.1 = (bf16[1,16,80,768]{3,2,1,0:T(8,128)(2,1)S(1)}, bf16[1,16,80,768]{3,2,1,0:T(8,128)(2,1)}, u32[]{:S(2)}) copy-start(bf16[1,16,80,768]{3,2,1,0:T(8,128)(2,1)} %param.13) | copy-start | bytes 5898244
  56.8 7.3 %copy-start.3 = (bf16[768,32]{0,1:T(8,128)(2,1)S(1)}, bf16[768,32]{0,1:T(8,128)(2,1)}, u32[]{:S(2)}) copy-start(bf16[768,32]{0,1:T(8,128)(2,1)} %param.15) | copy-start | bytes 147460
  56.8 193.4 %all-to-all-start.1 = ((bf16[16,80,4096]{2,1,0:T(8,128)(2,1)}), bf16[16,80,4096]{2,1,0:T(8,128)(2,1)}, u32[]{:S(2)}, u32[]{:S(2)}) async-start(bf16[16,80,4096]{2,1,0:T(8,128)(2,1)} %bitcast.52), calls=%async_computation.1 | async-start | bytes 20971520 | tf_op jit(solution)/shard_map/all_to_all | solution.py:117
  63.0 324.9 %all-reduce.3.cloned.1.call-start = ((), (), s32[]{:S(2)}) async-start(), calls=%async_computation.4 | async-start | bytes 1245184 | tf_op jit(solution)/shard_map/psum | solution.py:142
  272.4 79.3 %all-to-all-start.3 = ((f32[16,1,80]{2,1,0:T(1,128)}), f32[16,1,80]{2,1,0:T(1,128)S(1)}, u32[]{:S(2)}, u32[]{:S(2)}) async-start(f32[16,1,80]{2,1,0:T(1,128)} %all_to_all.22), calls=%async_computation.3 | async-start | bytes 16384 | tf_op jit(solution)/shard_map/all_to_all | solution.py:137
Sparse Core Ops, SparseCore 0:
  257.1 130.8 all-reduce.2
where the time goes:
time: 399 us; the launch traced here: 398 us
  waiting for transfers between devices  206 us (52%)
  starting transfers between devices  64.7 us (16%)
  local copies, waits for them, and re-layouts  40.5 us (10%)
  blocking collectives  34.4 us (9%)
  matrix products  27 us (7%)
  between operations  14.3 us (4%)
  other arithmetic  11.2 us (3%)
    all_to_all x1, waiting for transfers between devices, body(): lax.all_to_all(row_send, 'ex', split_axis=0, concat_axis=0, tiled=True)  178 us
    all_to_all x1, starting transfers between devices, body(): lax.all_to_all(weight_grad.reshape(sources, capacity), 'ex', split_axis=0...  44.9 us
    psum x1, blocking collectives, body(): a_total, b_total, gate_total = lax.psum((a_grad, b_grad, own_gate), 'ex')  34.4 us
    psum x1, waiting for transfers between devices, body(): a_total, b_total, gate_total = lax.psum((a_grad, b_grad, own_gate), 'ex')  28.1 us
    dot_general x1, matrix products, per_expert_terms(): lax.dot_general(current_row_block, expert_down_matrix, contract_dimension...  14.8 us
    gather x1, local copies, waits for them, and re-layouts, body(): row_send = grad_out[token_of].reshape(experts, capacity, -1)  8.22 us
  transfers between devices with their start and end apart: 5, of which 2 were waited for; matrix products, arithmetic and copies ran while one was open for 13% of the time, Pallas kernels for 0%

commit v1 on v0

--- a/solution.py
+++ b/solution.py
@@ -1,7 +1,470 @@
+import functools
+
 import jax
 import jax.numpy as jnp
 from jax import lax
+from jax.experimental import pallas as pl
+from jax.experimental.pallas import tpu as pltpu
 from jax.sharding import PartitionSpec as P
+
+F32, BF16 = jnp.float32, jnp.bfloat16
+VMEM_LIMIT = 40 * 1024 * 1024
+ROWS = (((0,), (0,)), ((), ()))
+LANES = (((1,), (1,)), ((), ()))
+PLAIN = (((1,), (0,)), ((), ()))
+
+
+def dot(a, b, dims):
+    return lax.dot_general(a, b, dims, preferred_element_type=F32)
+
+
+def params():
+    return pltpu.CompilerParams(vmem_limit_bytes=VMEM_LIMIT)
+
+
+def whole(count):
+    return [pl.BlockSpec(memory_space=pltpu.VMEM)] * count
+
+
+def scale_kernel(mantissa_ref, exponent_ref, low_ref, high_ref):
+    exponents = exponent_ref[...]
+    scale = jnp.zeros(exponents.shape, F32)
+    for power in range(-2, 3):
+        scale = scale + jnp.where(exponents == power, F32(2.0**power), F32(0.0))
+    columns = scale.T
+    half = low_ref.shape[0]
+    width = mantissa_ref.shape[1] // exponents.shape[0]
+    for block in range(exponents.shape[0]):
+        lanes = slice(block * width, (block + 1) * width)
+        piece = (mantissa_ref[:, lanes].astype(F32) * columns[:, block : block + 1]).astype(BF16)
+        low_ref[:, lanes] = piece[:half]
+        high_ref[:, lanes] = piece[half:]
+
+
+def share_table(routes, weights, experts):
+    expert = lax.broadcasted_iota(jnp.int32, (experts, routes.shape[1]), 0)
+    table = jnp.zeros(expert.shape, F32)
+    for k in range(routes.shape[0]):
+        table = table + jnp.where(routes[k : k + 1] == expert, weights[k : k + 1], F32(0.0))
+    return table
+
+
+def pack_kernel(
+    own_ref, low_ref, high_ref, second_ref, routes_ref, weights_ref, stored_ref, first_ref, gate_ref, out_ref
+):
+    devices, cap = stored_ref.shape[0], stored_ref.shape[1]
+    rank = second_ref.shape[0]
+    gate = gate_ref[own_ref[0]]
+    reduced = jnp.concatenate(
+        [dot(second_ref[...], low_ref[...], LANES), dot(second_ref[...], high_ref[...], LANES)], axis=1
+    ).astype(BF16)
+    table = share_table(routes_ref[...], weights_ref[...].astype(F32), devices).astype(BF16)
+    first = first_ref[...]
+    pad = jnp.zeros((rank, out_ref.shape[2] - cap), BF16)
+    for peer in range(devices):
+        out_ref[peer, 0:rank, :] = reduced
+        pulled = (gate * dot(first, stored_ref[peer], LANES)).astype(BF16)
+        out_ref[peer, rank : 2 * rank, :] = jnp.concatenate([pulled, pad], axis=1)
+        out_ref[peer, 2 * rank :, :] = table
+
+
+def slot_of(table):
+    tokens = table.shape[1]
+    earlier = lax.broadcasted_iota(jnp.int32, (tokens, tokens), 0) < lax.broadcasted_iota(
+        jnp.int32, (tokens, tokens), 1
+    )
+    taken = jnp.where(table > 0, F32(1.0), F32(0.0)).astype(BF16)
+    count = dot(taken, jnp.where(earlier, F32(1.0), F32(0.0)).astype(BF16), PLAIN)
+    return jnp.where(table > 0, count, F32(-1.0)).astype(jnp.int32)
+
+
+def take_row(table, row):
+    rows = lax.broadcasted_iota(jnp.int32, table.shape, 0)
+    return jnp.sum(jnp.where(rows == row, table, F32(0.0)), axis=0, keepdims=True)
+
+
+def xor_mask(j):
+    return ((j >> 3) & 1) | (((j >> 2) & 1) << 1) | (((j >> 1) & 1) << 2) | ((j & 1) << 3)
+
+
+def low_rank_kernel(
+    own_ref,
+    got_ref,
+    stored_ref,
+    first_ref,
+    gate_ref,
+    routes_ref,
+    weights_ref,
+    low_ref,
+    high_ref,
+    out_ref,
+    wide_ref,
+    narrow_ref,
+):
+    devices, cap = stored_ref.shape[0], stored_ref.shape[1]
+    own = own_ref[0]
+    rank = first_ref.shape[0]
+    tokens = got_ref.shape[2]
+    gate = gate_ref[own]
+    shares = jnp.concatenate(
+        [take_row(got_ref[s, 2 * rank :, :].astype(F32), own) for s in range(devices)], axis=0
+    )
+    slots = slot_of(shares)
+    place = lax.broadcasted_iota(jnp.int32, (tokens, tokens), 0)
+    total = jnp.zeros((rank, stored_ref.shape[2]), F32)
+    for s in range(devices):
+        chosen = jnp.where(place == slots[s : s + 1], F32(1.0), F32(0.0)).astype(BF16)
+        pushed = (got_ref[s, 0:rank, :].astype(F32) * shares[s : s + 1]).astype(BF16)
+        by_slot = dot(pushed, chosen[:cap], LANES).astype(BF16)
+        total = total + dot(by_slot, stored_ref[s], PLAIN)
+    gate_term = jnp.sum(total * first_ref[...].astype(F32))
+    total = gate * total
+    narrow_ref[...] = jnp.zeros(narrow_ref.shape, F32)
+    for i in range(2 * (total.shape[1] // 128)):
+        narrow_ref[i] = total[(i % 2) * 16 : (i % 2) * 16 + 16, (i // 2) * 128 : (i // 2) * 128 + 128]
+    lane = lax.broadcasted_iota(jnp.int32, (16, 128), 1)
+    row = lax.broadcasted_iota(jnp.int32, (16, 128), 0)
+    narrow_ref[devices - 1] = jnp.where((lane == own) & (row == 0), gate_term, F32(0.0))
+
+    table = share_table(routes_ref[...], weights_ref[...].astype(F32), devices)
+    mine = slot_of(table)
+    pulled = jnp.zeros((rank, tokens), F32)
+    for e in range(devices):
+        weighted = jnp.where(place == mine[e : e + 1], table[e : e + 1], F32(0.0)).astype(BF16)
+        pulled = pulled + dot(got_ref[e, rank : 2 * rank, :], weighted, PLAIN)
+    coarse = pulled.astype(BF16)
+    fine = (pulled - coarse.astype(F32)).astype(BF16)
+    both = jnp.concatenate([coarse, fine], axis=0)
+    half = low_ref.shape[0]
+    result = dot(both[:, :half], low_ref[...], PLAIN) + dot(both[:, half:], high_ref[...], PLAIN)
+    wide_ref[...] = result[:rank] + result[rank:]
+    columns = wide_ref.shape[1] // devices
+    for j in range(devices):
+        chunk = own ^ xor_mask(j)
+        for b in range(columns // 128):
+            lanes = pl.ds(pl.multiple_of(chunk * columns + b * 128, 128), 128)
+            out_ref[j, b * rank : (b + 1) * rank, :] = wide_ref[:, lanes]
+        out_ref[j, 64:80, :] = narrow_ref[chunk]
+
+
+def unpack_kernel(own_ref, got_ref, second_ref, first_ref, gate_ref, narrow_ref):
+    devices = got_ref.shape[0]
+    own = own_ref[0]
+    rank = second_ref.shape[0]
+    columns = second_ref.shape[1] // devices
+    for j in range(devices):
+        chunk = own ^ xor_mask(j)
+        for b in range(columns // 128):
+            lanes = pl.ds(pl.multiple_of(chunk * columns + b * 128, 128), 128)
+            second_ref[:, lanes] = got_ref[j, b * rank : (b + 1) * rank, :]
+        narrow_ref[chunk] = got_ref[j, 64:80, :]
+    for i in range(2 * (first_ref.shape[1] // 128)):
+        first_ref[(i % 2) * 16 : (i % 2) * 16 + 16, (i // 2) * 128 : (i // 2) * 128 + 128] = narrow_ref[i]
+    gate_ref[...] = narrow_ref[devices - 1][0:8]
+
+
+def expert_kernel(
+    place_ref,
+    gate_ref,
+    a0_ref,
+    a1_ref,
+    b0_ref,
+    b1_ref,
+    weight_ref,
+    other_weight_ref,
+    stored_ref,
+    other_stored_ref,
+    first_ref,
+    got_ref,
+    *rest,
+):
+    hidden_ref, other_hidden_ref, dots_ref, rows_ref, sem = rest[-5:]
+    step = pl.program_id(0)
+    own, is_end = place_ref[0], place_ref[1]
+    half = a0_ref.shape[0]
+    cap = stored_ref.shape[1]
+    rank = first_ref.shape[0]
+    tokens = 2 * half
+
+    @pl.when(step == 0)
+    def _():
+        def load(first_half, second_half):
+            one = pltpu.make_async_copy(first_half, rows_ref.at[0:half], sem.at[0])
+            two = pltpu.make_async_copy(second_half, rows_ref.at[half:tokens], sem.at[1])
+            one.start()
+            two.start()
+            one.wait()
+            two.wait()
+
+        @pl.when(is_end == 1)
+        def _():
+            load(a0_ref, a1_ref)
+
+        @pl.when(is_end == 0)
+        def _():
+            load(b0_ref, b1_ref)
+
+        dots_ref[...] = jnp.zeros(dots_ref.shape, F32)
+
+    def work(expert, row, weight_block, stored_block, hidden_block):
+        share = take_row(got_ref[0, 2 * rank :, :].astype(F32), expert)
+        slot = slot_of(jnp.broadcast_to(share, (8, tokens)))[0:1]
+        chosen = jnp.where(
+            lax.broadcasted_iota(jnp.int32, (cap, tokens), 0) == slot, F32(1.0), F32(0.0)
+        ).astype(BF16)
+        grad = dot(weight_block[0], rows_ref[...], LANES)
+        grad = grad + gate_ref[expert] * dot(first_ref[...], got_ref[0, 0:rank, :], ROWS)
+        by_token = dot(stored_block[0], chosen, ROWS)
+        rows = lax.broadcasted_iota(jnp.int32, dots_ref.shape, 0)
+        partial = jnp.sum(by_token * grad, axis=0, keepdims=True)
+        dots_ref[...] += jnp.where(rows == row, partial, F32(0.0))
+        hidden_block[0] = dot(chosen, (share * grad).astype(BF16), LANES).astype(BF16)
+
+    steps = pl.num_programs(0) // 2
+
+    @pl.when(step < steps)
+    def _():
+        work(own, 0, weight_ref, stored_ref, hidden_ref)
+
+    @pl.when(step >= steps)
+    def _():
+        work(own ^ 1, 1, other_weight_ref, other_stored_ref, other_hidden_ref)
+
+
+def expert_call(place, gate, buffers, weight, other_weight, stored, other_stored, first, got, turn, prev):
+    devices, cap, hidden = stored.shape
+    half, width = buffers[0].shape
+    tile = 256
+    steps = hidden // tile
+    near = lambda n: jnp.minimum(n, steps - 1)
+    far = lambda n: jnp.maximum(n - steps, 0)
+    any_spec = pl.BlockSpec(memory_space=pl.ANY)
+    in_specs = [any_spec] * 4 + [
+        pl.BlockSpec((1, tile, width), lambda n, p, g: (0, near(n), 0)),
+        pl.BlockSpec((1, tile, width), lambda n, p, g: (0, far(n), 0)),
+        pl.BlockSpec((1, cap, tile), lambda n, p, g: (p[2], 0, near(n))),
+        pl.BlockSpec((1, cap, tile), lambda n, p, g: (p[2], 0, far(n))),
+        pl.BlockSpec((first.shape[0], tile), lambda n, p, g: (0, n % steps)),
+        pl.BlockSpec((1,) + got.shape[1:], lambda n, p, g: (p[2], 0, 0)),
+    ]
+    operands = [place, gate, *buffers, weight, other_weight, stored, other_stored, first, got]
+    aliases = {}
+    if prev is not None:
+        aliases = {len(operands): 0, len(operands) + 1: 1}
+        operands += list(prev)
+        in_specs += [any_spec, any_spec]
+    flops = 2 * 2 * half * width * 2 * hidden
+    return pl.pallas_call(
+        expert_kernel,
+        grid_spec=pltpu.PrefetchScalarGridSpec(
+            num_scalar_prefetch=2,
+            grid=(2 * steps,),
+            in_specs=in_specs,
+            out_specs=[
+                pl.BlockSpec((1, cap, tile), lambda n, p, g: (p[2], 0, near(n))),
+                pl.BlockSpec((1, cap, tile), lambda n, p, g: (turn, 0, far(n))),
+                pl.BlockSpec((8, 2 * half), lambda n, p, g: (0, 0)),
+            ],
+            scratch_shapes=[pltpu.VMEM((2 * half, width), BF16), pltpu.SemaphoreType.DMA((2,))],
+        ),
+        out_shape=[
+            jax.ShapeDtypeStruct((devices, cap, hidden), BF16),
+            jax.ShapeDtypeStruct((devices // 2, cap, hidden), BF16),
+            jax.ShapeDtypeStruct((8, 2 * half), F32),
+        ],
+        input_output_aliases=aliases,
+        compiler_params=params(),
+        cost_estimate=pl.CostEstimate(flops=flops, bytes_accessed=2 * 2 * hidden * width, transcendentals=0),
+    )(*operands)
+
+
+def finish_kernel(own_ref, masks, *refs):
+    count = len(masks)
+    dots, routes_ref, moved_ref = refs[:count], refs[count], refs[count + 1]
+    routing_ref, hidden_ref, sem = refs[count + 3 :]
+    own = own_ref[0]
+    copies = []
+    for k, mask in enumerate(masks):
+        source = own ^ 1 ^ (mask << 1)
+        copies.append(pltpu.make_async_copy(moved_ref.at[k], hidden_ref.at[source], sem.at[k]))
+    for copy in copies:
+        copy.start()
+    routes = routes_ref[...]
+    total = jnp.zeros(routes.shape, F32)
+    for k, mask in enumerate(masks):
+        for row in range(2):
+            expert = own ^ (mask << 1) ^ row
+            total = total + jnp.where(routes == expert, dots[k][row : row + 1, :], F32(0.0))
+    routing_ref[...] = total
+    for copy in copies:
+        copy.wait()
+
+
+def permutes():
+    number = lambda z, x, c: (z * 2 + x) * 2 + c
+    places = [(z, x, c) for z in range(4) for x in range(2) for c in range(2)]
+    end = lambda z: z in (0, 3)
+    return dict(
+        near=[(number(z, x, c), number(z ^ 1, x, c)) for z, x, c in places],
+        mid=[(number(z, x, c), number(3 - z, x, c)) for z, x, c in places if not end(z)],
+        out=[(number(z, x, c), number(z ^ 1, x, c)) for z, x, c in places if not end(z)],
+        inward=[(number(z, x, c), number(z ^ 1, x, c)) for z, x, c in places if end(z)],
+        side=[(number(z, x, c), number(z, 1 - x, c)) for z, x, c in places],
+        end_side=[(number(z, x, c), number(z, 1 - x, c)) for z, x, c in places if end(z)],
+        mid_side=[(number(z, x, c), number(z, 1 - x, c)) for z, x, c in places if not end(z)],
+    )
+
+
+def xor_pairs(mask):
+    return [(i, i ^ mask) for i in range(16)]
+
+
+def send(value, pairs):
+    return lax.ppermute(value, "ex", pairs)
+
+
+def spread(low, high):
+    to = permutes()
+    own = [low, high]
+    near = [send(h, to["near"]) for h in own]
+    mid = [send(h, to["mid"]) for h in own]
+    side = [send(h, to["side"]) for h in own]
+    out2 = [send(h, to["out"]) for h in mid]
+    mid2 = [send(h, to["mid"]) for h in near]
+    in2 = [send(h, to["inward"]) for h in side]
+    end1 = [send(h, to["end_side"]) for h in near]
+    mids1 = [send(h, to["mid_side"]) for h in mid]
+    out3 = [send(h, to["out"]) for h in mid2]
+    end2 = [send(h, to["end_side"]) for h in out2]
+    mids2 = [send(h, to["mid_side"]) for h in mid2]
+    end3 = send(out3[0], to["end_side"])
+    last = send(mids2[1], to["out"])
+    return {
+        0: (own, own),
+        2: (near, near),
+        1: (side, side),
+        4: (out2, mid2),
+        3: (end1, in2),
+        6: (out3, mid),
+        5: (end2, mids2),
+        7: ([end3, last], mids1),
+    }
+
+
+def sum_over_group(value):
+    for bit in (1, 2, 4, 8):
+        half = value.shape[0] // 2
+        value = value[:half] + send(value[half:], xor_pairs(bit))
+    for bit in (8, 4, 2, 1):
+        value = jnp.concatenate([value, send(value, xor_pairs(bit))], axis=0)
+    return value
+
+
+def small_body(
+    gradient_mantissas,
+    gradient_exponents,
+    routes,
+    routing_weight,
+    stored_hidden_rows,
+    frozen_down_weight,
+    adapter_first_factor,
+    adapter_second_factor,
+    expert_adapter_gate,
+):
+    tokens, width = gradient_mantissas.shape
+    stored = stored_hidden_rows[0]
+    devices, cap, hidden = stored.shape
+    rank = adapter_second_factor.shape[0]
+    first = adapter_first_factor.T
+    routes_t, weights_t = routes.T, routing_weight.T
+    own = lax.axis_index("ex").astype(jnp.int32)
+    own1 = own.reshape(1)
+    z = own >> 2
+    is_end = ((z == 0) | (z == 3)).astype(jnp.int32)
+    smem = pl.BlockSpec(memory_space=pltpu.SMEM)
+
+    other_weight = send(frozen_down_weight, xor_pairs(1))
+    other_stored = send(stored, xor_pairs(1))
+    low, high = pl.pallas_call(
+        scale_kernel,
+        in_specs=whole(2),
+        out_specs=whole(2),
+        out_shape=[jax.ShapeDtypeStruct((tokens // 2, width), BF16)] * 2,
+        compiler_params=params(),
+    )(gradient_mantissas, gradient_exponents.T)
+    buffers = spread(low, high)
+
+    packed = pl.pallas_call(
+        pack_kernel,
+        in_specs=[smem] + whole(7) + [smem],
+        out_specs=pl.BlockSpec(memory_space=pltpu.VMEM),
+        out_shape=jax.ShapeDtypeStruct((devices, 2 * rank + devices, tokens), BF16),
+        compiler_params=params(),
+    )(own1, low, high, adapter_second_factor, routes_t, weights_t, stored, first, expert_adapter_gate)
+    got = lax.all_to_all(packed, "ex", split_axis=0, concat_axis=0, tiled=True)
+    partial = pl.pallas_call(
+        low_rank_kernel,
+        in_specs=[smem] + whole(3) + [smem] + whole(4),
+        out_specs=pl.BlockSpec(memory_space=pltpu.VMEM),
+        out_shape=jax.ShapeDtypeStruct((devices, 80, 128), F32),
+        scratch_shapes=[pltpu.VMEM((rank, width), F32), pltpu.VMEM((devices, 16, 128), F32)],
+        compiler_params=params(),
+    )(own1, got, stored, first, expert_adapter_gate, routes_t, weights_t, low, high)
+    summed = sum_over_group(partial)
+    second_grad, first_grad, gate_grad = pl.pallas_call(
+        unpack_kernel,
+        in_specs=[smem] + whole(1),
+        out_specs=whole(3),
+        out_shape=[
+            jax.ShapeDtypeStruct((rank, width), F32),
+            jax.ShapeDtypeStruct((rank, hidden), F32),
+            jax.ShapeDtypeStruct((8, 128), F32),
+        ],
+        scratch_shapes=[pltpu.VMEM((devices, 16, 128), F32)],
+        compiler_params=params(),
+    )(own1, summed)
+
+    masks = (0, 2, 1, 4, 3, 6, 5, 7)
+    dots, prev = [], None
+    for turn, mask in enumerate(masks):
+        place = jnp.stack([own, is_end, own ^ (mask << 1)])
+        as_end, as_mid = buffers[mask]
+        *prev, dot_rows = expert_call(
+            place,
+            expert_adapter_gate,
+            [*as_end, *as_mid],
+            frozen_down_weight,
+            other_weight,
+            stored,
+            other_stored,
+            first,
+            got,
+            turn,
+            prev,
+        )
+        dots.append(send(dot_rows, xor_pairs(mask << 1)) if mask else dot_rows)
+    hidden_part, other_part = prev
+    moved = send(other_part, xor_pairs(1))
+    any_spec = pl.BlockSpec(memory_space=pl.ANY)
+    routing_t, hidden_gradient = pl.pallas_call(
+        lambda own_ref, *refs: finish_kernel(own_ref, masks, *refs),
+        in_specs=[smem] + whole(len(masks) + 1) + [any_spec, any_spec],
+        out_specs=[pl.BlockSpec(memory_space=pltpu.VMEM), any_spec],
+        out_shape=[
+            jax.ShapeDtypeStruct(routes_t.shape, F32),
+            jax.ShapeDtypeStruct((devices, cap, hidden), BF16),
+        ],
+        input_output_aliases={len(masks) + 3: 1},
+        scratch_shapes=[pltpu.SemaphoreType.DMA((len(masks),))],
+        compiler_params=params(),
+    )(own1, *dots, routes_t, moved, hidden_part)
+    return (
+        hidden_gradient[None],
+        routing_t.T,
+        first_grad.T,
+        second_grad,
+        gate_grad[0, :devices],
+    )
 
 
 def block_scale(gradient_exponents):
@@ -146,7 +609,7 @@
 
 def solution(mesh):
     return jax.shard_map(
-        body,
+        small_body if mesh.shape["ex"] == 16 else body,
         mesh=mesh,
         in_specs=(
             P(("groups", "ex"), None),

time: 399 us -> 246 us (0.62)
  waiting for transfers between devices: 206 us -> 48.9 us
  Pallas kernels: 0 us -> 95.4 us
  blocking collectives: 34.4 us -> 0 us
  local copies, waits for them, and re-layouts: 40.5 us -> 12.1 us
  matrix products: 27 us -> 0 us
  starting transfers between devices: 64.7 us -> 85.7 us
  between operations: 14.3 us -> 1.42 us
  other arithmetic: 11.2 us -> 1.08 us
    all_to_all x4 -> x1, waiting for transfers between devices: 178 us -> 0.65 us  [small_body(): got = lax.all_to_all(packed, 'ex', split_axis=0, concat_axis=0, tiled=True)]
    pallas_call x0 -> x13, Pallas kernels: none -> 95.4 us  [the longest x8 83.4 us: expert_call(): pl.pallas_call(expert_kernel, grid_spec=pltpu.PrefetchScalarGridSpec(num_...]
    ppermute x0 -> x42, starting transfers between devices: none -> 80.7 us  [send(): return lax.ppermute(value, 'ex', pairs)]
    all_to_all x4 -> x1, starting transfers between devices: 64.5 us -> 4.98 us  [small_body(): got = lax.all_to_all(packed, 'ex', split_axis=0, concat_axis=0, tiled=True)]
    ppermute x0 -> x42, waiting for transfers between devices: none -> 48.3 us  [send(): return lax.ppermute(value, 'ex', pairs)]
    psum x1 -> x0, blocking collectives: 34.4 us -> none  [body(): a_total, b_total, gate_total = lax.psum((a_grad, b_grad, own_gate), 'ex')]
    psum x1 -> x0, waiting for transfers between devices: 28.1 us -> none  [body(): a_total, b_total, gate_total = lax.psum((a_grad, b_grad, own_gate), 'ex')]
    dot_general x6 -> x0, matrix products: 27 us -> none  [the longest x1 14.8 us: per_expert_terms(): lax.dot_general(current_row_block, expert_down_matrix, contract_dimension...]
  transfers between devices with their start and end apart: 5 -> 43, of which waited for: 2 -> 12; matrix products, arithmetic and copies ran while one was open for 13% -> 1% of each run, Pallas kernels for 0% -> 38%
where the time goes in v1:
time: 246 us; the launch traced here: 245 us
  Pallas kernels  95.4 us (39%)
  starting transfers between devices  85.7 us (35%)
  waiting for transfers between devices  48.9 us (20%)
  local copies, waits for them, and re-layouts  12.1 us (5%)
    pallas_call x8, Pallas kernels, expert_call(): pl.pallas_call(expert_kernel, grid_spec=pltpu.PrefetchScalarGridSpec(num_...  83.4 us
    ppermute x42, starting transfers between devices, send(): return lax.ppermute(value, 'ex', pairs)  80.7 us
    ppermute x42, waiting for transfers between devices, send(): return lax.ppermute(value, 'ex', pairs)  48.3 us
    unnamed x45, local copies, waits for them, and re-layouts  10.9 us
    pallas_call x1, Pallas kernels, small_body(): pl.pallas_call(low_rank_kernel, in_specs=[smem] + whole(3) + [smem] + who...  5.45 us
    all_to_all x1, starting transfers between devices, small_body(): got = lax.all_to_all(packed, 'ex', split_axis=0, concat_axis=0, tiled=True)  4.98 us
  transfers between devices with their start and end apart: 43, of which 12 were waited for; matrix products, arithmetic and copies ran while one was open for 1% of the time, Pallas kernels for 38%

profile of v1, /device:TPU:0, one launch (start us, length us, event | category | flops | bytes accessed | tf_op | source)
XLA Modules:
  0.0 244.6 jit_solution(14304011859582829230)
XLA Ops:
  3.9 2.7 %collective-permute-start.2 = (bf16[64,4096]{1,0:T(8,128)(2,1)S(1)}, bf16[64,4096]{1,0:T(8,128)(2,1)}, u32[]{:S(2)}, u32[]{:S(2)}) collective-permute-start(bf16[64,4096]{1,0:T(8,128)(2,1)S(1)} %get-tuple-element.36.low_ref.a0_ref.b0_ref), channel_id=1, source_target_pairs={{0,4},{1,5},{2,6},{3,7},{4,0},{5,1},{6,2},{7,3},{8,12},{9,13},{10,... | collective-permute-start | bytes 1572872 | tf_op jit(solution)/shard_map/ppermute | solution.py:323
  12.2 3.3 %shard_map.129 = bf16[16,80,128]{2,1,0:T(8,128)(2,1)} custom-call(s32[1]{0:T(128)} %bitcast.own_ref, bf16[64,4096]{1,0:T(8,128)(2,1)S(1)} %get-tuple-element.36.low_ref.a0_ref.b0_ref, bf16[64,4096]{1,0:T(8,128)(2,1)S(1)} %get-tuple-element.37.high_ref.a1_ref.b1_ref, bf16[32,4096]{1,0:T(8,128)(2,1)S(1)} %copy-done.10, s32[8,128]{1,0:T(8,128)S(1)} %bitcast.31, ...), custom_call_target="tpu_custom_call" | custom-call | tf_op jit(solution)/shard_map/pallas_call | solution.py:397
  15.5 5.0 %all-to-all-start = ((bf16[16,80,128]{2,1,0:T(8,128)(2,1)}), bf16[16,80,128]{2,1,0:T(8,128)(2,1)S(1)}, u32[]{:S(2)}, u32[]{:S(2)}) async-start(bf16[16,80,128]{2,1,0:T(8,128)(2,1)} %shard_map.129), calls=%async_computation | async-start | bytes 655360 | tf_op jit(solution)/shard_map/all_to_all | solution.py:404
  23.9 8.7 %collective-permute-done.3.a1_ref.b1_ref = bf16[64,4096]{1,0:T(8,128)(2,1)} collective-permute-done((bf16[64,4096]{1,0:T(8,128)(2,1)S(1)}, bf16[64,4096]{1,0:T(8,128)(2,1)}, u32[]{:S(2)}, u32[]{:S(2)}) %collective-permute-start.3) | collective-permute-done | bytes 524320 | tf_op jit(solution)/shard_map/ppermute | solution.py:323
  35.5 2.6 %collective-permute-done.6.a1_ref.b1_ref = bf16[64,4096]{1,0:T(8,128)(2,1)} collective-permute-done((bf16[64,4096]{1,0:T(8,128)(2,1)S(1)}, bf16[64,4096]{1,0:T(8,128)(2,1)}, u32[]{:S(2)}, u32[]{:S(2)}) %collective-permute-start.6) | collective-permute-done | bytes 524320 | tf_op jit(solution)/shard_map/ppermute | solution.py:323
  38.8 5.5 %shard_map.139 = f32[16,80,128]{2,1,0:T(8,128)S(1)} custom-call(s32[1]{0:T(128)} %bitcast.own_ref, bf16[16,80,128]{2,1,0:T(8,128)(2,1)S(1)} %all-to-all-done.got_ref, bf16[16,80,768]{2,1,0:T(8,128)(2,1)} %bitcast.3.stored_ref, bf16[32,768]{1,0:T(8,128)(2,1)S(1)} %bitcast.22, f32[16]{0:T(128)S(1)} %copy-done.12, s32[8,128]{1,0:T(8,128)S(1)} %bitcast.32, ...), custom_call_target="tpu_custom_call" | custom-call | tf_op jit(solution)/shard_map/pallas_call | solution.py:405
  49.5 5.7 %collective-permute-done.35 = f32[4,80,128]{2,1,0:T(8,128)S(1)} collective-permute-done((f32[4,80,128]{2,1,0:T(8,128)S(1)}, f32[4,80,128]{2,1,0:T(8,128)S(1)}, u32[]{:S(2)}, u32[]{:S(2)}) %collective-permute-start.35) | collective-permute-done | bytes 163872 | tf_op jit(solution)/shard_map/ppermute | solution.py:323
  55.2 2.5 %collective-permute-start.15 = (bf16[64,4096]{1,0:T(8,128)(2,1)}, bf16[64,4096]{1,0:T(8,128)(2,1)S(1)}, u32[]{:S(2)}, u32[]{:S(2)}) collective-permute-start(bf16[64,4096]{1,0:T(8,128)(2,1)} %collective-permute-done.2.a0_ref.b0_ref), channel_id=1, source_target_pairs={{0,2},{1,3},{2,0},{3,1},{12,14},{13,15},{14,12},{15,13},{16,18},{1... | collective-permute-start | bytes 1572872 | tf_op jit(solution)/shard_map/ppermute | solution.py:323
  57.7 14.7 %collective-permute-done.11.a1_ref = bf16[64,4096]{1,0:T(8,128)(2,1)} collective-permute-done((bf16[64,4096]{1,0:T(8,128)(2,1)}, bf16[64,4096]{1,0:T(8,128)(2,1)}, u32[]{:S(2)}, u32[]{:S(2)}) %collective-permute-start.11) | collective-permute-done | bytes 524320 | tf_op jit(solution)/shard_map/ppermute | solution.py:323
  72.4 11.0 %collective-permute-start.36 = (f32[2,80,128]{2,1,0:T(8,128)S(1)}, f32[2,80,128]{2,1,0:T(8,128)S(1)}, u32[]{:S(2)}, u32[]{:S(2)}) collective-permute-start(f32[2,80,128]{2,1,0:T(8,128)S(1)} %slice.41), channel_id=1, source_target_pairs={{0,4},{1,5},{2,6},{3,7},{4,0},{5,1},{6,2},{7,3},{8,12},{9,13},{10,... | collective-permute-start | bytes 245768 | tf_op jit(solution)/shard_map/ppermute | solution.py:323
  83.4 3.6 %collective-permute-start.16 = (bf16[64,4096]{1,0:T(8,128)(2,1)}, bf16[64,4096]{1,0:T(8,128)(2,1)}, u32[]{:S(2)}, u32[]{:S(2)}) collective-permute-start(bf16[64,4096]{1,0:T(8,128)(2,1)} %collective-permute-done.3.a1_ref.b1_ref), channel_id=1, source_target_pairs={{0,2},{1,3},{2,0},{3,1},{12,14},{13,15},{14,12},{15,13},{16,18},{1... | collective-permute-start | bytes 1572872 | tf_op jit(solution)/shard_map/ppermute | solution.py:323
  87.1 3.5 %collective-permute-start.17 = (bf16[64,4096]{1,0:T(8,128)(2,1)}, bf16[64,4096]{1,0:T(8,128)(2,1)}, u32[]{:S(2)}, u32[]{:S(2)}) collective-permute-start(bf16[64,4096]{1,0:T(8,128)(2,1)} %collective-permute-done.5.a0_ref.b0_ref), channel_id=1, source_target_pairs={{0,4},{1,5},{2,6},{3,7},{12,8},{13,9},{14,10},{15,11},{16,20},{17,... | collective-permute-start | bytes 1572872 | tf_op jit(solution)/shard_map/ppermute | solution.py:323
  92.1 7.5 %collective-permute-done.37 = f32[1,80,128]{2,1,0:T(8,128)} collective-permute-done((f32[1,80,128]{2,1,0:T(8,128)}, f32[1,80,128]{2,1,0:T(8,128)}, u32[]{:S(2)}, u32[]{:S(2)}) %collective-permute-start.37) | collective-permute-done | bytes 40992 | tf_op jit(solution)/shard_map/ppermute | solution.py:323
  99.6 4.2 %collective-permute-start.18 = (bf16[64,4096]{1,0:T(8,128)(2,1)}, bf16[64,4096]{1,0:T(8,128)(2,1)S(1)}, u32[]{:S(2)}, u32[]{:S(2)}) collective-permute-start(bf16[64,4096]{1,0:T(8,128)(2,1)} %collective-permute-done.6.a1_ref.b1_ref), channel_id=1, source_target_pairs={{0,4},{1,5},{2,6},{3,7},{12,8},{13,9},{14,10},{15,11},{16,20},{17,... | collective-permute-start | bytes 1572872 | tf_op jit(solution)/shard_map/ppermute | solution.py:323
  106.0 3.8 %collective-permute-start.38 = (f32[1,80,128]{2,1,0:T(8,128)S(1)}, f32[1,80,128]{2,1,0:T(8,128)S(1)}, u32[]{:S(2)}, u32[]{:S(2)}) collective-permute-start(f32[1,80,128]{2,1,0:T(8,128)S(1)} %get-tuple-element.68), channel_id=1, source_target_pairs={{0,8},{1,9},{2,10},{3,11},{4,12},{5,13},{6,14},{7,15},{8,0},{9,1},... | collective-permute-start | bytes 122888 | tf_op jit(solution)/shard_map/ppermute | solution.py:323
  114.1 4.1 %collective-permute-start.23 = (bf16[64,4096]{1,0:T(8,128)(2,1)}, bf16[64,4096]{1,0:T(8,128)(2,1)}, u32[]{:S(2)}, u32[]{:S(2)}) collective-permute-start(bf16[64,4096]{1,0:T(8,128)(2,1)} %collective-permute-done.9.a0_ref), channel_id=1, source_target_pairs={{0,2},{1,3},{2,0},{3,1},{12,14},{13,15},{14,12},{15,13},{16,18},{1... | collective-permute-start | bytes 1572872 | tf_op jit(solution)/shard_map/ppermute | solution.py:323
  118.3 2.8 %copy-done = bf16[1,768,4096]{2,1,0:T(8,128)(2,1)S(1)} copy-done((bf16[1,768,4096]{2,1,0:T(8,128)(2,1)S(1)}, bf16[1,768,4096]{2,1,0:T(8,128)(2,1)}, u32[]{:S(2)}) %copy-start) | copy-done | bytes 6291480
  121.0 10.0 %shard_map.130 = (bf16[16,80,768]{2,1,0:T(8,128)(2,1)}, bf16[8,80,768]{2,1,0:T(8,128)(2,1)S(1)}, f32[8,128]{1,0:T(8,128)S(1)}) custom-call(s32[3]{0:T(128)S(1)} %get-tuple-element.77.place_ref, f32[16]{0:T(128)S(1)} %copy-done.12, bf16[64,4096]{1,0:T(8,128)(2,1)S(1)} %get-tuple-element.36.low_ref.a0_ref.b0_ref, ...), custom_call_target="tpu_custom_call" | custom-call | flops 1610612736 | bytes 12582912 | tf_op jit(solution)/shard_map/pallas_call | solution.py:257
  131.1 10.8 %shard_map.131 = (bf16[16,80,768]{2,1,0:T(8,128)(2,1)}, bf16[8,80,768]{2,1,0:T(8,128)(2,1)S(1)}, f32[8,128]{1,0:T(8,128)S(1)}) custom-call(s32[3]{0:T(128)S(1)} %get-tuple-element.76.place_ref, f32[16]{0:T(128)S(1)} %copy-done.12, bf16[64,4096]{1,0:T(8,128)(2,1)} %collective-permute-done.2.a0_ref.b0_ref, ...), custom_call_target="tpu_custom_call", output_to_operand_aliasing={{0}: (12, {}), {1}: (13, {})} | custom-call | flops 1610612736 | bytes 12582912 | tf_op jit(solution)/shard_map/pallas_call | solution.py:257
  141.9 1.9 collective-permute-start.24
  143.9 10.8 %shard_map.132 = (bf16[16,80,768]{2,1,0:T(8,128)(2,1)}, bf16[8,80,768]{2,1,0:T(8,128)(2,1)S(1)}, f32[8,128]{1,0:T(8,128)S(1)}) custom-call(s32[3]{0:T(128)S(1)} %get-tuple-element.75.place_ref, f32[16]{0:T(128)S(1)} %copy-done.12, bf16[64,4096]{1,0:T(8,128)(2,1)} %collective-permute-done.5.a0_ref.b0_ref, ...), custom_call_target="tpu_custom_call", output_to_operand_aliasing={{0}: (12, {}), {1}: (13, {})} | custom-call | flops 1610612736 | bytes 12582912 | tf_op jit(solution)/shard_map/pallas_call | solution.py:257
  157.7 3.9 %collective-permute-start.28 = (bf16[64,4096]{1,0:T(8,128)(2,1)S(1)}, bf16[64,4096]{1,0:T(8,128)(2,1)S(1)}, u32[]{:S(2)}, u32[]{:S(2)}) collective-permute-start(bf16[64,4096]{1,0:T(8,128)(2,1)S(1)} %collective-permute-done.20.a0_ref), channel_id=1, source_target_pairs={{0,2},{1,3},{2,0},{3,1},{12,14},{13,15},{14,12},{15,13},{16,18},{1... | collective-permute-start | bytes 1572872 | tf_op jit(solution)/shard_map/ppermute | solution.py:323
  163.2 10.8 %shard_map.133 = (bf16[16,80,768]{2,1,0:T(8,128)(2,1)}, bf16[8,80,768]{2,1,0:T(8,128)(2,1)S(1)}, f32[8,128]{1,0:T(8,128)S(1)}) custom-call(s32[3]{0:T(128)S(1)} %get-tuple-element.74.place_ref, f32[16]{0:T(128)S(1)} %copy-done.12, bf16[64,4096]{1,0:T(8,128)(2,1)} %collective-permute-done.9.a0_ref, ...), custom_call_target="tpu_custom_call", output_to_operand_aliasing={{0}: (12, {}), {1}: (13, {})} | custom-call | flops 1610612736 | bytes 12582912 | tf_op jit(solution)/shard_map/pallas_call | solution.py:257
  174.0 10.7 %shard_map.134 = (bf16[16,80,768]{2,1,0:T(8,128)(2,1)}, bf16[8,80,768]{2,1,0:T(8,128)(2,1)S(1)}, f32[8,128]{1,0:T(8,128)S(1)}) custom-call(s32[3]{0:T(128)S(1)} %get-tuple-element.73.place_ref, f32[16]{0:T(128)S(1)} %copy-done.12, bf16[64,4096]{1,0:T(8,128)(2,1)S(1)} %copy-done.5, ...), custom_call_target="tpu_custom_call", output_to_operand_aliasing={{0}: (12, {}), {1}: (13, {})} | custom-call | flops 1610612736 | bytes 12582912 | tf_op jit(solution)/shard_map/pallas_call | solution.py:257
  184.8 9.7 %shard_map.135 = (bf16[16,80,768]{2,1,0:T(8,128)(2,1)}, bf16[8,80,768]{2,1,0:T(8,128)(2,1)S(1)}, f32[8,128]{1,0:T(8,128)S(1)}) custom-call(s32[3]{0:T(128)S(1)} %get-tuple-element.72.place_ref, f32[16]{0:T(128)S(1)} %copy-done.12, bf16[64,4096]{1,0:T(8,128)(2,1)S(1)} %collective-permute-done.20.a0_ref, ...), custom_call_target="tpu_custom_call", output_to_operand_aliasing={{0}: (12, {}), {1}: (13, {})} | custom-call | flops 1610612736 | bytes 12582912 | tf_op jit(solution)/shard_map/pallas_call | solution.py:257
  194.5 6.4 %collective-permute-start.39 = (f32[2,80,128]{2,1,0:T(8,128)S(1)}, f32[2,80,128]{2,1,0:T(8,128)S(1)}, u32[]{:S(2)}, u32[]{:S(2)}) collective-permute-start(f32[2,80,128]{2,1,0:T(8,128)S(1)} %pad_maximum_fusion.2), channel_id=1, source_target_pairs={{0,4},{1,5},{2,6},{3,7},{4,0},{5,1},{6,2},{7,3},{8,12},{9,13},{10,... | collective-permute-start | bytes 245768 | tf_op jit(solution)/shard_map/ppermute | solution.py:323
  201.0 10.7 %shard_map.136 = (bf16[16,80,768]{2,1,0:T(8,128)(2,1)}, bf16[8,80,768]{2,1,0:T(8,128)(2,1)S(1)}, f32[8,128]{1,0:T(8,128)S(1)}) custom-call(s32[3]{0:T(128)S(1)} %get-tuple-element.71.place_ref, f32[16]{0:T(128)S(1)} %copy-done.12, bf16[64,4096]{1,0:T(8,128)(2,1)} %collective-permute-done.23.a0_ref, ...), custom_call_target="tpu_custom_call", output_to_operand_aliasing={{0}: (12, {}), {1}: (13, {})} | custom-call | flops 1610612736 | bytes 12582912 | tf_op jit(solution)/shard_map/pallas_call | solution.py:257
  211.7 9.7 %shard_map.137 = (bf16[16,80,768]{2,1,0:T(8,128)(2,1)}, bf16[8,80,768]{2,1,0:T(8,128)(2,1)S(1)}, f32[8,128]{1,0:T(8,128)S(1)}) custom-call(s32[3]{0:T(128)S(1)} %get-tuple-element.69.place_ref, f32[16]{0:T(128)S(1)} %copy-done.12, bf16[64,4096]{1,0:T(8,128)(2,1)S(1)} %collective-permute-done.28.a0_ref, ...), custom_call_target="tpu_custom_call", output_to_operand_aliasing={{0}: (12, {}), {1}: (13, {})} | custom-call | flops 1610612736 | bytes 12582912 | tf_op jit(solution)/shard_map/pallas_call | solution.py:257
  221.5 2.1 collective-permute-start.40
  223.6 4.8 %collective-permute-done.40 = f32[4,80,128]{2,1,0:T(8,128)S(1)} collective-permute-done((f32[4,80,128]{2,1,0:T(8,128)S(1)}, f32[4,80,128]{2,1,0:T(8,128)S(1)}, u32[]{:S(2)}, u32[]{:S(2)}) %collective-permute-start.40) | collective-permute-done | bytes 163872 | tf_op jit(solution)/shard_map/ppermute | solution.py:323
  228.6 3.9 %collective-permute-start.32 = (f32[8,128]{1,0:T(8,128)S(1)}, f32[8,128]{1,0:T(8,128)S(1)}, u32[]{:S(2)}, u32[]{:S(2)}) collective-permute-start(f32[8,128]{1,0:T(8,128)S(1)} %get-tuple-element.59), channel_id=1, source_target_pairs={{0,14},{1,15},{2,12},{3,13},{4,10},{5,11},{6,8},{7,9},{8,6},{9,7},... | collective-permute-start | bytes 12296 | tf_op jit(solution)/shard_map/ppermute | solution.py:323
  234.6 3.2 %collective-permute-start.19 = (f32[8,128]{1,0:T(8,128)S(1)}, f32[8,128]{1,0:T(8,128)S(1)}, u32[]{:S(2)}, u32[]{:S(2)}) collective-permute-start(f32[8,128]{1,0:T(8,128)S(1)} %get-tuple-element.50), channel_id=1, source_target_pairs={{0,6},{1,7},{2,4},{3,5},{4,2},{5,3},{6,0},{7,1},{8,14},{9,15},{10,... | collective-permute-start | bytes 12296 | tf_op jit(solution)/shard_map/ppermute | solution.py:323
  (128 shorter events, 42.4 us)
Async XLA Ops:
  0.6 113.4 %collective-permute-start = (bf16[1,768,4096]{2,1,0:T(8,128)(2,1)}, bf16[1,768,4096]{2,1,0:T(8,128)(2,1)}, u32[]{:S(2)}, u32[]{:S(2)}) collective-permute-start(bf16[1,768,4096]{2,1,0:T(8,128)(2,1)} %weight_ref.15), channel_id=1, source_target_pairs={{0,1},{1,0},{2,3},{3,2},{4,5},{5,4},{6,7},{7,6},{8,9},{9,8},{10,11... | collective-permute-start | bytes 18874376 | tf_op jit(solution)/shard_map/ppermute | solution.py:323
  3.9 18.6 %collective-permute-start.2 = (bf16[64,4096]{1,0:T(8,128)(2,1)S(1)}, bf16[64,4096]{1,0:T(8,128)(2,1)}, u32[]{:S(2)}, u32[]{:S(2)}) collective-permute-start(bf16[64,4096]{1,0:T(8,128)(2,1)S(1)} %get-tuple-element.36.low_ref.a0_ref.b0_ref), channel_id=1, source_target_pairs={{0,4},{1,5},{2,6},{3,7},{4,0},{5,1},{6,2},{7,3},{8,12},{9,13},{10,... | collective-permute-start | bytes 1572872 | tf_op jit(solution)/shard_map/ppermute | solution.py:323
  6.5 26.0 %collective-permute-start.3 = (bf16[64,4096]{1,0:T(8,128)(2,1)S(1)}, bf16[64,4096]{1,0:T(8,128)(2,1)}, u32[]{:S(2)}, u32[]{:S(2)}) collective-permute-start(bf16[64,4096]{1,0:T(8,128)(2,1)S(1)} %get-tuple-element.37.high_ref.a1_ref.b1_ref), channel_id=1, source_target_pairs={{0,4},{1,5},{2,6},{3,7},{4,0},{5,1},{6,2},{7,3},{8,12},{9,13},{10,... | collective-permute-start | bytes 1572872 | tf_op jit(solution)/shard_map/ppermute | solution.py:323
  6.6 27.4 %collective-permute-start.5 = (bf16[64,4096]{1,0:T(8,128)(2,1)S(1)}, bf16[64,4096]{1,0:T(8,128)(2,1)}, u32[]{:S(2)}, u32[]{:S(2)}) collective-permute-start(bf16[64,4096]{1,0:T(8,128)(2,1)S(1)} %get-tuple-element.36.low_ref.a0_ref.b0_ref), channel_id=1, source_target_pairs={{0,2},{1,3},{2,0},{3,1},{4,6},{5,7},{6,4},{7,5},{8,10},{9,11},{10,... | collective-permute-start | bytes 1572872 | tf_op jit(solution)/shard_map/ppermute | solution.py:323
  15.5 23.2 %all-to-all-start = ((bf16[16,80,128]{2,1,0:T(8,128)(2,1)}), bf16[16,80,128]{2,1,0:T(8,128)(2,1)S(1)}, u32[]{:S(2)}, u32[]{:S(2)}) async-start(bf16[16,80,128]{2,1,0:T(8,128)(2,1)} %shard_map.129), calls=%async_computation | async-start | bytes 655360 | tf_op jit(solution)/shard_map/all_to_all | solution.py:404
  20.5 17.6 %collective-permute-start.6 = (bf16[64,4096]{1,0:T(8,128)(2,1)S(1)}, bf16[64,4096]{1,0:T(8,128)(2,1)}, u32[]{:S(2)}, u32[]{:S(2)}) collective-permute-start(bf16[64,4096]{1,0:T(8,128)(2,1)S(1)} %get-tuple-element.37.high_ref.a1_ref.b1_ref), channel_id=1, source_target_pairs={{0,2},{1,3},{2,0},{3,1},{4,6},{5,7},{6,4},{7,5},{8,10},{9,11},{10,... | collective-permute-start | bytes 1572872 | tf_op jit(solution)/shard_map/ppermute | solution.py:323
  22.4 21.8 %collective-permute-start.10 = (bf16[64,4096]{1,0:T(8,128)(2,1)S(1)}, bf16[64,4096]{1,0:T(8,128)(2,1)}, u32[]{:S(2)}, u32[]{:S(2)}) collective-permute-start(bf16[64,4096]{1,0:T(8,128)(2,1)S(1)} %get-tuple-element.37.high_ref.a1_ref.b1_ref), channel_id=1, source_target_pairs={{4,8},{5,9},{6,10},{7,11},{8,4},{9,5},{10,6},{11,7},{20,24},{21,25... | collective-permute-start | bytes 1572872 | tf_op jit(solution)/shard_map/ppermute | solution.py:323
  32.6 11.8 %collective-permute-start.8 = (bf16[64,4096]{1,0:T(8,128)(2,1)S(1)}, bf16[64,4096]{1,0:T(8,128)(2,1)}, u32[]{:S(2)}, u32[]{:S(2)}) collective-permute-start(bf16[64,4096]{1,0:T(8,128)(2,1)S(1)} %get-tuple-element.36.low_ref.a0_ref.b0_ref), channel_id=1, source_target_pairs={{4,8},{5,9},{6,10},{7,11},{8,4},{9,5},{10,6},{11,7},{20,24},{21,25... | collective-permute-start | bytes 1572872 | tf_op jit(solution)/shard_map/ppermute | solution.py:323
  34.0 13.3 %collective-permute-start.12 = (bf16[64,4096]{1,0:T(8,128)(2,1)}, bf16[64,4096]{1,0:T(8,128)(2,1)}, u32[]{:S(2)}, u32[]{:S(2)}) collective-permute-start(bf16[64,4096]{1,0:T(8,128)(2,1)} %collective-permute-done.2.a0_ref.b0_ref), channel_id=1, source_target_pairs={{4,8},{5,9},{6,10},{7,11},{8,4},{9,5},{10,6},{11,7},{20,24},{21,25... | collective-permute-start | bytes 1572872 | tf_op jit(solution)/shard_map/ppermute | solution.py:323
  38.1 75.3 %collective-permute-start.1 = (bf16[16,80,768]{2,1,0:T(8,128)(2,1)}, bf16[16,80,768]{2,1,0:T(8,128)(2,1)}, u32[]{:S(2)}, u32[]{:S(2)}) collective-permute-start(bf16[16,80,768]{2,1,0:T(8,128)(2,1)} %bitcast.3.stored_ref), channel_id=1, source_target_pairs={{0,1},{1,0},{2,3},{3,2},{4,5},{5,4},{6,7},{7,6},{8,9},{9,8},{10,11... | collective-permute-start | bytes 5898248 | tf_op jit(solution)/shard_map/ppermute | solution.py:323
  46.0 26.5 %collective-permute-start.11 = (bf16[64,4096]{1,0:T(8,128)(2,1)}, bf16[64,4096]{1,0:T(8,128)(2,1)}, u32[]{:S(2)}, u32[]{:S(2)}) collective-permute-start(bf16[64,4096]{1,0:T(8,128)(2,1)} %collective-permute-done.10.b1_ref), channel_id=1, source_target_pairs={{4,0},{5,1},{6,2},{7,3},{8,12},{9,13},{10,14},{11,15},{20,16},{21,... | collective-permute-start | bytes 1572872 | tf_op jit(solution)/shard_map/ppermute | solution.py:323
  47.3 36.2 %collective-permute-start.9 = (bf16[64,4096]{1,0:T(8,128)(2,1)}, bf16[64,4096]{1,0:T(8,128)(2,1)}, u32[]{:S(2)}, u32[]{:S(2)}) collective-permute-start(bf16[64,4096]{1,0:T(8,128)(2,1)} %collective-permute-done.8.b0_ref), channel_id=1, source_target_pairs={{4,0},{5,1},{6,2},{7,3},{8,12},{9,13},{10,14},{11,15},{20,16},{21,... | collective-permute-start | bytes 1572872 | tf_op jit(solution)/shard_map/ppermute | solution.py:323
  55.2 36.1 %collective-permute-start.15 = (bf16[64,4096]{1,0:T(8,128)(2,1)}, bf16[64,4096]{1,0:T(8,128)(2,1)S(1)}, u32[]{:S(2)}, u32[]{:S(2)}) collective-permute-start(bf16[64,4096]{1,0:T(8,128)(2,1)} %collective-permute-done.2.a0_ref.b0_ref), channel_id=1, source_target_pairs={{0,2},{1,3},{2,0},{3,1},{12,14},{13,15},{14,12},{15,13},{16,18},{1... | collective-permute-start | bytes 1572872 | tf_op jit(solution)/shard_map/ppermute | solution.py:323
  72.4 14.7 %collective-permute-start.36 = (f32[2,80,128]{2,1,0:T(8,128)S(1)}, f32[2,80,128]{2,1,0:T(8,128)S(1)}, u32[]{:S(2)}, u32[]{:S(2)}) collective-permute-start(f32[2,80,128]{2,1,0:T(8,128)S(1)} %slice.41), channel_id=1, source_target_pairs={{0,4},{1,5},{2,6},{3,7},{4,0},{5,1},{6,2},{7,3},{8,12},{9,13},{10,... | collective-permute-start | bytes 245768 | tf_op jit(solution)/shard_map/ppermute | solution.py:323
  83.4 21.3 %collective-permute-start.16 = (bf16[64,4096]{1,0:T(8,128)(2,1)}, bf16[64,4096]{1,0:T(8,128)(2,1)}, u32[]{:S(2)}, u32[]{:S(2)}) collective-permute-start(bf16[64,4096]{1,0:T(8,128)(2,1)} %collective-permute-done.3.a1_ref.b1_ref), channel_id=1, source_target_pairs={{0,2},{1,3},{2,0},{3,1},{12,14},{13,15},{14,12},{15,13},{16,18},{1... | collective-permute-start | bytes 1572872 | tf_op jit(solution)/shard_map/ppermute | solution.py:323
  87.1 18.9 %collective-permute-start.17 = (bf16[64,4096]{1,0:T(8,128)(2,1)}, bf16[64,4096]{1,0:T(8,128)(2,1)}, u32[]{:S(2)}, u32[]{:S(2)}) collective-permute-start(bf16[64,4096]{1,0:T(8,128)(2,1)} %collective-permute-done.5.a0_ref.b0_ref), channel_id=1, source_target_pairs={{0,4},{1,5},{2,6},{3,7},{12,8},{13,9},{14,10},{15,11},{16,20},{17,... | collective-permute-start | bytes 1572872 | tf_op jit(solution)/shard_map/ppermute | solution.py:323
  92.1 7.6 %collective-permute-start.37 = (f32[1,80,128]{2,1,0:T(8,128)}, f32[1,80,128]{2,1,0:T(8,128)}, u32[]{:S(2)}, u32[]{:S(2)}) collective-permute-start(f32[1,80,128]{2,1,0:T(8,128)} %slice.43), channel_id=1, source_target_pairs={{0,8},{1,9},{2,10},{3,11},{4,12},{5,13},{6,14},{7,15},{8,0},{9,1},... | collective-permute-start | bytes 122888 | tf_op jit(solution)/shard_map/ppermute | solution.py:323
  99.6 11.8 %collective-permute-start.18 = (bf16[64,4096]{1,0:T(8,128)(2,1)}, bf16[64,4096]{1,0:T(8,128)(2,1)S(1)}, u32[]{:S(2)}, u32[]{:S(2)}) collective-permute-start(bf16[64,4096]{1,0:T(8,128)(2,1)} %collective-permute-done.6.a1_ref.b1_ref), channel_id=1, source_target_pairs={{0,4},{1,5},{2,6},{3,7},{12,8},{13,9},{14,10},{15,11},{16,20},{17,... | collective-permute-start | bytes 1572872 | tf_op jit(solution)/shard_map/ppermute | solution.py:323
  104.7 37.2 %collective-permute-start.20 = (bf16[64,4096]{1,0:T(8,128)(2,1)}, bf16[64,4096]{1,0:T(8,128)(2,1)S(1)}, u32[]{:S(2)}, u32[]{:S(2)}) collective-permute-start(bf16[64,4096]{1,0:T(8,128)(2,1)} %collective-permute-done.12.b0_ref), channel_id=1, source_target_pairs={{4,0},{5,1},{6,2},{7,3},{8,12},{9,13},{10,14},{11,15},{20,16},{21,... | collective-permute-start | bytes 1572872 | tf_op jit(solution)/shard_map/ppermute | solution.py:323
  111.4 43.4 %collective-permute-start.21 = (bf16[64,4096]{1,0:T(8,128)(2,1)}, bf16[64,4096]{1,0:T(8,128)(2,1)S(1)}, u32[]{:S(2)}, u32[]{:S(2)}) collective-permute-start(bf16[64,4096]{1,0:T(8,128)(2,1)} %collective-permute-done.13.b1_ref), channel_id=1, source_target_pairs={{4,0},{5,1},{6,2},{7,3},{8,12},{9,13},{10,14},{11,15},{20,16},{21,... | collective-permute-start | bytes 1572872 | tf_op jit(solution)/shard_map/ppermute | solution.py:323
  112.7 43.6 %collective-permute-start.26 = (bf16[64,4096]{1,0:T(8,128)(2,1)}, bf16[64,4096]{1,0:T(8,128)(2,1)S(1)}, u32[]{:S(2)}, u32[]{:S(2)}) collective-permute-start(bf16[64,4096]{1,0:T(8,128)(2,1)} %collective-permute-done.13.b1_ref), channel_id=1, source_target_pairs={{4,6},{5,7},{6,4},{7,5},{8,10},{9,11},{10,8},{11,9},{20,22},{21,23... | collective-permute-start | bytes 1572872 | tf_op jit(solution)/shard_map/ppermute | solution.py:323
  113.4 43.6 %collective-permute-start.25 = (bf16[64,4096]{1,0:T(8,128)(2,1)}, bf16[64,4096]{1,0:T(8,128)(2,1)S(1)}, u32[]{:S(2)}, u32[]{:S(2)}) collective-permute-start(bf16[64,4096]{1,0:T(8,128)(2,1)} %collective-permute-done.12.b0_ref), channel_id=1, source_target_pairs={{4,6},{5,7},{6,4},{7,5},{8,10},{9,11},{10,8},{11,9},{20,22},{21,23... | collective-permute-start | bytes 1572872 | tf_op jit(solution)/shard_map/ppermute | solution.py:323
  114.1 47.6 %collective-permute-start.23 = (bf16[64,4096]{1,0:T(8,128)(2,1)}, bf16[64,4096]{1,0:T(8,128)(2,1)}, u32[]{:S(2)}, u32[]{:S(2)}) collective-permute-start(bf16[64,4096]{1,0:T(8,128)(2,1)} %collective-permute-done.9.a0_ref), channel_id=1, source_target_pairs={{0,2},{1,3},{2,0},{3,1},{12,14},{13,15},{14,12},{15,13},{16,18},{1... | collective-permute-start | bytes 1572872 | tf_op jit(solution)/shard_map/ppermute | solution.py:323
  141.9 52.6 %collective-permute-start.24 = (bf16[64,4096]{1,0:T(8,128)(2,1)}, bf16[64,4096]{1,0:T(8,128)(2,1)S(1)}, u32[]{:S(2)}, u32[]{:S(2)}) collective-permute-start(bf16[64,4096]{1,0:T(8,128)(2,1)} %collective-permute-done.11.a1_ref), channel_id=1, source_target_pairs={{0,2},{1,3},{2,0},{3,1},{12,14},{13,15},{14,12},{15,13},{16,18},{1... | collective-permute-start | bytes 1572872 | tf_op jit(solution)/shard_map/ppermute | solution.py:323
  155.5 56.1 %collective-permute-start.30 = (bf16[64,4096]{1,0:T(8,128)(2,1)}, bf16[64,4096]{1,0:T(8,128)(2,1)S(1)}, u32[]{:S(2)}, u32[]{:S(2)}) collective-permute-start(bf16[64,4096]{1,0:T(8,128)(2,1)} %collective-permute-done.8.b0_ref), channel_id=1, source_target_pairs={{4,6},{5,7},{6,4},{7,5},{8,10},{9,11},{10,8},{11,9},{20,22},{21,23... | collective-permute-start | bytes 1572872 | tf_op jit(solution)/shard_map/ppermute | solution.py:323
  156.2 55.4 %collective-permute-start.31 = (bf16[64,4096]{1,0:T(8,128)(2,1)}, bf16[64,4096]{1,0:T(8,128)(2,1)S(1)}, u32[]{:S(2)}, u32[]{:S(2)}) collective-permute-start(bf16[64,4096]{1,0:T(8,128)(2,1)} %collective-permute-done.10.b1_ref), channel_id=1, source_target_pairs={{4,6},{5,7},{6,4},{7,5},{8,10},{9,11},{10,8},{11,9},{20,22},{21,23... | collective-permute-start | bytes 1572872 | tf_op jit(solution)/shard_map/ppermute | solution.py:323
  157.7 53.9 %collective-permute-start.28 = (bf16[64,4096]{1,0:T(8,128)(2,1)S(1)}, bf16[64,4096]{1,0:T(8,128)(2,1)S(1)}, u32[]{:S(2)}, u32[]{:S(2)}) collective-permute-start(bf16[64,4096]{1,0:T(8,128)(2,1)S(1)} %collective-permute-done.20.a0_ref), channel_id=1, source_target_pairs={{0,2},{1,3},{2,0},{3,1},{12,14},{13,15},{14,12},{15,13},{16,18},{1... | collective-permute-start | bytes 1572872 | tf_op jit(solution)/shard_map/ppermute | solution.py:323
  161.7 50.0 %collective-permute-start.29 = (bf16[64,4096]{1,0:T(8,128)(2,1)S(1)}, bf16[64,4096]{1,0:T(8,128)(2,1)S(1)}, u32[]{:S(2)}, u32[]{:S(2)}) collective-permute-start(bf16[64,4096]{1,0:T(8,128)(2,1)S(1)} %collective-permute-done.26.b1_ref), channel_id=1, source_target_pairs={{4,0},{5,1},{6,2},{7,3},{8,12},{9,13},{10,14},{11,15},{20,16},{21,... | collective-permute-start | bytes 1572872 | tf_op jit(solution)/shard_map/ppermute | solution.py:323
  194.5 27.0 %collective-permute-start.39 = (f32[2,80,128]{2,1,0:T(8,128)S(1)}, f32[2,80,128]{2,1,0:T(8,128)S(1)}, u32[]{:S(2)}, u32[]{:S(2)}) collective-permute-start(f32[2,80,128]{2,1,0:T(8,128)S(1)} %pad_maximum_fusion.2), channel_id=1, source_target_pairs={{0,4},{1,5},{2,6},{3,7},{4,0},{5,1},{6,2},{7,3},{8,12},{9,13},{10,... | collective-permute-start | bytes 245768 | tf_op jit(solution)/shard_map/ppermute | solution.py:323
  221.4 21.4 %collective-permute-start.33 = (bf16[8,80,768]{2,1,0:T(8,128)(2,1)S(1)}, bf16[8,80,768]{2,1,0:T(8,128)(2,1)S(1)}, u32[]{:S(2)}, u32[]{:S(2)}) collective-permute-start(bf16[8,80,768]{2,1,0:T(8,128)(2,1)S(1)} %get-tuple-element.60), channel_id=1, source_target_pairs={{0,1},{1,0},{2,3},{3,2},{4,5},{5,4},{6,7},{7,6},{8,9},{9,8},{10,11... | collective-permute-start | bytes 2949128 | tf_op jit(solution)/shard_map/ppermute | solution.py:323
  221.5 6.9 %collective-permute-start.40 = (f32[4,80,128]{2,1,0:T(8,128)S(1)}, f32[4,80,128]{2,1,0:T(8,128)S(1)}, u32[]{:S(2)}, u32[]{:S(2)}) collective-permute-start(f32[4,80,128]{2,1,0:T(8,128)S(1)} %pad_maximum_fusion.1), channel_id=1, source_target_pairs={{0,2},{1,3},{2,0},{3,1},{4,6},{5,7},{6,4},{7,5},{8,10},{9,11},{10,... | collective-permute-start | bytes 491528 | tf_op jit(solution)/shard_map/ppermute | solution.py:323
  228.6 9.2 %collective-permute-start.32 = (f32[8,128]{1,0:T(8,128)S(1)}, f32[8,128]{1,0:T(8,128)S(1)}, u32[]{:S(2)}, u32[]{:S(2)}) collective-permute-start(f32[8,128]{1,0:T(8,128)S(1)} %get-tuple-element.59), channel_id=1, source_target_pairs={{0,14},{1,15},{2,12},{3,13},{4,10},{5,11},{6,8},{7,9},{8,6},{9,7},... | collective-permute-start | bytes 12296 | tf_op jit(solution)/shard_map/ppermute | solution.py:323
  (32 other events, 312.6 us)

commit v2 on v1

--- a/solution.py
+++ b/solution.py
@@ -8,7 +8,9 @@
 from jax.sharding import PartitionSpec as P
 
 F32, BF16 = jnp.float32, jnp.bfloat16
-VMEM_LIMIT = 40 * 1024 * 1024
+VMEM_LIMIT = 16 * 1024 * 1024
+BIG_LIMIT = 59 * 1024 * 1024
+TILE, AHEAD = 384, 2
 ROWS = (((0,), (0,)), ((), ()))
 LANES = (((1,), (1,)), ((), ()))
 PLAIN = (((1,), (0,)), ((), ()))
@@ -18,27 +20,29 @@
     return lax.dot_general(a, b, dims, preferred_element_type=F32)
 
 
-def params():
-    return pltpu.CompilerParams(vmem_limit_bytes=VMEM_LIMIT)
+SMALL = pl.CostEstimate(flops=1000000, bytes_accessed=10000, transcendentals=0)
+
+LARGE = pl.CostEstimate(flops=30000000000, bytes_accessed=10000, transcendentals=0)
+
+
+def params(limit=VMEM_LIMIT):
+    return pltpu.CompilerParams(vmem_limit_bytes=limit)
 
 
 def whole(count):
     return [pl.BlockSpec(memory_space=pltpu.VMEM)] * count
 
 
-def scale_kernel(mantissa_ref, exponent_ref, low_ref, high_ref):
+def scale_kernel(mantissa_ref, exponent_ref, rows_ref):
     exponents = exponent_ref[...]
     scale = jnp.zeros(exponents.shape, F32)
     for power in range(-2, 3):
         scale = scale + jnp.where(exponents == power, F32(2.0**power), F32(0.0))
     columns = scale.T
-    half = low_ref.shape[0]
     width = mantissa_ref.shape[1] // exponents.shape[0]
     for block in range(exponents.shape[0]):
         lanes = slice(block * width, (block + 1) * width)
-        piece = (mantissa_ref[:, lanes].astype(F32) * columns[:, block : block + 1]).astype(BF16)
-        low_ref[:, lanes] = piece[:half]
-        high_ref[:, lanes] = piece[half:]
+        rows_ref[:, lanes] = (mantissa_ref[:, lanes].astype(F32) * columns[:, block : block + 1]).astype(BF16)
 
 
 def share_table(routes, weights, experts):
@@ -50,14 +54,12 @@
 
 
 def pack_kernel(
-    own_ref, low_ref, high_ref, second_ref, routes_ref, weights_ref, stored_ref, first_ref, gate_ref, out_ref
+    own_ref, rows_ref, second_ref, routes_ref, weights_ref, stored_ref, first_ref, gate_ref, out_ref
 ):
     devices, cap = stored_ref.shape[0], stored_ref.shape[1]
     rank = second_ref.shape[0]
     gate = gate_ref[own_ref[0]]
-    reduced = jnp.concatenate(
-        [dot(second_ref[...], low_ref[...], LANES), dot(second_ref[...], high_ref[...], LANES)], axis=1
-    ).astype(BF16)
+    reduced = dot(second_ref[...], rows_ref[...], LANES).astype(BF16)
     table = share_table(routes_ref[...], weights_ref[...].astype(F32), devices).astype(BF16)
     first = first_ref[...]
     pad = jnp.zeros((rank, out_ref.shape[2] - cap), BF16)
@@ -83,8 +85,9 @@
     return jnp.sum(jnp.where(rows == row, table, F32(0.0)), axis=0, keepdims=True)
 
 
-def xor_mask(j):
-    return ((j >> 3) & 1) | (((j >> 2) & 1) << 1) | (((j >> 1) & 1) << 2) | ((j & 1) << 3)
+def chunk_of(j, own, devices):
+    half = devices // 2
+    return 2 * j + (own & 1) if j < half else 2 * (j - half) + ((own & 1) ^ 1)
 
 
 def low_rank_kernel(
@@ -95,8 +98,7 @@
     gate_ref,
     routes_ref,
     weights_ref,
-    low_ref,
-    high_ref,
+    rows_ref,
     out_ref,
     wide_ref,
     narrow_ref,
@@ -135,12 +137,11 @@
     coarse = pulled.astype(BF16)
     fine = (pulled - coarse.astype(F32)).astype(BF16)
     both = jnp.concatenate([coarse, fine], axis=0)
-    half = low_ref.shape[0]
-    result = dot(both[:, :half], low_ref[...], PLAIN) + dot(both[:, half:], high_ref[...], PLAIN)
+    result = dot(both, rows_ref[...], PLAIN)
     wide_ref[...] = result[:rank] + result[rank:]
     columns = wide_ref.shape[1] // devices
     for j in range(devices):
-        chunk = own ^ xor_mask(j)
+        chunk = chunk_of(j, own, devices)
         for b in range(columns // 128):
             lanes = pl.ds(pl.multiple_of(chunk * columns + b * 128, 128), 128)
             out_ref[j, b * rank : (b + 1) * rank, :] = wide_ref[:, lanes]
@@ -153,11 +154,11 @@
     rank = second_ref.shape[0]
     columns = second_ref.shape[1] // devices
     for j in range(devices):
-        chunk = own ^ xor_mask(j)
+        chunk = chunk_of(j, own, devices)
         for b in range(columns // 128):
             lanes = pl.ds(pl.multiple_of(chunk * columns + b * 128, 128), 128)
-            second_ref[:, lanes] = got_ref[j, b * rank : (b + 1) * rank, :]
-        narrow_ref[chunk] = got_ref[j, 64:80, :]
+            second_ref[:, lanes] = got_ref[j, b * rank : (b + 1) * rank, :].astype(F32)
+        narrow_ref[chunk] = got_ref[j, 64:80, :].astype(F32)
     for i in range(2 * (first_ref.shape[1] // 128)):
         first_ref[(i % 2) * 16 : (i % 2) * 16 + 16, (i // 2) * 128 : (i // 2) * 128 + 128] = narrow_ref[i]
     gate_ref[...] = narrow_ref[devices - 1][0:8]
@@ -166,10 +167,6 @@
 def expert_kernel(
     place_ref,
     gate_ref,
-    a0_ref,
-    a1_ref,
-    b0_ref,
-    b1_ref,
     weight_ref,
     other_weight_ref,
     stored_ref,
@@ -177,118 +174,200 @@
     first_ref,
     got_ref,
     *rest,
+    layout,
+    slot,
 ):
-    hidden_ref, other_hidden_ref, dots_ref, rows_ref, sem = rest[-5:]
-    step = pl.program_id(0)
+    hidden_out, other_out, dots_ref, rows_ref, held_ref, kept_ref, hidden_ref = rest[-15:-8]
+    adapted_ref, chosen_ref, shares_ref, results_ref, load_sem, held_sem, kept_sem, write_sem = rest[-8:]
+    tile = held_ref.shape[1]
+    tiles = weight_ref.shape[1] // tile
     own, is_end = place_ref[0], place_ref[1]
-    half = a0_ref.shape[0]
     cap = stored_ref.shape[1]
     rank = first_ref.shape[0]
-    tokens = 2 * half
-
-    @pl.when(step == 0)
-    def _():
-        def load(first_half, second_half):
-            one = pltpu.make_async_copy(first_half, rows_ref.at[0:half], sem.at[0])
-            two = pltpu.make_async_copy(second_half, rows_ref.at[half:tokens], sem.at[1])
-            one.start()
-            two.start()
-            one.wait()
-            two.wait()
-
-        @pl.when(is_end == 1)
+    units = len(layout)
+    tokens = rows_ref.shape[0] // units
+    choices, taken = ([], []), 0
+    for unit, counts in enumerate(layout):
+        for role, count in enumerate(counts):
+            begin = unit * tokens
+            for k in range(count):
+                piece = rest[taken]
+                target = rows_ref.at[begin : begin + piece.shape[0]]
+                choices[role].append(pltpu.make_async_copy(piece, target, load_sem.at[len(choices[role])]))
+                begin += piece.shape[0]
+                taken += 1
+    for flag, copies in ((1, choices[0]), (0, choices[1])):
+
+        @pl.when(is_end == flag)
         def _():
-            load(a0_ref, a1_ref)
-
-        @pl.when(is_end == 0)
+            for copy in copies:
+                copy.start()
+
+    kept = []
+    for k, stored in enumerate((stored_ref, other_stored_ref)):
+        for unit in range(units):
+            kept.append(
+                pltpu.make_async_copy(
+                    stored.at[place_ref[2 + unit]], kept_ref.at[k, unit], kept_sem.at[k * units + unit]
+                )
+            )
+            kept[-1].start()
+
+    def load(n):
+        begin = pl.multiple_of(n % tiles * tile, tile)
+        at = lambda weight: pltpu.make_async_copy(weight.at[0, pl.ds(begin, tile)], held_ref.at[n], held_sem.at[n])
+
+        @pl.when(n < tiles)
         def _():
-            load(b0_ref, b1_ref)
-
-        dots_ref[...] = jnp.zeros(dots_ref.shape, F32)
-
-    def work(expert, row, weight_block, stored_block, hidden_block):
-        share = take_row(got_ref[0, 2 * rank :, :].astype(F32), expert)
-        slot = slot_of(jnp.broadcast_to(share, (8, tokens)))[0:1]
-        chosen = jnp.where(
-            lax.broadcasted_iota(jnp.int32, (cap, tokens), 0) == slot, F32(1.0), F32(0.0)
-        ).astype(BF16)
-        grad = dot(weight_block[0], rows_ref[...], LANES)
-        grad = grad + gate_ref[expert] * dot(first_ref[...], got_ref[0, 0:rank, :], ROWS)
-        by_token = dot(stored_block[0], chosen, ROWS)
-        rows = lax.broadcasted_iota(jnp.int32, dots_ref.shape, 0)
-        partial = jnp.sum(by_token * grad, axis=0, keepdims=True)
-        dots_ref[...] += jnp.where(rows == row, partial, F32(0.0))
-        hidden_block[0] = dot(chosen, (share * grad).astype(BF16), LANES).astype(BF16)
-
-    steps = pl.num_programs(0) // 2
-
-    @pl.when(step < steps)
-    def _():
-        work(own, 0, weight_ref, stored_ref, hidden_ref)
-
-    @pl.when(step >= steps)
-    def _():
-        work(own ^ 1, 1, other_weight_ref, other_stored_ref, other_hidden_ref)
-
-
-def expert_call(place, gate, buffers, weight, other_weight, stored, other_stored, first, got, turn, prev):
-    devices, cap, hidden = stored.shape
-    half, width = buffers[0].shape
-    tile = 256
-    steps = hidden // tile
-    near = lambda n: jnp.minimum(n, steps - 1)
-    far = lambda n: jnp.maximum(n - steps, 0)
+            at(weight_ref).start()
+
+        @pl.when(n >= tiles)
+        def _():
+            at(other_weight_ref).start()
+
+    for n in range(AHEAD):
+        load(jnp.int32(n))
+
+    place = lax.broadcasted_iota(jnp.int32, (cap, tokens), 0)
+    for unit in range(units):
+        source = place_ref[2 + unit]
+        table = got_ref[source, 2 * rank :, :].astype(F32)
+        shares = jnp.concatenate(
+            [take_row(table, own), take_row(table, own ^ 1), jnp.zeros((6, tokens), F32)], axis=0
+        )
+        slots = slot_of(shares)
+        columns = shares.T
+        adapted_ref[unit] = dot(got_ref[source, 0:rank, :], first_ref[...], ROWS)
+        for k in range(2):
+            chosen_ref[k, unit] = jnp.where(place == slots[k : k + 1], F32(1.0), F32(0.0)).astype(BF16)
+            shares_ref[k, unit] = jnp.broadcast_to(columns[:, k : k + 1], (tokens, 128))
+    results_ref[...] = jnp.zeros(results_ref.shape, F32)
+    for copy in kept:
+        copy.wait()
+    for flag, copies in ((1, choices[0]), (0, choices[1])):
+
+        @pl.when(is_end == flag)
+        def _():
+            for copy in copies:
+                copy.wait()
+
+    lane = lax.broadcasted_iota(jnp.int32, (tokens, 128), 1)
+
+    @pl.loop(0, 2 * tiles)
+    def _(n):
+        @pl.when(n + AHEAD < 2 * tiles)
+        def _():
+            load(n + AHEAD)
+
+        k = n // tiles
+        span = pl.ds(pl.multiple_of(n % tiles * tile, tile), tile)
+        pltpu.make_async_copy(weight_ref.at[0, 0:tile], held_ref.at[n], held_sem.at[n]).wait()
+        grads = dot(rows_ref[...], held_ref[n], LANES)
+        gate = gate_ref[own ^ k]
+        for unit in range(units):
+            chosen = chosen_ref[k, unit]
+            by_token = dot(chosen, kept_ref[k, unit, :, span], ROWS)
+            grad = grads[unit * tokens : (unit + 1) * tokens] + gate * adapted_ref[unit, :, span]
+            partial = jnp.sum(by_token * grad, axis=1, keepdims=True)
+            results_ref[unit] += jnp.where(lane == k, partial, F32(0.0))
+            shared = dot(chosen, (shares_ref[k, unit, :, 0:1] * grad).astype(BF16), PLAIN)
+            hidden_ref[k, unit, :, span] = shared.astype(BF16)
+
+    writes = []
+    for unit in range(units):
+        for k, target in enumerate((hidden_out.at[place_ref[2 + unit]], other_out.at[slot + unit])):
+            writes.append(pltpu.make_async_copy(hidden_ref.at[k, unit], target, write_sem.at[len(writes)]))
+            writes[-1].start()
+    for unit in range(units):
+        dots_ref[unit] = results_ref[unit].T[:8]
+    for copy in writes:
+        copy.wait()
+
+
+def expert_call(place, gate, weight, other_weight, stored, other_stored, first, got, buffers, hidden, other, slot):
+    devices, cap, width_hidden = stored.shape
+    layout = [(len(as_end), len(as_mid)) for as_end, as_mid in buffers]
+    pieces = [piece for pair in buffers for side in pair for piece in side]
+    width = pieces[0].shape[1]
+    tokens = got.shape[2]
+    units = len(buffers)
     any_spec = pl.BlockSpec(memory_space=pl.ANY)
-    in_specs = [any_spec] * 4 + [
-        pl.BlockSpec((1, tile, width), lambda n, p, g: (0, near(n), 0)),
-        pl.BlockSpec((1, tile, width), lambda n, p, g: (0, far(n), 0)),
-        pl.BlockSpec((1, cap, tile), lambda n, p, g: (p[2], 0, near(n))),
-        pl.BlockSpec((1, cap, tile), lambda n, p, g: (p[2], 0, far(n))),
-        pl.BlockSpec((first.shape[0], tile), lambda n, p, g: (0, n % steps)),
-        pl.BlockSpec((1,) + got.shape[1:], lambda n, p, g: (p[2], 0, 0)),
-    ]
-    operands = [place, gate, *buffers, weight, other_weight, stored, other_stored, first, got]
-    aliases = {}
-    if prev is not None:
-        aliases = {len(operands): 0, len(operands) + 1: 1}
-        operands += list(prev)
-        in_specs += [any_spec, any_spec]
-    flops = 2 * 2 * half * width * 2 * hidden
+    smem = pl.BlockSpec(memory_space=pltpu.SMEM)
+    operands = [place, gate, weight, other_weight, stored, other_stored, first, got, *pieces]
+    in_specs = [smem] * 2 + [any_spec] * 4 + whole(2) + [any_spec] * len(pieces)
+    aliases, sizes = {}, []
+    for number, value in enumerate((hidden, other)):
+        if isinstance(value, int):
+            sizes.append(value)
+        else:
+            sizes.append(value.shape[0])
+            aliases[len(operands)] = number
+            operands.append(value)
+            in_specs.append(any_spec)
+    loads = max(sum(counts[role] for counts in layout) for role in range(2))
     return pl.pallas_call(
-        expert_kernel,
-        grid_spec=pltpu.PrefetchScalarGridSpec(
-            num_scalar_prefetch=2,
-            grid=(2 * steps,),
-            in_specs=in_specs,
-            out_specs=[
-                pl.BlockSpec((1, cap, tile), lambda n, p, g: (p[2], 0, near(n))),
-                pl.BlockSpec((1, cap, tile), lambda n, p, g: (turn, 0, far(n))),
-                pl.BlockSpec((8, 2 * half), lambda n, p, g: (0, 0)),
-            ],
-            scratch_shapes=[pltpu.VMEM((2 * half, width), BF16), pltpu.SemaphoreType.DMA((2,))],
-        ),
+        functools.partial(expert_kernel, layout=layout, slot=slot),
+        in_specs=in_specs,
+        out_specs=[any_spec, any_spec, pl.BlockSpec(memory_space=pltpu.VMEM)],
         out_shape=[
-            jax.ShapeDtypeStruct((devices, cap, hidden), BF16),
-            jax.ShapeDtypeStruct((devices // 2, cap, hidden), BF16),
-            jax.ShapeDtypeStruct((8, 2 * half), F32),
+            jax.ShapeDtypeStruct((sizes[0], cap, width_hidden), BF16),
+            jax.ShapeDtypeStruct((sizes[1], cap, width_hidden), BF16),
+            jax.ShapeDtypeStruct((units, 8, tokens), F32),
+        ],
+        scratch_shapes=[
+            pltpu.VMEM((units * tokens, width), BF16),
+            pltpu.VMEM((2 * width_hidden // TILE, TILE, width), BF16),
+            pltpu.VMEM((2, units, cap, width_hidden), BF16),
+            pltpu.VMEM((2, units, cap, width_hidden), BF16),
+            pltpu.VMEM((units, tokens, width_hidden), F32),
+            pltpu.VMEM((2, units, cap, tokens), BF16),
+            pltpu.VMEM((2, units, tokens, 128), F32),
+            pltpu.VMEM((units, tokens, 128), F32),
+            pltpu.SemaphoreType.DMA((loads,)),
+            pltpu.SemaphoreType.DMA((2 * width_hidden // TILE,)),
+            pltpu.SemaphoreType.DMA((2 * units,)),
+            pltpu.SemaphoreType.DMA((2 * units,)),
         ],
         input_output_aliases=aliases,
+        compiler_params=params(BIG_LIMIT),
+        cost_estimate=SMALL,
+    )(*operands)
+
+
+def place_kernel(own_ref, *refs, masks):
+    hidden_ref, sem = refs[-2:]
+    copies = []
+    for moved_ref, turns in zip(refs, masks):
+        for k, mask in enumerate(turns):
+            source = own_ref[0] ^ 1 ^ (mask << 1)
+            copies.append(pltpu.make_async_copy(moved_ref.at[k], hidden_ref.at[source], sem.at[len(copies)]))
+    for copy in copies:
+        copy.start()
+    for copy in copies:
+        copy.wait()
+
+
+def place_call(own1, moved, hidden, masks):
+    any_spec = pl.BlockSpec(memory_space=pl.ANY)
+    return pl.pallas_call(
+        functools.partial(place_kernel, masks=masks),
+        in_specs=[pl.BlockSpec(memory_space=pltpu.SMEM)] + whole(len(moved)) + [any_spec],
+        out_specs=any_spec,
+        out_shape=jax.ShapeDtypeStruct(hidden.shape, hidden.dtype),
+        input_output_aliases={1 + len(moved): 0},
+        scratch_shapes=[pltpu.SemaphoreType.DMA((sum(len(turns) for turns in masks),))],
         compiler_params=params(),
-        cost_estimate=pl.CostEstimate(flops=flops, bytes_accessed=2 * 2 * hidden * width, transcendentals=0),
-    )(*operands)
-
-
-def finish_kernel(own_ref, masks, *refs):
+        cost_estimate=SMALL,
+    )(own1, *moved, hidden)
+
+
+def finish_kernel(own_ref, *refs, masks):
     count = len(masks)
     dots, routes_ref, moved_ref = refs[:count], refs[count], refs[count + 1]
     routing_ref, hidden_ref, sem = refs[count + 3 :]
     own = own_ref[0]
-    copies = []
-    for k, mask in enumerate(masks):
-        source = own ^ 1 ^ (mask << 1)
-        copies.append(pltpu.make_async_copy(moved_ref.at[k], hidden_ref.at[source], sem.at[k]))
-    for copy in copies:
-        copy.start()
+    copy = pltpu.make_async_copy(moved_ref.at[0], hidden_ref.at[own ^ 1 ^ (masks[-1] << 1)], sem)
+    copy.start()
     routes = routes_ref[...]
     total = jnp.zeros(routes.shape, F32)
     for k, mask in enumerate(masks):
@@ -296,8 +375,7 @@
             expert = own ^ (mask << 1) ^ row
             total = total + jnp.where(routes == expert, dots[k][row : row + 1, :], F32(0.0))
     routing_ref[...] = total
-    for copy in copies:
-        copy.wait()
+    copy.wait()
 
 
 def permutes():
@@ -308,10 +386,8 @@
         near=[(number(z, x, c), number(z ^ 1, x, c)) for z, x, c in places],
         mid=[(number(z, x, c), number(3 - z, x, c)) for z, x, c in places if not end(z)],
         out=[(number(z, x, c), number(z ^ 1, x, c)) for z, x, c in places if not end(z)],
-        inward=[(number(z, x, c), number(z ^ 1, x, c)) for z, x, c in places if end(z)],
         side=[(number(z, x, c), number(z, 1 - x, c)) for z, x, c in places],
         end_side=[(number(z, x, c), number(z, 1 - x, c)) for z, x, c in places if end(z)],
-        mid_side=[(number(z, x, c), number(z, 1 - x, c)) for z, x, c in places if not end(z)],
     )
 
 
@@ -323,41 +399,8 @@
     return lax.ppermute(value, "ex", pairs)
 
 
-def spread(low, high):
-    to = permutes()
-    own = [low, high]
-    near = [send(h, to["near"]) for h in own]
-    mid = [send(h, to["mid"]) for h in own]
-    side = [send(h, to["side"]) for h in own]
-    out2 = [send(h, to["out"]) for h in mid]
-    mid2 = [send(h, to["mid"]) for h in near]
-    in2 = [send(h, to["inward"]) for h in side]
-    end1 = [send(h, to["end_side"]) for h in near]
-    mids1 = [send(h, to["mid_side"]) for h in mid]
-    out3 = [send(h, to["out"]) for h in mid2]
-    end2 = [send(h, to["end_side"]) for h in out2]
-    mids2 = [send(h, to["mid_side"]) for h in mid2]
-    end3 = send(out3[0], to["end_side"])
-    last = send(mids2[1], to["out"])
-    return {
-        0: (own, own),
-        2: (near, near),
-        1: (side, side),
-        4: (out2, mid2),
-        3: (end1, in2),
-        6: (out3, mid),
-        5: (end2, mids2),
-        7: ([end3, last], mids1),
-    }
-
-
-def sum_over_group(value):
-    for bit in (1, 2, 4, 8):
-        half = value.shape[0] // 2
-        value = value[:half] + send(value[half:], xor_pairs(bit))
-    for bit in (8, 4, 2, 1):
-        value = jnp.concatenate([value, send(value, xor_pairs(bit))], axis=0)
-    return value
+def then(value, *earlier):
+    return lax.optimization_barrier((value, *earlier))[0]
 
 
 def small_body(
@@ -381,36 +424,111 @@
     own1 = own.reshape(1)
     z = own >> 2
     is_end = ((z == 0) | (z == 3)).astype(jnp.int32)
+
     smem = pl.BlockSpec(memory_space=pltpu.SMEM)
+    vmem = pl.BlockSpec(memory_space=pltpu.VMEM)
+    any_spec = pl.BlockSpec(memory_space=pl.ANY)
+    to = permutes()
+    pick = lambda as_end, as_mid: jnp.where(is_end == 1, as_end, as_mid)
+
+    smem = pl.BlockSpec(memory_space=pltpu.SMEM)
+    vmem = pl.BlockSpec(memory_space=pltpu.VMEM)
+    any_spec = pl.BlockSpec(memory_space=pl.ANY)
+    to = permutes()
+    pick = lambda as_end, as_mid: jnp.where(is_end == 1, as_end, as_mid)
 
     other_weight = send(frozen_down_weight, xor_pairs(1))
     other_stored = send(stored, xor_pairs(1))
-    low, high = pl.pallas_call(
+    rows = pl.pallas_call(
         scale_kernel,
         in_specs=whole(2),
-        out_specs=whole(2),
-        out_shape=[jax.ShapeDtypeStruct((tokens // 2, width), BF16)] * 2,
+        out_specs=vmem,
+        out_shape=jax.ShapeDtypeStruct((tokens, width), BF16),
         compiler_params=params(),
+        cost_estimate=SMALL,
     )(gradient_mantissas, gradient_exponents.T)
-    buffers = spread(low, high)
-
+    masks = (0, 2, 1, 4, 3, 6, 5, 7)
+    final = len(masks) - 1
+    half = tokens // 2
+    dots, hidden_part, other_part = [], devices, 5
+
+    def experts(count, buffers, *earlier):
+        nonlocal hidden_part, other_part
+        begin = len(dots)
+        turns = masks[begin : begin + count]
+        place = jnp.stack([own, is_end] + [own ^ (mask << 1) for mask in turns])
+        hidden_part, other_part, found = expert_call(
+            then(place, *earlier),
+            expert_adapter_gate,
+            frozen_down_weight,
+            other_weight,
+            stored,
+            other_stored,
+            first,
+            got,
+            buffers,
+            hidden_part,
+            other_part,
+            begin if begin < 5 else 0,
+        )
+        for k, mask in enumerate(turns):
+            dots.append(send(found[k], xor_pairs(mask << 1)) if mask else found[k])
+        return found
+
+    near, side, mid = send(rows, to["near"]), send(rows, to["side"]), send(rows, to["mid"])
     packed = pl.pallas_call(
         pack_kernel,
-        in_specs=[smem] + whole(7) + [smem],
-        out_specs=pl.BlockSpec(memory_space=pltpu.VMEM),
+        in_specs=[smem] + whole(6) + [smem],
+        out_specs=vmem,
         out_shape=jax.ShapeDtypeStruct((devices, 2 * rank + devices, tokens), BF16),
         compiler_params=params(),
-    )(own1, low, high, adapter_second_factor, routes_t, weights_t, stored, first, expert_adapter_gate)
+        cost_estimate=SMALL,
+    )(
+        then(own1, other_stored),
+        rows,
+        adapter_second_factor,
+        routes_t,
+        weights_t,
+        stored,
+        first,
+        expert_adapter_gate,
+    )
     got = lax.all_to_all(packed, "ex", split_axis=0, concat_axis=0, tiled=True)
+    near, side, mid, _, _ = lax.optimization_barrier((near, side, mid, got, other_weight))
+    near2 = send(pick(side, mid), to["near"])
+    side2 = send(pick(near, mid), to["side"])
+    mid2 = send(near, to["mid"])
     partial = pl.pallas_call(
         low_rank_kernel,
-        in_specs=[smem] + whole(3) + [smem] + whole(4),
-        out_specs=pl.BlockSpec(memory_space=pltpu.VMEM),
+        in_specs=[smem] + whole(3) + [smem] + whole(3),
+        out_specs=vmem,
         out_shape=jax.ShapeDtypeStruct((devices, 80, 128), F32),
         scratch_shapes=[pltpu.VMEM((rank, width), F32), pltpu.VMEM((devices, 16, 128), F32)],
         compiler_params=params(),
-    )(own1, got, stored, first, expert_adapter_gate, routes_t, weights_t, low, high)
-    summed = sum_over_group(partial)
+        cost_estimate=SMALL,
+    )(then(own1, near, side, mid), got, stored, first, expert_adapter_gate, routes_t, weights_t, rows)
+    lanes = [[2 * chip + core for chip in range(devices // 2)] for core in range(2)]
+    among_lane = lambda value: lax.all_to_all(
+        value, "ex", split_axis=0, concat_axis=0, axis_index_groups=lanes, tiled=True
+    )
+    found = experts(3, [([rows], [rows]), ([near], [near]), ([side], [side])], partial, near, side, mid)
+    near2, mid2, side2, partial, _ = lax.optimization_barrier((near2, mid2, side2, partial, found))
+    pair = (partial[: devices // 2] + send(partial[devices // 2 :], xor_pairs(1))).astype(BF16)
+    parts = among_lane(pair)
+    near3 = send(mid2, to["out"])
+    side3 = send(pick(near2, mid2), to["side"])
+    found = experts(2, [([near2], [mid2]), ([side2], [near2])], near2, side2, mid2)
+    summed = jnp.sum(then(parts, found).astype(F32), axis=0).astype(BF16)
+    near3, side3, _, summed = lax.optimization_barrier((near3, side3, found, summed))
+    summed = among_lane(jnp.broadcast_to(summed[None], (devices // 2, 80, 128)))
+    last = [send(near3[:half], to["end_side"]), send(side3[half:], to["out"])]
+    moved, other_part = [send(then(other_part, found), xor_pairs(1))], 2
+    found = experts(2, [([near3], [mid]), ([side3], [side3])], near3, side3, moved[0])
+    summed = jnp.concatenate([summed, send(summed, xor_pairs(1))], axis=0)
+    moved.append(send(other_part, xor_pairs(1)))
+    other_part = 1
+    found = experts(1, [(last, [side2])], *last)
+    last_moved = send(other_part, xor_pairs(1))
     second_grad, first_grad, gate_grad = pl.pallas_call(
         unpack_kernel,
         in_specs=[smem] + whole(1),
@@ -422,41 +540,22 @@
         ],
         scratch_shapes=[pltpu.VMEM((devices, 16, 128), F32)],
         compiler_params=params(),
-    )(own1, summed)
-
-    masks = (0, 2, 1, 4, 3, 6, 5, 7)
-    dots, prev = [], None
-    for turn, mask in enumerate(masks):
-        place = jnp.stack([own, is_end, own ^ (mask << 1)])
-        as_end, as_mid = buffers[mask]
-        *prev, dot_rows = expert_call(
-            place,
-            expert_adapter_gate,
-            [*as_end, *as_mid],
-            frozen_down_weight,
-            other_weight,
-            stored,
-            other_stored,
-            first,
-            got,
-            turn,
-            prev,
-        )
-        dots.append(send(dot_rows, xor_pairs(mask << 1)) if mask else dot_rows)
-    hidden_part, other_part = prev
-    moved = send(other_part, xor_pairs(1))
-    any_spec = pl.BlockSpec(memory_space=pl.ANY)
+        cost_estimate=SMALL,
+    )(then(own1, found), summed)
+    hidden_part = place_call(own1, moved, hidden_part, (masks[:5], masks[5:final]))
+    moved = last_moved
     routing_t, hidden_gradient = pl.pallas_call(
-        lambda own_ref, *refs: finish_kernel(own_ref, masks, *refs),
-        in_specs=[smem] + whole(len(masks) + 1) + [any_spec, any_spec],
-        out_specs=[pl.BlockSpec(memory_space=pltpu.VMEM), any_spec],
+        functools.partial(finish_kernel, masks=masks),
+        in_specs=[smem] + whole(len(masks) + 2) + [any_spec],
+        out_specs=[vmem, any_spec],
         out_shape=[
             jax.ShapeDtypeStruct(routes_t.shape, F32),
             jax.ShapeDtypeStruct((devices, cap, hidden), BF16),
         ],
         input_output_aliases={len(masks) + 3: 1},
-        scratch_shapes=[pltpu.SemaphoreType.DMA((len(masks),))],
+        scratch_shapes=[pltpu.SemaphoreType.DMA],
         compiler_params=params(),
+        cost_estimate=SMALL,
     )(own1, *dots, routes_t, moved, hidden_part)
     return (
         hidden_gradient[None],

time: 246 us -> 160 us (0.65)
  Pallas kernels: 95.4 us -> 55.5 us
  starting transfers between devices: 85.7 us -> 49.5 us
  waiting for transfers between devices: 48.9 us -> 35.4 us
  other arithmetic: 1.08 us -> 9.28 us
  local copies, waits for them, and re-layouts: 12.1 us -> 7.91 us
    ppermute x42 -> x24, starting transfers between devices: 80.7 us -> 34.5 us  [send(): return lax.ppermute(value, 'ex', pairs)]
    pallas_call x11 -> x8, Pallas kernels: 89 us -> 50.6 us  [the longest x4 46.2 us: expert_call(): pl.pallas_call(functools.partial(expert_kernel, layout=layout, slot=slot)...]
    ppermute x42 -> x24, waiting for transfers between devices: 48.3 us -> 23.3 us  [send(): return lax.ppermute(value, 'ex', pairs)]
    all_to_all x0 -> x2, starting transfers between devices: none -> 7.67 us  [small_body(): lax.all_to_all(value, 'ex', split_axis=0, concat_axis=0, axis_index_group...]
    unnamed x45 -> x32, local copies, waits for them, and re-layouts: 10.9 us -> 3.66 us
    all_to_all x1, waiting for transfers between devices: 0.65 us -> 7.89 us  [small_body(): got = lax.all_to_all(packed, 'ex', split_axis=0, concat_axis=0, tiled=True)]
    select_n x0 -> x2, other arithmetic: none -> 5.72 us  [small_body(): pick = lambda as_end, as_mid: jnp.where(is_end == 1, as_end, as_mid)]
    all_to_all x0 -> x2, waiting for transfers between devices: none -> 4.21 us  [small_body(): lax.all_to_all(value, 'ex', split_axis=0, concat_axis=0, axis_index_group...]
  transfers between devices with their start and end apart: 43 -> 27, of which waited for: 12 -> 10; matrix products, arithmetic and copies ran while one was open for 1% -> 9% of each run, Pallas kernels for 38% -> 34%
where the time goes in v2:
time: 160 us; the launch traced here: 159 us
  Pallas kernels  55.5 us (35%)
  starting transfers between devices  49.5 us (31%)
  waiting for transfers between devices  35.4 us (22%)
  other arithmetic  9.28 us (6%)
  local copies, waits for them, and re-layouts  7.91 us (5%)
    pallas_call x4, Pallas kernels, expert_call(): pl.pallas_call(functools.partial(expert_kernel, layout=layout, slot=slot)...  46.2 us
    ppermute x24, starting transfers between devices, send(): return lax.ppermute(value, 'ex', pairs)  34.5 us
    ppermute x24, waiting for transfers between devices, send(): return lax.ppermute(value, 'ex', pairs)  23.3 us
    all_to_all x1, waiting for transfers between devices, small_body(): got = lax.all_to_all(packed, 'ex', split_axis=0, concat_axis=0, tiled=True)  7.89 us
    all_to_all x2, starting transfers between devices, small_body(): lax.all_to_all(value, 'ex', split_axis=0, concat_axis=0, axis_index_group...  7.67 us
    all_to_all x1, starting transfers between devices, small_body(): got = lax.all_to_all(packed, 'ex', split_axis=0, concat_axis=0, tiled=True)  7.28 us
    select_n x2, other arithmetic, small_body(): pick = lambda as_end, as_mid: jnp.where(is_end == 1, as_end, as_mid)  5.72 us
    all_to_all x2, waiting for transfers between devices, small_body(): lax.all_to_all(value, 'ex', split_axis=0, concat_axis=0, axis_index_group...  4.21 us
  transfers between devices with their start and end apart: 27, of which 10 were waited for; matrix products, arithmetic and copies ran while one was open for 9% of the time, Pallas kernels for 34%

profile of v2, /device:TPU:0, one launch (start us, length us, event | category | flops | bytes accessed | tf_op | source)
XLA Modules:
  0.0 158.7 jit_solution(6401096508638684282)
XLA Ops:
  4.0 3.1 %collective-permute-start = (bf16[128,4096]{1,0:T(8,128)(2,1)S(1)}, bf16[128,4096]{1,0:T(8,128)(2,1)}, u32[]{:S(2)}, u32[]{:S(2)}) collective-permute-start(bf16[128,4096]{1,0:T(8,128)(2,1)S(1)} %shard_map.128.rows_ref.rest_0_.rest_1_), channel_id=1, source_target_pairs={{0,4},{1,5},{2,6},{3,7},{4,0},{5,1},{6,2},{7,3},{8,12},{9,13},{10,... | collective-permute-start | bytes 3145736 | tf_op jit(solution)/shard_map/ppermute | solution.py:399
  7.1 1.5 collective-permute-start.1
  8.6 1.6 %collective-permute-start.2 = (bf16[128,4096]{1,0:T(8,128)(2,1)S(1)}, bf16[128,4096]{1,0:T(8,128)(2,1)}, u32[]{:S(2)}, u32[]{:S(2)}) collective-permute-start(bf16[128,4096]{1,0:T(8,128)(2,1)S(1)} %shard_map.128.rows_ref.rest_0_.rest_1_), channel_id=1, source_target_pairs={{4,8},{5,9},{6,10},{7,11},{8,4},{9,5},{10,6},{11,7},{20,24},{21,25... | collective-permute-start | bytes 3145736 | tf_op jit(solution)/shard_map/ppermute | solution.py:399
  10.2 3.9 %collective-permute-done.3.other_stored_ref = bf16[16,80,768]{2,1,0:T(8,128)(2,1)} collective-permute-done((bf16[16,80,768]{2,1,0:T(8,128)(2,1)}, bf16[16,80,768]{2,1,0:T(8,128)(2,1)}, u32[]{:S(2)}, u32[]{:S(2)}) %collective-permute-start.3) | collective-permute-done | bytes 1966112 | tf_op jit(solution)/shard_map/ppermute | solution.py:399
  17.3 7.3 %all-to-all-start = ((bf16[16,80,128]{2,1,0:T(8,128)(2,1)}), bf16[16,80,128]{2,1,0:T(8,128)(2,1)S(1)}, u32[]{:S(2)}, u32[]{:S(2)}) async-start(bf16[16,80,128]{2,1,0:T(8,128)(2,1)} %copy-done.5), calls=%async_computation | async-start | bytes 655360 | tf_op jit(solution)/shard_map/all_to_all | solution.py:496
  24.6 6.6 %collective-permute-done.rest_2_.rest_3_ = bf16[128,4096]{1,0:T(8,128)(2,1)} collective-permute-done((bf16[128,4096]{1,0:T(8,128)(2,1)S(1)}, bf16[128,4096]{1,0:T(8,128)(2,1)}, u32[]{:S(2)}, u32[]{:S(2)}) %collective-permute-start) | collective-permute-done | bytes 1048608 | tf_op jit(solution)/shard_map/ppermute | solution.py:399
  31.1 2.0 %collective-permute-done.1.rest_4_.rest_5_ = bf16[128,4096]{1,0:T(8,128)(2,1)} collective-permute-done((bf16[128,4096]{1,0:T(8,128)(2,1)S(1)}, bf16[128,4096]{1,0:T(8,128)(2,1)}, u32[]{:S(2)}, u32[]{:S(2)}) %collective-permute-start.1) | collective-permute-done | bytes 1048608 | tf_op jit(solution)/shard_map/ppermute | solution.py:399
  33.1 7.9 %all-to-all-done.got_ref = bf16[16,80,128]{2,1,0:T(8,128)(2,1)S(1)} async-done(((bf16[16,80,128]{2,1,0:T(8,128)(2,1)}), bf16[16,80,128]{2,1,0:T(8,128)(2,1)S(1)}, u32[]{:S(2)}, u32[]{:S(2)}) %all-to-all-start) | async-done | bytes 327712 | tf_op jit(solution)/shard_map/all_to_all | solution.py:496
  41.0 1.6 %collective-permute-start.8 = (bf16[128,4096]{1,0:T(8,128)(2,1)}, bf16[128,4096]{1,0:T(8,128)(2,1)}, u32[]{:S(2)}, u32[]{:S(2)}) collective-permute-start(bf16[128,4096]{1,0:T(8,128)(2,1)} %collective-permute-done.rest_2_.rest_3_), channel_id=1, source_target_pairs={{4,8},{5,9},{6,10},{7,11},{8,4},{9,5},{10,6},{11,7},{20,24},{21,25... | collective-permute-start | bytes 3145736 | tf_op jit(solution)/shard_map/ppermute | solution.py:399
  42.7 3.4 %broadcast_select_fusion.1 = (bf16[128,4096]{1,0:T(8,128)(2,1)}, bf16[128,4096]{1,0:T(8,128)(2,1)}) fusion(bf16[128,4096]{1,0:T(8,128)(2,1)} %collective-permute-done.rest_2_.rest_3_, bf16[128,4096]{1,0:T(8,128)(2,1)} %collective-permute-done.2.rest_1_, pred[]{:T(512)S(6)} %eq.13, bf16[128,4096]{1,0:T(8,128)(2,1)} %collective-permute-done.1.rest_4_.rest_5_), kind=kLoop, calls=%fused_computation.1 | loop fusion | flops 1048576 | bytes 5242881 | tf_op jit(solution)/shard_map/jit(_where)/select_n | solution.py:438
  46.0 3.8 %collective-permute-start.7 = (bf16[128,4096]{1,0:T(8,128)(2,1)}, bf16[128,4096]{1,0:T(8,128)(2,1)}, u32[]{:S(2)}, u32[]{:S(2)}) collective-permute-start(bf16[128,4096]{1,0:T(8,128)(2,1)} %get-tuple-element.78), channel_id=1, source_target_pairs={{0,4},{1,5},{2,6},{3,7},{4,0},{5,1},{6,2},{7,3},{8,12},{9,13},{10,... | collective-permute-start | bytes 3145736 | tf_op jit(solution)/shard_map/ppermute | solution.py:399
  50.6 3.9 %shard_map.130 = f32[16,80,128]{2,1,0:T(8,128)S(1)} custom-call(s32[1]{0:T(128)} %bitcast.own_ref, bf16[16,80,128]{2,1,0:T(8,128)(2,1)S(1)} %all-to-all-done.got_ref, bf16[16,80,768]{2,1,0:T(8,128)(2,1)S(1)} %bitcast.40, bf16[32,768]{1,0:T(8,128)(2,1)S(1)} %bitcast.46, f32[16]{0:T(128)S(1)} %copy-done.9, s32[8,128]{1,0:T(8,128)S(1)} %bitcast.48, ...), custom_call_target="tpu_custom_call" | custom-call | flops 1000000 | bytes 10000 | tf_op jit(solution)/shard_map/pallas_call | solution.py:501
  54.6 14.1 %shard_map.131 = (bf16[16,80,768]{2,1,0:T(8,128)(2,1)}, bf16[5,80,768]{2,1,0:T(8,128)(2,1)}, f32[3,8,128]{2,1,0:T(8,128)}) custom-call(s32[5]{0:T(128)} %stack.47.place_ref, f32[16]{0:T(128)} %gate_ref.11, bf16[1,768,4096]{2,1,0:T(8,128)(2,1)} %weight_ref.7, bf16[1,768,4096]{2,1,0:T(8,128)(2,1)} %collective-permute-done.4.other_weight_ref, ...), custom_call_target="tpu_custom_call" | custom-call | flops 1000000 | bytes 10000 | tf_op jit(solution)/shard_map/pallas_call | solution.py:308
  68.7 3.8 %collective-permute-done.7.rest_0_.rest_3_ = bf16[128,4096]{1,0:T(8,128)(2,1)} collective-permute-done((bf16[128,4096]{1,0:T(8,128)(2,1)}, bf16[128,4096]{1,0:T(8,128)(2,1)}, u32[]{:S(2)}, u32[]{:S(2)}) %collective-permute-start.7) | collective-permute-done | bytes 1048608 | tf_op jit(solution)/shard_map/ppermute | solution.py:399
  75.1 2.4 %broadcast_select_fusion = bf16[128,4096]{1,0:T(8,128)(2,1)} fusion(bf16[128,4096]{1,0:T(8,128)(2,1)} %collective-permute-done.7.rest_0_.rest_3_, bf16[128,4096]{1,0:T(8,128)(2,1)} %collective-permute-done.8.rest_1_, pred[]{:T(512)S(6)} %eq.13), kind=kLoop, calls=%fused_computation | loop fusion | flops 524288 | bytes 3145729 | tf_op jit(solution)/shard_map/jit(_where)/select_n | solution.py:438
  77.5 1.7 %collective-permute-start.13 = (bf16[128,4096]{1,0:T(8,128)(2,1)}, bf16[128,4096]{1,0:T(8,128)(2,1)S(1)}, u32[]{:S(2)}, u32[]{:S(2)}) collective-permute-start(bf16[128,4096]{1,0:T(8,128)(2,1)} %broadcast_select_fusion), channel_id=1, source_target_pairs={{0,2},{1,3},{2,0},{3,1},{4,6},{5,7},{6,4},{7,5},{8,10},{9,11},{10,... | collective-permute-start | bytes 3145736 | tf_op jit(solution)/shard_map/ppermute | solution.py:399
  79.3 1.6 %collective-permute-done.14 = f32[8,80,128]{2,1,0:T(8,128)S(1)} collective-permute-done((f32[8,80,128]{2,1,0:T(8,128)S(1)}, f32[8,80,128]{2,1,0:T(8,128)S(1)}, u32[]{:S(2)}, u32[]{:S(2)}) %collective-permute-start.14) | collective-permute-done | bytes 327712 | tf_op jit(solution)/shard_map/ppermute | solution.py:399
  80.9 1.7 %add_convert_fusion = bf16[8,80,128]{2,1,0:T(8,128)(2,1)} fusion(f32[8,80,128]{2,1,0:T(8,128)S(1)} %collective-permute-done.14, f32[16,80,128]{2,1,0:T(8,128)} %copy-done.3), kind=kLoop, calls=%fused_computation.4 | loop fusion | flops 163840 | bytes 819200 | tf_op jit(solution)/shard_map/convert_element_type | solution.py:516
  82.6 4.2 %all-to-all-start.1 = ((bf16[8,80,128]{2,1,0:T(8,128)(2,1)}), bf16[8,80,128]{2,1,0:T(8,128)(2,1)S(1)}, u32[]{:S(2)}, u32[]{:S(2)}) async-start(bf16[8,80,128]{2,1,0:T(8,128)(2,1)} %add_convert_fusion), calls=%async_computation.1 | async-start | bytes 327680 | tf_op jit(solution)/shard_map/all_to_all | solution.py:511
  87.4 11.2 %shard_map.132 = (bf16[16,80,768]{2,1,0:T(8,128)(2,1)}, bf16[5,80,768]{2,1,0:T(8,128)(2,1)}, f32[2,8,128]{2,1,0:T(8,128)}) custom-call(s32[4]{0:T(128)} %pad_add_fusion.place_ref, f32[16]{0:T(128)} %gate_ref.11, bf16[1,768,4096]{2,1,0:T(8,128)(2,1)} %weight_ref.7, ...), custom_call_target="tpu_custom_call", output_to_operand_aliasing={{0}: (12, {}), {1}: (13, {})} | custom-call | flops 1000000 | bytes 10000 | tf_op jit(solution)/shard_map/pallas_call | solution.py:308
  99.9 4.2 %all-to-all-done.1 = bf16[8,80,128]{2,1,0:T(8,128)(2,1)S(1)} async-done(((bf16[8,80,128]{2,1,0:T(8,128)(2,1)}), bf16[8,80,128]{2,1,0:T(8,128)(2,1)S(1)}, u32[]{:S(2)}, u32[]{:S(2)}) %all-to-all-start.1) | async-done | bytes 163872 | tf_op jit(solution)/shard_map/all_to_all | solution.py:511
  105.0 3.4 %collective-permute-start.18 = (bf16[64,4096]{1,0:T(8,128)(2,1)}, bf16[64,4096]{1,0:T(8,128)(2,1)}, u32[]{:S(2)}, u32[]{:S(2)}) collective-permute-start(bf16[64,4096]{1,0:T(8,128)(2,1)} %slice.45), channel_id=1, source_target_pairs={{0,2},{1,3},{2,0},{3,1},{12,14},{13,15},{14,12},{15,13},{16,18},{1... | collective-permute-start | bytes 1572872 | tf_op jit(solution)/shard_map/ppermute | solution.py:399
  109.1 3.5 %all-to-all-start.2 = ((bf16[8,80,128]{2,1,0:T(8,128)(2,1)}), bf16[8,80,128]{2,1,0:T(8,128)(2,1)S(1)}, u32[]{:S(2)}, u32[]{:S(2)}) async-start(bf16[8,80,128]{2,1,0:T(8,128)(2,1)} %broadcast_in_dim.10), calls=%async_computation.2 | async-start | bytes 327680 | tf_op jit(solution)/shard_map/all_to_all | solution.py:511
  112.6 2.1 %collective-permute-start.5 = (f32[8,128]{1,0:T(8,128)S(1)}, f32[8,128]{1,0:T(8,128)S(1)}, u32[]{:S(2)}, u32[]{:S(2)}) collective-permute-start(f32[8,128]{1,0:T(8,128)S(1)} %get-tuple-element.80), channel_id=1, source_target_pairs={{0,4},{1,5},{2,6},{3,7},{4,0},{5,1},{6,2},{7,3},{8,12},{9,13},{10,... | collective-permute-start | bytes 12296 | tf_op jit(solution)/shard_map/ppermute | solution.py:399
  117.0 11.2 %shard_map.133 = (bf16[16,80,768]{2,1,0:T(8,128)(2,1)}, bf16[2,80,768]{2,1,0:T(8,128)(2,1)}, f32[2,8,128]{2,1,0:T(8,128)}) custom-call(s32[4]{0:T(128)} %pad_add_fusion.2.place_ref, f32[16]{0:T(128)} %gate_ref.11, bf16[1,768,4096]{2,1,0:T(8,128)(2,1)} %weight_ref.7, ...), custom_call_target="tpu_custom_call", output_to_operand_aliasing={{0}: (12, {})} | custom-call | flops 1000000 | bytes 10000 | tf_op jit(solution)/shard_map/pallas_call | solution.py:308
  130.0 1.5 collective-permute-start.6
  131.5 4.2 %collective-permute-start.10 = (f32[8,128]{1,0:T(8,128)S(1)}, f32[8,128]{1,0:T(8,128)S(1)}, u32[]{:S(2)}, u32[]{:S(2)}) collective-permute-start(f32[8,128]{1,0:T(8,128)S(1)} %get-tuple-element.85), channel_id=1, source_target_pairs={{0,8},{1,9},{2,10},{3,11},{4,12},{5,13},{6,14},{7,15},{8,0},{9,1},... | collective-permute-start | bytes 12296 | tf_op jit(solution)/shard_map/ppermute | solution.py:399
  135.8 9.7 %shard_map.134 = (bf16[16,80,768]{2,1,0:T(8,128)(2,1)}, bf16[1,80,768]{2,1,0:T(8,128)(2,1)}, f32[1,8,128]{2,1,0:T(8,128)}) custom-call(s32[3]{0:T(128)} %pad_add_fusion.3.place_ref, f32[16]{0:T(128)} %gate_ref.11, bf16[1,768,4096]{2,1,0:T(8,128)(2,1)} %weight_ref.7, ...), custom_call_target="tpu_custom_call", output_to_operand_aliasing={{0}: (11, {})} | custom-call | flops 1000000 | bytes 10000 | tf_op jit(solution)/shard_map/pallas_call | solution.py:308
  146.4 1.5 collective-permute-start.16
  147.9 2.9 %collective-permute-start.17 = (f32[8,128]{1,0:T(8,128)S(1)}, f32[8,128]{1,0:T(8,128)S(1)}, u32[]{:S(2)}, u32[]{:S(2)}) collective-permute-start(f32[8,128]{1,0:T(8,128)S(1)} %get-tuple-element.82), channel_id=1, source_target_pairs={{0,10},{1,11},{2,8},{3,9},{4,14},{5,15},{6,12},{7,13},{8,2},{9,3},... | collective-permute-start | bytes 12296 | tf_op jit(solution)/shard_map/ppermute | solution.py:399
  150.8 1.5 collective-permute-start.20
  153.7 3.5 %collective-permute-done.20.refs_7_ = f32[8,128]{1,0:T(8,128)S(1)} collective-permute-done((f32[8,128]{1,0:T(8,128)}, f32[8,128]{1,0:T(8,128)S(1)}, u32[]{:S(2)}, u32[]{:S(2)}) %collective-permute-start.20) | collective-permute-done | bytes 4128 | tf_op jit(solution)/shard_map/ppermute | solution.py:399
  (81 shorter events, 21.3 us)
Async XLA Ops:
  0.6 13.5 %copy-start = (bf16[1,16,80,768]{3,2,1,0:T(8,128)(2,1)S(1)}, bf16[1,16,80,768]{3,2,1,0:T(8,128)(2,1)}, u32[]{:S(2)}) copy-start(bf16[1,16,80,768]{3,2,1,0:T(8,128)(2,1)} %param.13) | copy-start | bytes 5898244
  0.7 40.4 %collective-permute-start.4 = (bf16[1,768,4096]{2,1,0:T(8,128)(2,1)}, bf16[1,768,4096]{2,1,0:T(8,128)(2,1)}, u32[]{:S(2)}, u32[]{:S(2)}) collective-permute-start(bf16[1,768,4096]{2,1,0:T(8,128)(2,1)} %weight_ref.7), channel_id=1, source_target_pairs={{0,1},{1,0},{2,3},{3,2},{4,5},{5,4},{6,7},{7,6},{8,9},{9,8},{10,11... | collective-permute-start | bytes 18874376 | tf_op jit(solution)/shard_map/ppermute | solution.py:399
  1.2 12.9 %collective-permute-start.3 = (bf16[16,80,768]{2,1,0:T(8,128)(2,1)}, bf16[16,80,768]{2,1,0:T(8,128)(2,1)}, u32[]{:S(2)}, u32[]{:S(2)}) collective-permute-start(bf16[16,80,768]{2,1,0:T(8,128)(2,1)} %bitcast.34), channel_id=1, source_target_pairs={{0,1},{1,0},{2,3},{3,2},{4,5},{5,4},{6,7},{7,6},{8,9},{9,8},{10,11... | collective-permute-start | bytes 5898248 | tf_op jit(solution)/shard_map/ppermute | solution.py:399
  4.0 46.6 %copy-start.1 = (bf16[128,4096]{1,0:T(8,128)(2,1)}, bf16[128,4096]{1,0:T(8,128)(2,1)S(1)}, u32[]{:S(2)}) copy-start(bf16[128,4096]{1,0:T(8,128)(2,1)S(1)} %shard_map.128.rows_ref.rest_0_.rest_1_) | copy-start | bytes 3145732
  4.0 27.1 %collective-permute-start = (bf16[128,4096]{1,0:T(8,128)(2,1)S(1)}, bf16[128,4096]{1,0:T(8,128)(2,1)}, u32[]{:S(2)}, u32[]{:S(2)}) collective-permute-start(bf16[128,4096]{1,0:T(8,128)(2,1)S(1)} %shard_map.128.rows_ref.rest_0_.rest_1_), channel_id=1, source_target_pairs={{0,4},{1,5},{2,6},{3,7},{4,0},{5,1},{6,2},{7,3},{8,12},{9,13},{10,... | collective-permute-start | bytes 3145736 | tf_op jit(solution)/shard_map/ppermute | solution.py:399
  7.1 26.1 %collective-permute-start.1 = (bf16[128,4096]{1,0:T(8,128)(2,1)S(1)}, bf16[128,4096]{1,0:T(8,128)(2,1)}, u32[]{:S(2)}, u32[]{:S(2)}) collective-permute-start(bf16[128,4096]{1,0:T(8,128)(2,1)S(1)} %shard_map.128.rows_ref.rest_0_.rest_1_), channel_id=1, source_target_pairs={{0,2},{1,3},{2,0},{3,1},{4,6},{5,7},{6,4},{7,5},{8,10},{9,11},{10,... | collective-permute-start | bytes 3145736 | tf_op jit(solution)/shard_map/ppermute | solution.py:399
  8.6 24.6 %collective-permute-start.2 = (bf16[128,4096]{1,0:T(8,128)(2,1)S(1)}, bf16[128,4096]{1,0:T(8,128)(2,1)}, u32[]{:S(2)}, u32[]{:S(2)}) collective-permute-start(bf16[128,4096]{1,0:T(8,128)(2,1)S(1)} %shard_map.128.rows_ref.rest_0_.rest_1_), channel_id=1, source_target_pairs={{4,8},{5,9},{6,10},{7,11},{8,4},{9,5},{10,6},{11,7},{20,24},{21,25... | collective-permute-start | bytes 3145736 | tf_op jit(solution)/shard_map/ppermute | solution.py:399
  17.3 23.7 %all-to-all-start = ((bf16[16,80,128]{2,1,0:T(8,128)(2,1)}), bf16[16,80,128]{2,1,0:T(8,128)(2,1)S(1)}, u32[]{:S(2)}, u32[]{:S(2)}) async-start(bf16[16,80,128]{2,1,0:T(8,128)(2,1)} %copy-done.5), calls=%async_computation | async-start | bytes 655360 | tf_op jit(solution)/shard_map/all_to_all | solution.py:496
  41.0 31.4 %collective-permute-start.8 = (bf16[128,4096]{1,0:T(8,128)(2,1)}, bf16[128,4096]{1,0:T(8,128)(2,1)}, u32[]{:S(2)}, u32[]{:S(2)}) collective-permute-start(bf16[128,4096]{1,0:T(8,128)(2,1)} %collective-permute-done.rest_2_.rest_3_), channel_id=1, source_target_pairs={{4,8},{5,9},{6,10},{7,11},{8,4},{9,5},{10,6},{11,7},{20,24},{21,25... | collective-permute-start | bytes 3145736 | tf_op jit(solution)/shard_map/ppermute | solution.py:399
  46.0 26.4 %collective-permute-start.7 = (bf16[128,4096]{1,0:T(8,128)(2,1)}, bf16[128,4096]{1,0:T(8,128)(2,1)}, u32[]{:S(2)}, u32[]{:S(2)}) collective-permute-start(bf16[128,4096]{1,0:T(8,128)(2,1)} %get-tuple-element.78), channel_id=1, source_target_pairs={{0,4},{1,5},{2,6},{3,7},{4,0},{5,1},{6,2},{7,3},{8,12},{9,13},{10,... | collective-permute-start | bytes 3145736 | tf_op jit(solution)/shard_map/ppermute | solution.py:399
  49.8 24.0 %collective-permute-start.9 = (bf16[128,4096]{1,0:T(8,128)(2,1)}, bf16[128,4096]{1,0:T(8,128)(2,1)}, u32[]{:S(2)}, u32[]{:S(2)}) collective-permute-start(bf16[128,4096]{1,0:T(8,128)(2,1)} %get-tuple-element.77), channel_id=1, source_target_pairs={{0,2},{1,3},{2,0},{3,1},{4,6},{5,7},{6,4},{7,5},{8,10},{9,11},{10,... | collective-permute-start | bytes 3145736 | tf_op jit(solution)/shard_map/ppermute | solution.py:399
  54.5 24.6 %copy-start.3 = (f32[16,80,128]{2,1,0:T(8,128)}, f32[16,80,128]{2,1,0:T(8,128)S(1)}, u32[]{:S(2)}) copy-start(f32[16,80,128]{2,1,0:T(8,128)S(1)} %shard_map.130) | copy-start | bytes 1966084
  73.8 30.3 %collective-permute-start.12 = (bf16[128,4096]{1,0:T(8,128)(2,1)}, bf16[128,4096]{1,0:T(8,128)(2,1)S(1)}, u32[]{:S(2)}, u32[]{:S(2)}) collective-permute-start(bf16[128,4096]{1,0:T(8,128)(2,1)} %collective-permute-done.8.rest_1_), channel_id=1, source_target_pairs={{4,0},{5,1},{6,2},{7,3},{8,12},{9,13},{10,14},{11,15},{20,16},{21,... | collective-permute-start | bytes 3145736 | tf_op jit(solution)/shard_map/ppermute | solution.py:399
  77.5 26.7 %collective-permute-start.13 = (bf16[128,4096]{1,0:T(8,128)(2,1)}, bf16[128,4096]{1,0:T(8,128)(2,1)S(1)}, u32[]{:S(2)}, u32[]{:S(2)}) collective-permute-start(bf16[128,4096]{1,0:T(8,128)(2,1)} %broadcast_select_fusion), channel_id=1, source_target_pairs={{0,2},{1,3},{2,0},{3,1},{4,6},{5,7},{6,4},{7,5},{8,10},{9,11},{10,... | collective-permute-start | bytes 3145736 | tf_op jit(solution)/shard_map/ppermute | solution.py:399
  79.2 1.7 %collective-permute-start.14 = (f32[8,80,128]{2,1,0:T(8,128)S(1)}, f32[8,80,128]{2,1,0:T(8,128)S(1)}, u32[]{:S(2)}, u32[]{:S(2)}) collective-permute-start(f32[8,80,128]{2,1,0:T(8,128)S(1)} %slice.42), channel_id=1, source_target_pairs={{0,1},{1,0},{2,3},{3,2},{4,5},{5,4},{6,7},{7,6},{8,9},{9,8},{10,11... | collective-permute-start | bytes 983048 | tf_op jit(solution)/shard_map/ppermute | solution.py:399
  82.6 21.5 %all-to-all-start.1 = ((bf16[8,80,128]{2,1,0:T(8,128)(2,1)}), bf16[8,80,128]{2,1,0:T(8,128)(2,1)S(1)}, u32[]{:S(2)}, u32[]{:S(2)}) async-start(bf16[8,80,128]{2,1,0:T(8,128)(2,1)} %add_convert_fusion), calls=%async_computation.1 | async-start | bytes 327680 | tf_op jit(solution)/shard_map/all_to_all | solution.py:511
  87.4 25.2 %copy-start.14 = (f32[3,8,128]{2,1,0:T(8,128)S(1)}, f32[3,8,128]{2,1,0:T(8,128)}, u32[]{:S(2)}) copy-start(f32[3,8,128]{2,1,0:T(8,128)} %get-tuple-element.47) | copy-start | bytes 36868
  98.5 18.4 %copy-start.15 = (f32[2,8,128]{2,1,0:T(8,128)S(1)}, f32[2,8,128]{2,1,0:T(8,128)}, u32[]{:S(2)}) copy-start(f32[2,8,128]{2,1,0:T(8,128)} %get-tuple-element.54) | copy-start | bytes 24580
  98.6 18.4 %collective-permute-start.15 = (bf16[5,80,768]{2,1,0:T(8,128)(2,1)}, bf16[5,80,768]{2,1,0:T(8,128)(2,1)S(1)}, u32[]{:S(2)}, u32[]{:S(2)}) collective-permute-start(bf16[5,80,768]{2,1,0:T(8,128)(2,1)} %get-tuple-element.60), channel_id=1, source_target_pairs={{0,1},{1,0},{2,3},{3,2},{4,5},{5,4},{6,7},{7,6},{8,9},{9,8},{10,11... | collective-permute-start | bytes 1843208 | tf_op jit(solution)/shard_map/ppermute | solution.py:399
  105.0 26.4 %collective-permute-start.18 = (bf16[64,4096]{1,0:T(8,128)(2,1)}, bf16[64,4096]{1,0:T(8,128)(2,1)}, u32[]{:S(2)}, u32[]{:S(2)}) collective-permute-start(bf16[64,4096]{1,0:T(8,128)(2,1)} %slice.45), channel_id=1, source_target_pairs={{0,2},{1,3},{2,0},{3,1},{12,14},{13,15},{14,12},{15,13},{16,18},{1... | collective-permute-start | bytes 1572872 | tf_op jit(solution)/shard_map/ppermute | solution.py:399
  109.1 19.2 %all-to-all-start.2 = ((bf16[8,80,128]{2,1,0:T(8,128)(2,1)}), bf16[8,80,128]{2,1,0:T(8,128)(2,1)S(1)}, u32[]{:S(2)}, u32[]{:S(2)}) async-start(bf16[8,80,128]{2,1,0:T(8,128)(2,1)} %broadcast_in_dim.10), calls=%async_computation.2 | async-start | bytes 327680 | tf_op jit(solution)/shard_map/all_to_all | solution.py:511
  112.6 33.8 %collective-permute-start.5 = (f32[8,128]{1,0:T(8,128)S(1)}, f32[8,128]{1,0:T(8,128)S(1)}, u32[]{:S(2)}, u32[]{:S(2)}) collective-permute-start(f32[8,128]{1,0:T(8,128)S(1)} %get-tuple-element.80), channel_id=1, source_target_pairs={{0,4},{1,5},{2,6},{3,7},{4,0},{5,1},{6,2},{7,3},{8,12},{9,13},{10,... | collective-permute-start | bytes 12296 | tf_op jit(solution)/shard_map/ppermute | solution.py:399
  115.5 20.2 %collective-permute-start.19 = (bf16[64,4096]{1,0:T(8,128)(2,1)}, bf16[64,4096]{1,0:T(8,128)(2,1)}, u32[]{:S(2)}, u32[]{:S(2)}) collective-permute-start(bf16[64,4096]{1,0:T(8,128)(2,1)} %slice.46), channel_id=1, source_target_pairs={{4,0},{5,1},{6,2},{7,3},{8,12},{9,13},{10,14},{11,15},{20,16},{21,... | collective-permute-start | bytes 1572872 | tf_op jit(solution)/shard_map/ppermute | solution.py:399
  128.2 24.0 %collective-permute-start.22 = (bf16[2,80,768]{2,1,0:T(8,128)(2,1)}, bf16[2,80,768]{2,1,0:T(8,128)(2,1)S(1)}, u32[]{:S(2)}, u32[]{:S(2)}) collective-permute-start(bf16[2,80,768]{2,1,0:T(8,128)(2,1)} %get-tuple-element.68), channel_id=1, source_target_pairs={{0,1},{1,0},{2,3},{3,2},{4,5},{5,4},{6,7},{7,6},{8,9},{9,8},{10,11... | collective-permute-start | bytes 737288 | tf_op jit(solution)/shard_map/ppermute | solution.py:399
  128.3 1.7 %collective-permute-start.23 = (bf16[8,80,128]{2,1,0:T(8,128)(2,1)S(1)}, bf16[8,80,128]{2,1,0:T(8,128)(2,1)S(1)}, u32[]{:S(2)}, u32[]{:S(2)}) collective-permute-start(bf16[8,80,128]{2,1,0:T(8,128)(2,1)S(1)} %all-to-all-done.2), channel_id=1, source_target_pairs={{0,1},{1,0},{2,3},{3,2},{4,5},{5,4},{6,7},{7,6},{8,9},{9,8},{10,11... | collective-permute-start | bytes 491528 | tf_op jit(solution)/shard_map/ppermute | solution.py:399
  130.0 17.9 %collective-permute-start.6 = (f32[8,128]{1,0:T(8,128)S(1)}, f32[8,128]{1,0:T(8,128)S(1)}, u32[]{:S(2)}, u32[]{:S(2)}) collective-permute-start(f32[8,128]{1,0:T(8,128)S(1)} %get-tuple-element.79), channel_id=1, source_target_pairs={{0,2},{1,3},{2,0},{3,1},{4,6},{5,7},{6,4},{7,5},{8,10},{9,11},{10,... | collective-permute-start | bytes 12296 | tf_op jit(solution)/shard_map/ppermute | solution.py:399
  131.5 19.3 %collective-permute-start.10 = (f32[8,128]{1,0:T(8,128)S(1)}, f32[8,128]{1,0:T(8,128)S(1)}, u32[]{:S(2)}, u32[]{:S(2)}) collective-permute-start(f32[8,128]{1,0:T(8,128)S(1)} %get-tuple-element.85), channel_id=1, source_target_pairs={{0,8},{1,9},{2,10},{3,11},{4,12},{5,13},{6,14},{7,15},{8,0},{9,1},... | collective-permute-start | bytes 12296 | tf_op jit(solution)/shard_map/ppermute | solution.py:399
  135.7 18.0 %collective-permute-start.11 = (f32[8,128]{1,0:T(8,128)S(1)}, f32[8,128]{1,0:T(8,128)S(1)}, u32[]{:S(2)}, u32[]{:S(2)}) collective-permute-start(f32[8,128]{1,0:T(8,128)S(1)} %get-tuple-element.84), channel_id=1, source_target_pairs={{0,6},{1,7},{2,4},{3,5},{4,2},{5,3},{6,0},{7,1},{8,14},{9,15},{10,... | collective-permute-start | bytes 12296 | tf_op jit(solution)/shard_map/ppermute | solution.py:399
  146.4 7.3 %collective-permute-start.16 = (f32[8,128]{1,0:T(8,128)S(1)}, f32[8,128]{1,0:T(8,128)S(1)}, u32[]{:S(2)}, u32[]{:S(2)}) collective-permute-start(f32[8,128]{1,0:T(8,128)S(1)} %get-tuple-element.83), channel_id=1, source_target_pairs={{0,12},{1,13},{2,14},{3,15},{4,8},{5,9},{6,10},{7,11},{8,4},{9,5},... | collective-permute-start | bytes 12296 | tf_op jit(solution)/shard_map/ppermute | solution.py:399
  147.9 5.9 %collective-permute-start.17 = (f32[8,128]{1,0:T(8,128)S(1)}, f32[8,128]{1,0:T(8,128)S(1)}, u32[]{:S(2)}, u32[]{:S(2)}) collective-permute-start(f32[8,128]{1,0:T(8,128)S(1)} %get-tuple-element.82), channel_id=1, source_target_pairs={{0,10},{1,11},{2,8},{3,9},{4,14},{5,15},{6,12},{7,13},{8,2},{9,3},... | collective-permute-start | bytes 12296 | tf_op jit(solution)/shard_map/ppermute | solution.py:399
  150.8 6.5 %collective-permute-start.20 = (f32[8,128]{1,0:T(8,128)}, f32[8,128]{1,0:T(8,128)S(1)}, u32[]{:S(2)}, u32[]{:S(2)}) collective-permute-start(f32[8,128]{1,0:T(8,128)} %bitcast.55), channel_id=1, source_target_pairs={{0,14},{1,15},{2,12},{3,13},{4,10},{5,11},{6,8},{7,9},{8,6},{9,7},... | collective-permute-start | bytes 12296 | tf_op jit(solution)/shard_map/ppermute | solution.py:399
  152.2 5.0 %collective-permute-start.21 = (bf16[1,80,768]{2,1,0:T(8,128)(2,1)}, bf16[1,80,768]{2,1,0:T(8,128)(2,1)S(1)}, u32[]{:S(2)}, u32[]{:S(2)}) collective-permute-start(bf16[1,80,768]{2,1,0:T(8,128)(2,1)} %get-tuple-element.67), channel_id=1, source_target_pairs={{0,1},{1,0},{2,3},{3,2},{4,5},{5,4},{6,7},{7,6},{8,9},{9,8},{10,11... | collective-permute-start | bytes 368648 | tf_op jit(solution)/shard_map/ppermute | solution.py:399
  (11 other events, 85.2 us)

commit v3 on v2

--- a/solution.py
+++ b/solution.py
@@ -177,7 +177,7 @@
     layout,
     slot,
 ):
-    hidden_out, other_out, dots_ref, rows_ref, held_ref, kept_ref, hidden_ref = rest[-15:-8]
+    hidden_out, other_out, dots_out, mark_ref, rows_ref, held_ref, kept_ref, hidden_ref, dots_ref = rest[-17:-8]
     adapted_ref, chosen_ref, shares_ref, results_ref, load_sem, held_sem, kept_sem, write_sem = rest[-8:]
     tile = held_ref.shape[1]
     tiles = weight_ref.shape[1] // tile
@@ -273,18 +273,24 @@
             shared = dot(chosen, (shares_ref[k, unit, :, 0:1] * grad).astype(BF16), PLAIN)
             hidden_ref[k, unit, :, span] = shared.astype(BF16)
 
+    for unit in range(units):
+        dots_ref[unit] = results_ref[unit].T[:8]
     writes = []
     for unit in range(units):
-        for k, target in enumerate((hidden_out.at[place_ref[2 + unit]], other_out.at[slot + unit])):
-            writes.append(pltpu.make_async_copy(hidden_ref.at[k, unit], target, write_sem.at[len(writes)]))
+        source = place_ref[2 + unit]
+        for value, target in (
+            (dots_ref.at[unit], dots_out.at[source >> 1]),
+            (hidden_ref.at[0, unit], hidden_out.at[source]),
+            (hidden_ref.at[1, unit], other_out.at[slot + unit]),
+        ):
+            writes.append(pltpu.make_async_copy(value, target, write_sem.at[len(writes)]))
             writes[-1].start()
-    for unit in range(units):
-        dots_ref[unit] = results_ref[unit].T[:8]
+    mark_ref[...] = jnp.zeros(mark_ref.shape, F32)
     for copy in writes:
         copy.wait()
 
 
-def expert_call(place, gate, weight, other_weight, stored, other_stored, first, got, buffers, hidden, other, slot):
+def expert_call(place, gate, weight, other_weight, stored, other_stored, first, got, buffers, hidden, other, dots, mark, slot):
     devices, cap, width_hidden = stored.shape
     layout = [(len(as_end), len(as_mid)) for as_end, as_mid in buffers]
     pieces = [piece for pair in buffers for side in pair for piece in side]
@@ -295,8 +301,11 @@
     smem = pl.BlockSpec(memory_space=pltpu.SMEM)
     operands = [place, gate, weight, other_weight, stored, other_stored, first, got, *pieces]
     in_specs = [smem] * 2 + [any_spec] * 4 + whole(2) + [any_spec] * len(pieces)
+    if mark is not None:
+        operands.append(mark)
+        in_specs.append(any_spec)
     aliases, sizes = {}, []
-    for number, value in enumerate((hidden, other)):
+    for number, value in enumerate((hidden, other, dots)):
         if isinstance(value, int):
             sizes.append(value)
         else:
@@ -308,17 +317,19 @@
     return pl.pallas_call(
         functools.partial(expert_kernel, layout=layout, slot=slot),
         in_specs=in_specs,
-        out_specs=[any_spec, any_spec, pl.BlockSpec(memory_space=pltpu.VMEM)],
+        out_specs=[any_spec, any_spec, any_spec, pl.BlockSpec(memory_space=pltpu.VMEM)],
         out_shape=[
             jax.ShapeDtypeStruct((sizes[0], cap, width_hidden), BF16),
             jax.ShapeDtypeStruct((sizes[1], cap, width_hidden), BF16),
-            jax.ShapeDtypeStruct((units, 8, tokens), F32),
+            jax.ShapeDtypeStruct((sizes[2], 8, tokens), F32),
+            jax.ShapeDtypeStruct((8, 128), F32),
         ],
         scratch_shapes=[
             pltpu.VMEM((units * tokens, width), BF16),
             pltpu.VMEM((2 * width_hidden // TILE, TILE, width), BF16),
             pltpu.VMEM((2, units, cap, width_hidden), BF16),
             pltpu.VMEM((2, units, cap, width_hidden), BF16),
+            pltpu.VMEM((units, 8, tokens), F32),
             pltpu.VMEM((units, tokens, width_hidden), F32),
             pltpu.VMEM((2, units, cap, tokens), BF16),
             pltpu.VMEM((2, units, tokens, 128), F32),
@@ -326,7 +337,7 @@
             pltpu.SemaphoreType.DMA((loads,)),
             pltpu.SemaphoreType.DMA((2 * width_hidden // TILE,)),
             pltpu.SemaphoreType.DMA((2 * units,)),
-            pltpu.SemaphoreType.DMA((2 * units,)),
+            pltpu.SemaphoreType.DMA((3 * units,)),
         ],
         input_output_aliases=aliases,
         compiler_params=params(BIG_LIMIT),
@@ -361,19 +372,16 @@
     )(own1, *moved, hidden)
 
 
-def finish_kernel(own_ref, *refs, masks):
-    count = len(masks)
-    dots, routes_ref, moved_ref = refs[:count], refs[count], refs[count + 1]
-    routing_ref, hidden_ref, sem = refs[count + 3 :]
+def finish_kernel(own_ref, dots_ref, routes_ref, moved_ref, _, __, routing_ref, hidden_ref, sem, *, mask):
     own = own_ref[0]
-    copy = pltpu.make_async_copy(moved_ref.at[0], hidden_ref.at[own ^ 1 ^ (masks[-1] << 1)], sem)
+    copy = pltpu.make_async_copy(moved_ref.at[0], hidden_ref.at[own ^ 1 ^ (mask << 1)], sem)
     copy.start()
     routes = routes_ref[...]
     total = jnp.zeros(routes.shape, F32)
-    for k, mask in enumerate(masks):
+    for chip in range(dots_ref.shape[0]):
         for row in range(2):
-            expert = own ^ (mask << 1) ^ row
-            total = total + jnp.where(routes == expert, dots[k][row : row + 1, :], F32(0.0))
+            expert = 2 * chip + ((own & 1) ^ row)
+            total = total + jnp.where(routes == expert, dots_ref[chip, row : row + 1, :], F32(0.0))
     routing_ref[...] = total
     copy.wait()
 
@@ -450,14 +458,13 @@
     masks = (0, 2, 1, 4, 3, 6, 5, 7)
     final = len(masks) - 1
     half = tokens // 2
-    dots, hidden_part, other_part = [], devices, 5
+    hidden_part, other_part, dots, mark, begin = devices, 5, devices // 2, None, 0
 
     def experts(count, buffers, *earlier):
-        nonlocal hidden_part, other_part
-        begin = len(dots)
+        nonlocal hidden_part, other_part, dots, mark, begin
         turns = masks[begin : begin + count]
         place = jnp.stack([own, is_end] + [own ^ (mask << 1) for mask in turns])
-        hidden_part, other_part, found = expert_call(
+        hidden_part, other_part, dots, mark = expert_call(
             then(place, *earlier),
             expert_adapter_gate,
             frozen_down_weight,
@@ -469,11 +476,12 @@
             buffers,
             hidden_part,
             other_part,
+            dots,
+            mark,
             begin if begin < 5 else 0,
         )
-        for k, mask in enumerate(turns):
-            dots.append(send(found[k], xor_pairs(mask << 1)) if mask else found[k])
-        return found
+        begin += count
+        return mark
 
     near, side, mid = send(rows, to["near"]), send(rows, to["side"]), send(rows, to["mid"])
     packed = pl.pallas_call(
@@ -511,19 +519,20 @@
     among_lane = lambda value: lax.all_to_all(
         value, "ex", split_axis=0, concat_axis=0, axis_index_groups=lanes, tiled=True
     )
-    found = experts(3, [([rows], [rows]), ([near], [near]), ([side], [side])], partial, near, side, mid)
-    near2, mid2, side2, partial, _ = lax.optimization_barrier((near2, mid2, side2, partial, found))
     pair = (partial[: devices // 2] + send(partial[devices // 2 :], xor_pairs(1))).astype(BF16)
     parts = among_lane(pair)
+    found = experts(1, [([rows], [rows])], pair, near, side, mid)
+    near2, mid2, side2, parts, _ = lax.optimization_barrier((near2, mid2, side2, parts, found))
     near3 = send(mid2, to["out"])
     side3 = send(pick(near2, mid2), to["side"])
-    found = experts(2, [([near2], [mid2]), ([side2], [near2])], near2, side2, mid2)
-    summed = jnp.sum(then(parts, found).astype(F32), axis=0).astype(BF16)
-    near3, side3, _, summed = lax.optimization_barrier((near3, side3, found, summed))
+    summed = jnp.sum(parts.astype(F32), axis=0).astype(BF16)
     summed = among_lane(jnp.broadcast_to(summed[None], (devices // 2, 80, 128)))
+    found = experts(4, [([near], [near]), ([side], [side]), ([near2], [mid2]), ([side2], [near2])], near2, side2, mid2)
+    near3, side3, summed, _ = lax.optimization_barrier((near3, side3, summed, found))
     last = [send(near3[:half], to["end_side"]), send(side3[half:], to["out"])]
-    moved, other_part = [send(then(other_part, found), xor_pairs(1))], 2
+    moved, other_part = [send(then(other_part, near3, side3), xor_pairs(1))], 2
     found = experts(2, [([near3], [mid]), ([side3], [side3])], near3, side3, moved[0])
+    summed = then(summed, found)
     summed = jnp.concatenate([summed, send(summed, xor_pairs(1))], axis=0)
     moved.append(send(other_part, xor_pairs(1)))
     other_part = 1
@@ -544,19 +553,20 @@
     )(then(own1, found), summed)
     hidden_part = place_call(own1, moved, hidden_part, (masks[:5], masks[5:final]))
     moved = last_moved
+    returned = among_lane(dots)
     routing_t, hidden_gradient = pl.pallas_call(
-        functools.partial(finish_kernel, masks=masks),
-        in_specs=[smem] + whole(len(masks) + 2) + [any_spec],
+        functools.partial(finish_kernel, mask=masks[-1]),
+        in_specs=[smem] + whole(3) + [any_spec, any_spec],
         out_specs=[vmem, any_spec],
         out_shape=[
             jax.ShapeDtypeStruct(routes_t.shape, F32),
             jax.ShapeDtypeStruct((devices, cap, hidden), BF16),
         ],
-        input_output_aliases={len(masks) + 3: 1},
+        input_output_aliases={4: 1},
         scratch_shapes=[pltpu.SemaphoreType.DMA],
         compiler_params=params(),
         cost_estimate=SMALL,
-    )(own1, *dots, routes_t, moved, hidden_part)
+    )(own1, returned, routes_t, moved, hidden_part, mark)
     return (
         hidden_gradient[None],
         routing_t.T,

time: 160 us -> 151 us (0.944)
  starting transfers between devices: 49.5 us -> 40 us
  Pallas kernels: 55.5 us -> 57.4 us
    ppermute x24 -> x17, starting transfers between devices: 34.5 us -> 18.1 us  [send(): return lax.ppermute(value, 'ex', pairs)]
    all_to_all x2 -> x3, waiting for transfers between devices: 4.21 us -> 14.7 us  [small_body(): lax.all_to_all(value, 'ex', split_axis=0, concat_axis=0, axis_index_group...]
    all_to_all x2 -> x3, starting transfers between devices: 7.67 us -> 14.6 us  [small_body(): lax.all_to_all(value, 'ex', split_axis=0, concat_axis=0, axis_index_group...]
    all_to_all x1, waiting for transfers between devices: 7.89 us -> 2.32 us  [small_body(): got = lax.all_to_all(packed, 'ex', split_axis=0, concat_axis=0, tiled=True)]
    ppermute x24 -> x17, waiting for transfers between devices: 23.3 us -> 19.3 us  [send(): return lax.ppermute(value, 'ex', pairs)]
    pallas_call x4, Pallas kernels: 46.2 us -> 48.2 us  [expert_call(): pl.pallas_call(functools.partial(expert_kernel, layout=layout, slot=slot)...]
  transfers between devices with their start and end apart: 27 -> 21, of which waited for: 10 -> 9; matrix products, arithmetic and copies ran while one was open for 9% -> 6% of each run, Pallas kernels for 34% -> 37%
where the time goes in v3:
time: 151 us; the launch traced here: 150 us
  Pallas kernels  57.4 us (38%)
  starting transfers between devices  40 us (26%)
  waiting for transfers between devices  36.3 us (24%)
  other arithmetic  8.29 us (5%)
  local copies, waits for them, and re-layouts  7.27 us (5%)
    pallas_call x4, Pallas kernels, expert_call(): pl.pallas_call(functools.partial(expert_kernel, layout=layout, slot=slot)...  48.2 us
    ppermute x17, waiting for transfers between devices, send(): return lax.ppermute(value, 'ex', pairs)  19.3 us
    ppermute x17, starting transfers between devices, send(): return lax.ppermute(value, 'ex', pairs)  18.1 us
    all_to_all x3, waiting for transfers between devices, small_body(): lax.all_to_all(value, 'ex', split_axis=0, concat_axis=0, axis_index_group...  14.7 us
    all_to_all x3, starting transfers between devices, small_body(): lax.all_to_all(value, 'ex', split_axis=0, concat_axis=0, axis_index_group...  14.6 us
    all_to_all x1, starting transfers between devices, small_body(): got = lax.all_to_all(packed, 'ex', split_axis=0, concat_axis=0, tiled=True)  7.28 us
    select_n x2, other arithmetic, small_body(): pick = lambda as_end, as_mid: jnp.where(is_end == 1, as_end, as_mid)  5.68 us
    pallas_call x1, Pallas kernels, small_body(): pl.pallas_call(low_rank_kernel, in_specs=[smem] + whole(3) + [smem] + who...  3.94 us
  transfers between devices with their start and end apart: 21, of which 9 were waited for; matrix products, arithmetic and copies ran while one was open for 6% of the time, Pallas kernels for 37%

profile of v3, /device:TPU:0, one launch (start us, length us, event | category | flops | bytes accessed | tf_op | source)
XLA Modules:
  0.0 150.2 jit_solution(7160707765527095513)
XLA Ops:
  1.3 1.2 copy-done.5
  4.0 1.7 %collective-permute-start.2 = (bf16[128,4096]{1,0:T(8,128)(2,1)S(1)}, bf16[128,4096]{1,0:T(8,128)(2,1)}, u32[]{:S(2)}, u32[]{:S(2)}) collective-permute-start(bf16[128,4096]{1,0:T(8,128)(2,1)S(1)} %shard_map.128.rows_ref.rest_0_.rest_1_), channel_id=1, source_target_pairs={{4,8},{5,9},{6,10},{7,11},{8,4},{9,5},{10,6},{11,7},{20,24},{21,25... | collective-permute-start | bytes 3145736 | tf_op jit(solution)/shard_map/ppermute | solution.py:407
  5.6 2.9 %collective-permute-start.1 = (bf16[128,4096]{1,0:T(8,128)(2,1)S(1)}, bf16[128,4096]{1,0:T(8,128)(2,1)}, u32[]{:S(2)}, u32[]{:S(2)}) collective-permute-start(bf16[128,4096]{1,0:T(8,128)(2,1)S(1)} %shard_map.128.rows_ref.rest_0_.rest_1_), channel_id=1, source_target_pairs={{0,2},{1,3},{2,0},{3,1},{4,6},{5,7},{6,4},{7,5},{8,10},{9,11},{10,... | collective-permute-start | bytes 3145736 | tf_op jit(solution)/shard_map/ppermute | solution.py:407
  8.6 3.5 %collective-permute-start = (bf16[128,4096]{1,0:T(8,128)(2,1)S(1)}, bf16[128,4096]{1,0:T(8,128)(2,1)}, u32[]{:S(2)}, u32[]{:S(2)}) collective-permute-start(bf16[128,4096]{1,0:T(8,128)(2,1)S(1)} %shard_map.128.rows_ref.rest_0_.rest_1_), channel_id=1, source_target_pairs={{0,4},{1,5},{2,6},{3,7},{4,0},{5,1},{6,2},{7,3},{8,12},{9,13},{10,... | collective-permute-start | bytes 3145736 | tf_op jit(solution)/shard_map/ppermute | solution.py:407
  12.1 2.1 %collective-permute-done.3.other_stored_ref = bf16[16,80,768]{2,1,0:T(8,128)(2,1)} collective-permute-done((bf16[16,80,768]{2,1,0:T(8,128)(2,1)}, bf16[16,80,768]{2,1,0:T(8,128)(2,1)}, u32[]{:S(2)}, u32[]{:S(2)}) %collective-permute-start.3) | collective-permute-done | bytes 1966112 | tf_op jit(solution)/shard_map/ppermute | solution.py:407
  15.1 1.4 shard_map.129
  17.3 7.3 %all-to-all-start = ((bf16[16,80,128]{2,1,0:T(8,128)(2,1)}), bf16[16,80,128]{2,1,0:T(8,128)(2,1)S(1)}, u32[]{:S(2)}, u32[]{:S(2)}) async-start(bf16[16,80,128]{2,1,0:T(8,128)(2,1)} %copy-done.4), calls=%async_computation | async-start | bytes 655360 | tf_op jit(solution)/shard_map/all_to_all | solution.py:504
  24.6 7.9 %collective-permute-done.1.rest_2_.rest_3_ = bf16[128,4096]{1,0:T(8,128)(2,1)} collective-permute-done((bf16[128,4096]{1,0:T(8,128)(2,1)S(1)}, bf16[128,4096]{1,0:T(8,128)(2,1)}, u32[]{:S(2)}, u32[]{:S(2)}) %collective-permute-start.1) | collective-permute-done | bytes 1048608 | tf_op jit(solution)/shard_map/ppermute | solution.py:407
  32.5 6.4 %collective-permute-done.rest_0_.rest_1_ = bf16[128,4096]{1,0:T(8,128)(2,1)} collective-permute-done((bf16[128,4096]{1,0:T(8,128)(2,1)S(1)}, bf16[128,4096]{1,0:T(8,128)(2,1)}, u32[]{:S(2)}, u32[]{:S(2)}) %collective-permute-start) | collective-permute-done | bytes 1048608 | tf_op jit(solution)/shard_map/ppermute | solution.py:407
  38.9 2.3 %all-to-all-done.got_ref = bf16[16,80,128]{2,1,0:T(8,128)(2,1)S(1)} async-done(((bf16[16,80,128]{2,1,0:T(8,128)(2,1)}), bf16[16,80,128]{2,1,0:T(8,128)(2,1)S(1)}, u32[]{:S(2)}, u32[]{:S(2)}) %all-to-all-start) | async-done | bytes 327712 | tf_op jit(solution)/shard_map/all_to_all | solution.py:504
  41.2 1.6 %collective-permute-start.6 = (bf16[128,4096]{1,0:T(8,128)(2,1)}, bf16[128,4096]{1,0:T(8,128)(2,1)}, u32[]{:S(2)}, u32[]{:S(2)}) collective-permute-start(bf16[128,4096]{1,0:T(8,128)(2,1)} %collective-permute-done.rest_0_.rest_1_), channel_id=1, source_target_pairs={{4,8},{5,9},{6,10},{7,11},{8,4},{9,5},{10,6},{11,7},{20,24},{21,25... | collective-permute-start | bytes 3145736 | tf_op jit(solution)/shard_map/ppermute | solution.py:407
  42.8 3.4 %broadcast_select_fusion.1 = (bf16[128,4096]{1,0:T(8,128)(2,1)}, bf16[128,4096]{1,0:T(8,128)(2,1)}) fusion(bf16[128,4096]{1,0:T(8,128)(2,1)} %collective-permute-done.rest_0_.rest_1_, bf16[128,4096]{1,0:T(8,128)(2,1)} %collective-permute-done.2.rest_1_, pred[]{:T(512)S(6)} %eq.13, bf16[128,4096]{1,0:T(8,128)(2,1)} %collective-permute-done.1.rest_2_.rest_3_), kind=kLoop, calls=%fused_computation.1 | loop fusion | flops 1048576 | bytes 5242881 | tf_op jit(solution)/shard_map/jit(_where)/select_n | solution.py:446
  46.2 2.0 %collective-permute-start.5 = (bf16[128,4096]{1,0:T(8,128)(2,1)}, bf16[128,4096]{1,0:T(8,128)(2,1)}, u32[]{:S(2)}, u32[]{:S(2)}) collective-permute-start(bf16[128,4096]{1,0:T(8,128)(2,1)} %get-tuple-element.86), channel_id=1, source_target_pairs={{0,4},{1,5},{2,6},{3,7},{4,0},{5,1},{6,2},{7,3},{8,12},{9,13},{10,... | collective-permute-start | bytes 3145736 | tf_op jit(solution)/shard_map/ppermute | solution.py:407
  48.2 3.9 %shard_map.130 = f32[16,80,128]{2,1,0:T(8,128)S(1)} custom-call(s32[1]{0:T(128)} %bitcast.own_ref, bf16[16,80,128]{2,1,0:T(8,128)(2,1)S(1)} %all-to-all-done.got_ref, bf16[16,80,768]{2,1,0:T(8,128)(2,1)S(1)} %bitcast.25, bf16[32,768]{1,0:T(8,128)(2,1)S(1)} %bitcast.31, f32[16]{0:T(128)S(1)} %copy-done.8, s32[8,128]{1,0:T(8,128)S(1)} %bitcast.33, ...), custom_call_target="tpu_custom_call" | custom-call | flops 1000000 | bytes 10000 | tf_op jit(solution)/shard_map/pallas_call | solution.py:509
  52.3 1.6 %collective-permute-done.8 = f32[8,80,128]{2,1,0:T(8,128)S(1)} collective-permute-done((f32[8,80,128]{2,1,0:T(8,128)S(1)}, f32[8,80,128]{2,1,0:T(8,128)S(1)}, u32[]{:S(2)}, u32[]{:S(2)}) %collective-permute-start.8) | collective-permute-done | bytes 327712 | tf_op jit(solution)/shard_map/ppermute | solution.py:407
  54.6 4.1 %all-to-all-start.1 = ((bf16[8,80,128]{2,1,0:T(8,128)(2,1)}), bf16[8,80,128]{2,1,0:T(8,128)(2,1)S(1)}, u32[]{:S(2)}, u32[]{:S(2)}) async-start(bf16[8,80,128]{2,1,0:T(8,128)(2,1)} %fusion), calls=%async_computation.1 | async-start | bytes 327680 | tf_op jit(solution)/shard_map/all_to_all | solution.py:519
  59.3 9.8 %shard_map.131 = (bf16[16,80,768]{2,1,0:T(8,128)(2,1)}, bf16[5,80,768]{2,1,0:T(8,128)(2,1)}, f32[8,8,128]{2,1,0:T(8,128)}, f32[8,128]{1,0:T(8,128)}) custom-call(s32[3]{0:T(128)} %pad_add_fusion.2.place_ref, f32[16]{0:T(128)} %gate_ref.11, bf16[1,768,4096]{2,1,0:T(8,128)(2,1)} %weight_ref.7, bf16[1,768,4096]{2,1,0:T(8,128)(2,1)} %collective-permute-done.4.other_weight_ref, ...), custom_call_target="tpu_custom_call" | custom-call | flops 1000000 | bytes 10000 | tf_op jit(solution)/shard_map/pallas_call | solution.py:317
  69.1 7.0 %all-to-all-done.1 = bf16[8,80,128]{2,1,0:T(8,128)(2,1)S(1)} async-done(((bf16[8,80,128]{2,1,0:T(8,128)(2,1)}), bf16[8,80,128]{2,1,0:T(8,128)(2,1)S(1)}, u32[]{:S(2)}, u32[]{:S(2)}) %all-to-all-start.1) | async-done | bytes 163872 | tf_op jit(solution)/shard_map/all_to_all | solution.py:519
  76.1 2.3 %broadcast_select_fusion = bf16[128,4096]{1,0:T(8,128)(2,1)} fusion(bf16[128,4096]{1,0:T(8,128)(2,1)} %collective-permute-done.5.rest_4_.rest_7_, bf16[128,4096]{1,0:T(8,128)(2,1)} %collective-permute-done.6.rest_5_, pred[]{:T(512)S(6)} %eq.13), kind=kLoop, calls=%fused_computation | loop fusion | flops 524288 | bytes 3145729 | tf_op jit(solution)/shard_map/jit(_where)/select_n | solution.py:446
  78.5 1.3 collective-permute-start.9
  80.5 5.4 %all-to-all-start.2 = ((bf16[8,80,128]{2,1,0:T(8,128)(2,1)}), bf16[8,80,128]{2,1,0:T(8,128)(2,1)S(1)}, u32[]{:S(2)}, u32[]{:S(2)}) async-start(bf16[8,80,128]{2,1,0:T(8,128)(2,1)} %broadcast_in_dim.4), calls=%async_computation.2 | async-start | bytes 327680 | tf_op jit(solution)/shard_map/all_to_all | solution.py:519
  86.6 17.1 %shard_map.132 = (bf16[16,80,768]{2,1,0:T(8,128)(2,1)}, bf16[5,80,768]{2,1,0:T(8,128)(2,1)}, f32[8,8,128]{2,1,0:T(8,128)}, f32[8,128]{1,0:T(8,128)}) custom-call(s32[6]{0:T(128)} %stack.52.place_ref, f32[16]{0:T(128)} %gate_ref.11, bf16[1,768,4096]{2,1,0:T(8,128)(2,1)} %weight_ref.7, ...), custom_call_target="tpu_custom_call", output_to_operand_aliasing={{0}: (17, {}), {1}: (18, {}), {2}: (19, {})} | custom-call | flops 1000000 | bytes 10000 | tf_op jit(solution)/shard_map/pallas_call | solution.py:317
  103.6 4.0 %all-to-all-done.2 = bf16[8,80,128]{2,1,0:T(8,128)(2,1)S(1)} async-done(((bf16[8,80,128]{2,1,0:T(8,128)(2,1)}), bf16[8,80,128]{2,1,0:T(8,128)(2,1)S(1)}, u32[]{:S(2)}, u32[]{:S(2)}) %all-to-all-start.2) | async-done | bytes 163872 | tf_op jit(solution)/shard_map/all_to_all | solution.py:519
  107.7 1.0 slice.17
  109.5 1.3 collective-permute-start.12
  110.8 2.3 %collective-permute-start.11 = (bf16[64,4096]{1,0:T(8,128)(2,1)}, bf16[64,4096]{1,0:T(8,128)(2,1)}, u32[]{:S(2)}, u32[]{:S(2)}) collective-permute-start(bf16[64,4096]{1,0:T(8,128)(2,1)} %slice.17), channel_id=1, source_target_pairs={{0,2},{1,3},{2,0},{3,1},{12,14},{13,15},{14,12},{15,13},{16,18},{1... | collective-permute-start | bytes 1572872 | tf_op jit(solution)/shard_map/ppermute | solution.py:407
  113.8 11.4 %shard_map.133 = (bf16[16,80,768]{2,1,0:T(8,128)(2,1)}, bf16[2,80,768]{2,1,0:T(8,128)(2,1)}, f32[8,8,128]{2,1,0:T(8,128)}, f32[8,128]{1,0:T(8,128)}) custom-call(s32[4]{0:T(128)} %pad_add_fusion.3.place_ref, f32[16]{0:T(128)} %gate_ref.11, bf16[1,768,4096]{2,1,0:T(8,128)(2,1)} %weight_ref.7, ...), custom_call_target="tpu_custom_call", output_to_operand_aliasing={{0}: (13, {}), {2}: (14, {})} | custom-call | flops 1000000 | bytes 10000 | tf_op jit(solution)/shard_map/pallas_call | solution.py:317
  125.9 1.3 collective-permute-done.11.rest_0_
  127.2 9.9 %shard_map.134 = (bf16[16,80,768]{2,1,0:T(8,128)(2,1)}, bf16[1,80,768]{2,1,0:T(8,128)(2,1)}, f32[8,8,128]{2,1,0:T(8,128)}, f32[8,128]{1,0:T(8,128)}) custom-call(s32[3]{0:T(128)} %pad_add_fusion.place_ref, f32[16]{0:T(128)} %gate_ref.11, bf16[1,768,4096]{2,1,0:T(8,128)(2,1)} %weight_ref.7, ...), custom_call_target="tpu_custom_call", output_to_operand_aliasing={{0}: (12, {}), {2}: (13, {})} | custom-call | flops 1000000 | bytes 10000 | tf_op jit(solution)/shard_map/pallas_call | solution.py:317
  137.1 5.2 %all-to-all-start.3 = ((f32[8,8,128]{2,1,0:T(8,128)}), f32[8,8,128]{2,1,0:T(8,128)S(1)}, u32[]{:S(2)}, u32[]{:S(2)}) async-start(f32[8,8,128]{2,1,0:T(8,128)} %get-tuple-element.72), calls=%async_computation.3 | async-start | bytes 65536 | tf_op jit(solution)/shard_map/all_to_all | solution.py:519
  145.2 3.8 %all-to-all-done.3.dots_ref = f32[8,8,128]{2,1,0:T(8,128)S(1)} async-done(((f32[8,8,128]{2,1,0:T(8,128)}), f32[8,8,128]{2,1,0:T(8,128)S(1)}, u32[]{:S(2)}, u32[]{:S(2)}) %all-to-all-start.3) | async-done | bytes 32800 | tf_op jit(solution)/shard_map/all_to_all | solution.py:519
  148.9 1.3 shard_map.136
  (66 shorter events, 11.9 us)
Async XLA Ops:
  0.6 13.5 %copy-start = (bf16[1,16,80,768]{3,2,1,0:T(8,128)(2,1)S(1)}, bf16[1,16,80,768]{3,2,1,0:T(8,128)(2,1)}, u32[]{:S(2)}) copy-start(bf16[1,16,80,768]{3,2,1,0:T(8,128)(2,1)} %param.13) | copy-start | bytes 5898244
  0.6 13.5 %copy-start.3 = (bf16[768,32]{0,1:T(8,128)(2,1)S(1)}, bf16[768,32]{0,1:T(8,128)(2,1)}, u32[]{:S(2)}) copy-start(bf16[768,32]{0,1:T(8,128)(2,1)} %param.15) | copy-start | bytes 147460
  0.7 40.5 %collective-permute-start.4 = (bf16[1,768,4096]{2,1,0:T(8,128)(2,1)}, bf16[1,768,4096]{2,1,0:T(8,128)(2,1)}, u32[]{:S(2)}, u32[]{:S(2)}) collective-permute-start(bf16[1,768,4096]{2,1,0:T(8,128)(2,1)} %weight_ref.7), channel_id=1, source_target_pairs={{0,1},{1,0},{2,3},{3,2},{4,5},{5,4},{6,7},{7,6},{8,9},{9,8},{10,11... | collective-permute-start | bytes 18874376 | tf_op jit(solution)/shard_map/ppermute | solution.py:407
  1.2 12.9 %collective-permute-start.3 = (bf16[16,80,768]{2,1,0:T(8,128)(2,1)}, bf16[16,80,768]{2,1,0:T(8,128)(2,1)}, u32[]{:S(2)}, u32[]{:S(2)}) collective-permute-start(bf16[16,80,768]{2,1,0:T(8,128)(2,1)} %bitcast.19), channel_id=1, source_target_pairs={{0,1},{1,0},{2,3},{3,2},{4,5},{5,4},{6,7},{7,6},{8,9},{9,8},{10,11... | collective-permute-start | bytes 5898248 | tf_op jit(solution)/shard_map/ppermute | solution.py:407
  3.2 10.9 %copy-start.7 = (s32[128,8]{0,1:T(8,128)S(1)}, s32[128,8]{0,1:T(8,128)}, u32[]{:S(2)}) copy-start(s32[128,8]{0,1:T(8,128)} %param.11) | copy-start | bytes 12292
  3.2 10.9 %copy-start.8 = (f32[16]{0:T(128)S(1)}, f32[16]{0:T(128)}, u32[]{:S(2)}) copy-start(f32[16]{0:T(128)} %gate_ref.11) | copy-start | bytes 196
  3.2 10.9 %copy-start.10 = (bf16[128,8]{0,1:T(8,128)(2,1)S(1)}, bf16[128,8]{0,1:T(8,128)(2,1)}, u32[]{:S(2)}) copy-start(bf16[128,8]{0,1:T(8,128)(2,1)} %param.12) | copy-start | bytes 6148
  4.0 44.2 %copy-start.1 = (bf16[128,4096]{1,0:T(8,128)(2,1)}, bf16[128,4096]{1,0:T(8,128)(2,1)S(1)}, u32[]{:S(2)}) copy-start(bf16[128,4096]{1,0:T(8,128)(2,1)S(1)} %shard_map.128.rows_ref.rest_0_.rest_1_) | copy-start | bytes 3145732
  4.0 20.6 %collective-permute-start.2 = (bf16[128,4096]{1,0:T(8,128)(2,1)S(1)}, bf16[128,4096]{1,0:T(8,128)(2,1)}, u32[]{:S(2)}, u32[]{:S(2)}) collective-permute-start(bf16[128,4096]{1,0:T(8,128)(2,1)S(1)} %shard_map.128.rows_ref.rest_0_.rest_1_), channel_id=1, source_target_pairs={{4,8},{5,9},{6,10},{7,11},{8,4},{9,5},{10,6},{11,7},{20,24},{21,25... | collective-permute-start | bytes 3145736 | tf_op jit(solution)/shard_map/ppermute | solution.py:407
  5.6 26.9 %collective-permute-start.1 = (bf16[128,4096]{1,0:T(8,128)(2,1)S(1)}, bf16[128,4096]{1,0:T(8,128)(2,1)}, u32[]{:S(2)}, u32[]{:S(2)}) collective-permute-start(bf16[128,4096]{1,0:T(8,128)(2,1)S(1)} %shard_map.128.rows_ref.rest_0_.rest_1_), channel_id=1, source_target_pairs={{0,2},{1,3},{2,0},{3,1},{4,6},{5,7},{6,4},{7,5},{8,10},{9,11},{10,... | collective-permute-start | bytes 3145736 | tf_op jit(solution)/shard_map/ppermute | solution.py:407
  8.6 30.3 %collective-permute-start = (bf16[128,4096]{1,0:T(8,128)(2,1)S(1)}, bf16[128,4096]{1,0:T(8,128)(2,1)}, u32[]{:S(2)}, u32[]{:S(2)}) collective-permute-start(bf16[128,4096]{1,0:T(8,128)(2,1)S(1)} %shard_map.128.rows_ref.rest_0_.rest_1_), channel_id=1, source_target_pairs={{0,4},{1,5},{2,6},{3,7},{4,0},{5,1},{6,2},{7,3},{8,12},{9,13},{10,... | collective-permute-start | bytes 3145736 | tf_op jit(solution)/shard_map/ppermute | solution.py:407
  17.3 23.9 %all-to-all-start = ((bf16[16,80,128]{2,1,0:T(8,128)(2,1)}), bf16[16,80,128]{2,1,0:T(8,128)(2,1)S(1)}, u32[]{:S(2)}, u32[]{:S(2)}) async-start(bf16[16,80,128]{2,1,0:T(8,128)(2,1)} %copy-done.4), calls=%async_computation | async-start | bytes 655360 | tf_op jit(solution)/shard_map/all_to_all | solution.py:504
  41.2 7.0 %copy-start.2 = (bf16[16,80,128]{2,1,0:T(8,128)(2,1)}, bf16[16,80,128]{2,1,0:T(8,128)(2,1)S(1)}, u32[]{:S(2)}) copy-start(bf16[16,80,128]{2,1,0:T(8,128)(2,1)S(1)} %all-to-all-done.got_ref) | copy-start | bytes 983044
  41.2 34.9 %collective-permute-start.6 = (bf16[128,4096]{1,0:T(8,128)(2,1)}, bf16[128,4096]{1,0:T(8,128)(2,1)}, u32[]{:S(2)}, u32[]{:S(2)}) collective-permute-start(bf16[128,4096]{1,0:T(8,128)(2,1)} %collective-permute-done.rest_0_.rest_1_), channel_id=1, source_target_pairs={{4,8},{5,9},{6,10},{7,11},{8,4},{9,5},{10,6},{11,7},{20,24},{21,25... | collective-permute-start | bytes 3145736 | tf_op jit(solution)/shard_map/ppermute | solution.py:407
  46.2 29.9 %collective-permute-start.7 = (bf16[128,4096]{1,0:T(8,128)(2,1)}, bf16[128,4096]{1,0:T(8,128)(2,1)}, u32[]{:S(2)}, u32[]{:S(2)}) collective-permute-start(bf16[128,4096]{1,0:T(8,128)(2,1)} %get-tuple-element.85), channel_id=1, source_target_pairs={{0,2},{1,3},{2,0},{3,1},{4,6},{5,7},{6,4},{7,5},{8,10},{9,11},{10,... | collective-permute-start | bytes 3145736 | tf_op jit(solution)/shard_map/ppermute | solution.py:407
  46.2 29.9 %collective-permute-start.5 = (bf16[128,4096]{1,0:T(8,128)(2,1)}, bf16[128,4096]{1,0:T(8,128)(2,1)}, u32[]{:S(2)}, u32[]{:S(2)}) collective-permute-start(bf16[128,4096]{1,0:T(8,128)(2,1)} %get-tuple-element.86), channel_id=1, source_target_pairs={{0,4},{1,5},{2,6},{3,7},{4,0},{5,1},{6,2},{7,3},{8,12},{9,13},{10,... | collective-permute-start | bytes 3145736 | tf_op jit(solution)/shard_map/ppermute | solution.py:407
  52.2 1.7 %collective-permute-start.8 = (f32[8,80,128]{2,1,0:T(8,128)S(1)}, f32[8,80,128]{2,1,0:T(8,128)S(1)}, u32[]{:S(2)}, u32[]{:S(2)}) collective-permute-start(f32[8,80,128]{2,1,0:T(8,128)S(1)} %slice.21), channel_id=1, source_target_pairs={{0,1},{1,0},{2,3},{3,2},{4,5},{5,4},{6,7},{7,6},{8,9},{9,8},{10,11... | collective-permute-start | bytes 983048 | tf_op jit(solution)/shard_map/ppermute | solution.py:407
  54.6 21.5 %all-to-all-start.1 = ((bf16[8,80,128]{2,1,0:T(8,128)(2,1)}), bf16[8,80,128]{2,1,0:T(8,128)(2,1)S(1)}, u32[]{:S(2)}, u32[]{:S(2)}) async-start(bf16[8,80,128]{2,1,0:T(8,128)(2,1)} %fusion), calls=%async_computation.1 | async-start | bytes 327680 | tf_op jit(solution)/shard_map/all_to_all | solution.py:519
  78.4 29.2 %collective-permute-start.10 = (bf16[128,4096]{1,0:T(8,128)(2,1)}, bf16[128,4096]{1,0:T(8,128)(2,1)S(1)}, u32[]{:S(2)}, u32[]{:S(2)}) collective-permute-start(bf16[128,4096]{1,0:T(8,128)(2,1)} %broadcast_select_fusion), channel_id=1, source_target_pairs={{0,2},{1,3},{2,0},{3,1},{4,6},{5,7},{6,4},{7,5},{8,10},{9,11},{10,... | collective-permute-start | bytes 3145736 | tf_op jit(solution)/shard_map/ppermute | solution.py:407
  78.5 29.1 %collective-permute-start.9 = (bf16[128,4096]{1,0:T(8,128)(2,1)}, bf16[128,4096]{1,0:T(8,128)(2,1)S(1)}, u32[]{:S(2)}, u32[]{:S(2)}) collective-permute-start(bf16[128,4096]{1,0:T(8,128)(2,1)} %collective-permute-done.6.rest_5_), channel_id=1, source_target_pairs={{4,0},{5,1},{6,2},{7,3},{8,12},{9,13},{10,14},{11,15},{20,16},{21,... | collective-permute-start | bytes 3145736 | tf_op jit(solution)/shard_map/ppermute | solution.py:407
  80.5 27.1 %all-to-all-start.2 = ((bf16[8,80,128]{2,1,0:T(8,128)(2,1)}), bf16[8,80,128]{2,1,0:T(8,128)(2,1)S(1)}, u32[]{:S(2)}, u32[]{:S(2)}) async-start(bf16[8,80,128]{2,1,0:T(8,128)(2,1)} %broadcast_in_dim.4), calls=%async_computation.2 | async-start | bytes 327680 | tf_op jit(solution)/shard_map/all_to_all | solution.py:519
  107.6 6.1 %copy-start.12 = (bf16[128,4096]{1,0:T(8,128)(2,1)}, bf16[128,4096]{1,0:T(8,128)(2,1)S(1)}, u32[]{:S(2)}) copy-start(bf16[128,4096]{1,0:T(8,128)(2,1)S(1)} %collective-permute-done.10.rest_2_.rest_3_) | copy-start | bytes 3145732
  107.6 6.1 %copy-start.13 = (bf16[128,4096]{1,0:T(8,128)(2,1)}, bf16[128,4096]{1,0:T(8,128)(2,1)S(1)}, u32[]{:S(2)}) copy-start(bf16[128,4096]{1,0:T(8,128)(2,1)S(1)} %collective-permute-done.9.rest_0_) | copy-start | bytes 3145732
  107.7 6.1 %collective-permute-start.13 = (bf16[5,80,768]{2,1,0:T(8,128)(2,1)}, bf16[5,80,768]{2,1,0:T(8,128)(2,1)S(1)}, u32[]{:S(2)}, u32[]{:S(2)}) collective-permute-start(bf16[5,80,768]{2,1,0:T(8,128)(2,1)} %get-tuple-element.65), channel_id=1, source_target_pairs={{0,1},{1,0},{2,3},{3,2},{4,5},{5,4},{6,7},{7,6},{8,9},{9,8},{10,11... | collective-permute-start | bytes 1843208 | tf_op jit(solution)/shard_map/ppermute | solution.py:407
  109.5 16.4 %collective-permute-start.12 = (bf16[64,4096]{1,0:T(8,128)(2,1)}, bf16[64,4096]{1,0:T(8,128)(2,1)S(1)}, u32[]{:S(2)}, u32[]{:S(2)}) collective-permute-start(bf16[64,4096]{1,0:T(8,128)(2,1)} %slice.18), channel_id=1, source_target_pairs={{4,0},{5,1},{6,2},{7,3},{8,12},{9,13},{10,14},{11,15},{20,16},{21,... | collective-permute-start | bytes 1572872 | tf_op jit(solution)/shard_map/ppermute | solution.py:407
  110.8 16.4 %collective-permute-start.11 = (bf16[64,4096]{1,0:T(8,128)(2,1)}, bf16[64,4096]{1,0:T(8,128)(2,1)}, u32[]{:S(2)}, u32[]{:S(2)}) collective-permute-start(bf16[64,4096]{1,0:T(8,128)(2,1)} %slice.17), channel_id=1, source_target_pairs={{0,2},{1,3},{2,0},{3,1},{12,14},{13,15},{14,12},{15,13},{16,18},{1... | collective-permute-start | bytes 1572872 | tf_op jit(solution)/shard_map/ppermute | solution.py:407
  125.2 17.6 %collective-permute-start.16 = (bf16[8,80,128]{2,1,0:T(8,128)(2,1)S(1)}, bf16[8,80,128]{2,1,0:T(8,128)(2,1)S(1)}, u32[]{:S(2)}, u32[]{:S(2)}) collective-permute-start(bf16[8,80,128]{2,1,0:T(8,128)(2,1)S(1)} %all-to-all-done.2), channel_id=1, source_target_pairs={{0,1},{1,0},{2,3},{3,2},{4,5},{5,4},{6,7},{7,6},{8,9},{9,8},{10,11... | collective-permute-start | bytes 491528 | tf_op jit(solution)/shard_map/ppermute | solution.py:407
  127.2 15.2 %copy-start.15 = (bf16[2,80,768]{2,1,0:T(8,128)(2,1)S(1)}, bf16[2,80,768]{2,1,0:T(8,128)(2,1)}, u32[]{:S(2)}) copy-start(bf16[2,80,768]{2,1,0:T(8,128)(2,1)} %get-tuple-element.74) | copy-start | bytes 737284
  137.1 11.8 %all-to-all-start.3 = ((f32[8,8,128]{2,1,0:T(8,128)}), f32[8,8,128]{2,1,0:T(8,128)S(1)}, u32[]{:S(2)}, u32[]{:S(2)}) async-start(f32[8,8,128]{2,1,0:T(8,128)} %get-tuple-element.72), calls=%async_computation.3 | async-start | bytes 65536 | tf_op jit(solution)/shard_map/all_to_all | solution.py:519
  142.2 6.7 %collective-permute-start.14 = (bf16[1,80,768]{2,1,0:T(8,128)(2,1)}, bf16[1,80,768]{2,1,0:T(8,128)(2,1)S(1)}, u32[]{:S(2)}, u32[]{:S(2)}) collective-permute-start(bf16[1,80,768]{2,1,0:T(8,128)(2,1)} %get-tuple-element.73), channel_id=1, source_target_pairs={{0,1},{1,0},{2,3},{3,2},{4,5},{5,4},{6,7},{7,6},{8,9},{9,8},{10,11... | collective-permute-start | bytes 368648 | tf_op jit(solution)/shard_map/ppermute | solution.py:407
  142.4 1.8 %collective-permute-start.15 = (bf16[2,80,768]{2,1,0:T(8,128)(2,1)S(1)}, bf16[2,80,768]{2,1,0:T(8,128)(2,1)S(1)}, u32[]{:S(2)}, u32[]{:S(2)}) collective-permute-start(bf16[2,80,768]{2,1,0:T(8,128)(2,1)S(1)} %copy-done.15), channel_id=1, source_target_pairs={{0,1},{1,0},{2,3},{3,2},{4,5},{5,4},{6,7},{7,6},{8,9},{9,8},{10,11... | collective-permute-start | bytes 737288 | tf_op jit(solution)/shard_map/ppermute | solution.py:407
  144.2 4.7 %copy-start.11 = (f32[8,128]{1,0:T(8,128)S(1)}, f32[8,128]{1,0:T(8,128)}, u32[]{:S(2)}) copy-start(f32[8,128]{1,0:T(8,128)} %get-tuple-element.76.__) | copy-start | bytes 12292
  (5 other events, 4.9 us)

commit v4 on v3

--- a/solution.py
+++ b/solution.py
@@ -126,7 +126,9 @@
         narrow_ref[i] = total[(i % 2) * 16 : (i % 2) * 16 + 16, (i // 2) * 128 : (i // 2) * 128 + 128]
     lane = lax.broadcasted_iota(jnp.int32, (16, 128), 1)
     row = lax.broadcasted_iota(jnp.int32, (16, 128), 0)
-    narrow_ref[devices - 1] = jnp.where((lane == own) & (row == 0), gate_term, F32(0.0))
+    coarse_gate = jnp.full((16, 128), gate_term, F32).astype(BF16).astype(F32)
+    parts = jnp.where(row == 0, coarse_gate, gate_term - coarse_gate)
+    narrow_ref[devices - 1] = jnp.where((lane == own) & (row < 2), parts, F32(0.0))
 
     table = share_table(routes_ref[...], weights_ref[...].astype(F32), devices)
     mine = slot_of(table)
@@ -161,7 +163,8 @@
         narrow_ref[chunk] = got_ref[j, 64:80, :].astype(F32)
     for i in range(2 * (first_ref.shape[1] // 128)):
         first_ref[(i % 2) * 16 : (i % 2) * 16 + 16, (i // 2) * 128 : (i // 2) * 128 + 128] = narrow_ref[i]
-    gate_ref[...] = narrow_ref[devices - 1][0:8]
+    gates = narrow_ref[devices - 1]
+    gate_ref[...] = jnp.broadcast_to(gates[0:1] + gates[1:2], gate_ref.shape)
 
 
 def expert_kernel(
@@ -240,7 +243,7 @@
         adapted_ref[unit] = dot(got_ref[source, 0:rank, :], first_ref[...], ROWS)
         for k in range(2):
             chosen_ref[k, unit] = jnp.where(place == slots[k : k + 1], F32(1.0), F32(0.0)).astype(BF16)
-            shares_ref[k, unit] = jnp.broadcast_to(columns[:, k : k + 1], (tokens, 128))
+            shares_ref[k, unit * tokens : (unit + 1) * tokens] = jnp.broadcast_to(columns[:, k : k + 1], (tokens, 128))
     results_ref[...] = jnp.zeros(results_ref.shape, F32)
     for copy in kept:
         copy.wait()
@@ -269,12 +272,14 @@
             by_token = dot(chosen, kept_ref[k, unit, :, span], ROWS)
             grad = grads[unit * tokens : (unit + 1) * tokens] + gate * adapted_ref[unit, :, span]
             partial = jnp.sum(by_token * grad, axis=1, keepdims=True)
-            results_ref[unit] += jnp.where(lane == k, partial, F32(0.0))
-            shared = dot(chosen, (shares_ref[k, unit, :, 0:1] * grad).astype(BF16), PLAIN)
+            own_rows = slice(unit * tokens, (unit + 1) * tokens)
+            results_ref[own_rows] += jnp.where(lane == k, partial, F32(0.0))
+            share = jnp.concatenate([shares_ref[k, own_rows]] * (tile // 128), axis=1)
+            shared = dot(chosen, (share * grad).astype(BF16), PLAIN)
             hidden_ref[k, unit, :, span] = shared.astype(BF16)
 
     for unit in range(units):
-        dots_ref[unit] = results_ref[unit].T[:8]
+        dots_ref[unit] = results_ref[unit * tokens : (unit + 1) * tokens].T[:8]
     writes = []
     for unit in range(units):
         source = place_ref[2 + unit]
@@ -332,8 +337,8 @@
             pltpu.VMEM((units, 8, tokens), F32),
             pltpu.VMEM((units, tokens, width_hidden), F32),
             pltpu.VMEM((2, units, cap, tokens), BF16),
-            pltpu.VMEM((2, units, tokens, 128), F32),
-            pltpu.VMEM((units, tokens, 128), F32),
+            pltpu.VMEM((2, units * tokens, 128), F32),
+            pltpu.VMEM((units * tokens, 128), F32),
             pltpu.SemaphoreType.DMA((loads,)),
             pltpu.SemaphoreType.DMA((2 * width_hidden // TILE,)),
             pltpu.SemaphoreType.DMA((2 * units,)),

time: 151 us -> 151 us (level)
  no operation moved by 1% of the time
where the time goes in v4:
time: 151 us; the launch traced here: 150 us
  Pallas kernels  57.4 us (38%)
  starting transfers between devices  40 us (26%)
  waiting for transfers between devices  36.4 us (24%)
  other arithmetic  8.29 us (5%)
  local copies, waits for them, and re-layouts  7.27 us (5%)
    pallas_call x4, Pallas kernels, expert_call(): pl.pallas_call(functools.partial(expert_kernel, layout=layout, slot=slot)...  48.1 us
    ppermute x17, waiting for transfers between devices, send(): return lax.ppermute(value, 'ex', pairs)  19.3 us
    ppermute x17, starting transfers between devices, send(): return lax.ppermute(value, 'ex', pairs)  18.1 us
    all_to_all x3, waiting for transfers between devices, small_body(): lax.all_to_all(value, 'ex', split_axis=0, concat_axis=0, axis_index_group...  14.8 us
    all_to_all x3, starting transfers between devices, small_body(): lax.all_to_all(value, 'ex', split_axis=0, concat_axis=0, axis_index_group...  14.6 us
    all_to_all x1, starting transfers between devices, small_body(): got = lax.all_to_all(packed, 'ex', split_axis=0, concat_axis=0, tiled=True)  7.28 us
    select_n x2, other arithmetic, small_body(): pick = lambda as_end, as_mid: jnp.where(is_end == 1, as_end, as_mid)  5.68 us
    pallas_call x1, Pallas kernels, small_body(): pl.pallas_call(low_rank_kernel, in_specs=[smem] + whole(3) + [smem] + who...  3.94 us
  transfers between devices with their start and end apart: 21, of which 9 were waited for; matrix products, arithmetic and copies ran while one was open for 6% of the time, Pallas kernels for 37%

profile of v4, /device:TPU:0, one launch (start us, length us, event | category | flops | bytes accessed | tf_op | source)
XLA Modules:
  0.0 150.1 jit_solution(14939369139975533084)
XLA Ops:
  1.3 1.2 copy-done.5
  4.0 1.7 %collective-permute-start.2 = (bf16[128,4096]{1,0:T(8,128)(2,1)S(1)}, bf16[128,4096]{1,0:T(8,128)(2,1)}, u32[]{:S(2)}, u32[]{:S(2)}) collective-permute-start(bf16[128,4096]{1,0:T(8,128)(2,1)S(1)} %shard_map.128.rows_ref.rest_0_.rest_1_), channel_id=1, source_target_pairs={{4,8},{5,9},{6,10},{7,11},{8,4},{9,5},{10,6},{11,7},{20,24},{21,25... | collective-permute-start | bytes 3145736 | tf_op jit(solution)/shard_map/ppermute | solution.py:412
  5.6 2.9 %collective-permute-start.1 = (bf16[128,4096]{1,0:T(8,128)(2,1)S(1)}, bf16[128,4096]{1,0:T(8,128)(2,1)}, u32[]{:S(2)}, u32[]{:S(2)}) collective-permute-start(bf16[128,4096]{1,0:T(8,128)(2,1)S(1)} %shard_map.128.rows_ref.rest_0_.rest_1_), channel_id=1, source_target_pairs={{0,2},{1,3},{2,0},{3,1},{4,6},{5,7},{6,4},{7,5},{8,10},{9,11},{10,... | collective-permute-start | bytes 3145736 | tf_op jit(solution)/shard_map/ppermute | solution.py:412
  8.6 3.5 %collective-permute-start = (bf16[128,4096]{1,0:T(8,128)(2,1)S(1)}, bf16[128,4096]{1,0:T(8,128)(2,1)}, u32[]{:S(2)}, u32[]{:S(2)}) collective-permute-start(bf16[128,4096]{1,0:T(8,128)(2,1)S(1)} %shard_map.128.rows_ref.rest_0_.rest_1_), channel_id=1, source_target_pairs={{0,4},{1,5},{2,6},{3,7},{4,0},{5,1},{6,2},{7,3},{8,12},{9,13},{10,... | collective-permute-start | bytes 3145736 | tf_op jit(solution)/shard_map/ppermute | solution.py:412
  12.1 2.1 %collective-permute-done.3.other_stored_ref = bf16[16,80,768]{2,1,0:T(8,128)(2,1)} collective-permute-done((bf16[16,80,768]{2,1,0:T(8,128)(2,1)}, bf16[16,80,768]{2,1,0:T(8,128)(2,1)}, u32[]{:S(2)}, u32[]{:S(2)}) %collective-permute-start.3) | collective-permute-done | bytes 1966112 | tf_op jit(solution)/shard_map/ppermute | solution.py:412
  15.1 1.4 shard_map.129
  17.3 7.3 %all-to-all-start = ((bf16[16,80,128]{2,1,0:T(8,128)(2,1)}), bf16[16,80,128]{2,1,0:T(8,128)(2,1)S(1)}, u32[]{:S(2)}, u32[]{:S(2)}) async-start(bf16[16,80,128]{2,1,0:T(8,128)(2,1)} %copy-done.4), calls=%async_computation | async-start | bytes 655360 | tf_op jit(solution)/shard_map/all_to_all | solution.py:509
  24.6 7.9 %collective-permute-done.1.rest_2_.rest_3_ = bf16[128,4096]{1,0:T(8,128)(2,1)} collective-permute-done((bf16[128,4096]{1,0:T(8,128)(2,1)S(1)}, bf16[128,4096]{1,0:T(8,128)(2,1)}, u32[]{:S(2)}, u32[]{:S(2)}) %collective-permute-start.1) | collective-permute-done | bytes 1048608 | tf_op jit(solution)/shard_map/ppermute | solution.py:412
  32.5 6.4 %collective-permute-done.rest_0_.rest_1_ = bf16[128,4096]{1,0:T(8,128)(2,1)} collective-permute-done((bf16[128,4096]{1,0:T(8,128)(2,1)S(1)}, bf16[128,4096]{1,0:T(8,128)(2,1)}, u32[]{:S(2)}, u32[]{:S(2)}) %collective-permute-start) | collective-permute-done | bytes 1048608 | tf_op jit(solution)/shard_map/ppermute | solution.py:412
  38.9 2.3 %all-to-all-done.got_ref = bf16[16,80,128]{2,1,0:T(8,128)(2,1)S(1)} async-done(((bf16[16,80,128]{2,1,0:T(8,128)(2,1)}), bf16[16,80,128]{2,1,0:T(8,128)(2,1)S(1)}, u32[]{:S(2)}, u32[]{:S(2)}) %all-to-all-start) | async-done | bytes 327712 | tf_op jit(solution)/shard_map/all_to_all | solution.py:509
  41.2 1.6 %collective-permute-start.6 = (bf16[128,4096]{1,0:T(8,128)(2,1)}, bf16[128,4096]{1,0:T(8,128)(2,1)}, u32[]{:S(2)}, u32[]{:S(2)}) collective-permute-start(bf16[128,4096]{1,0:T(8,128)(2,1)} %collective-permute-done.rest_0_.rest_1_), channel_id=1, source_target_pairs={{4,8},{5,9},{6,10},{7,11},{8,4},{9,5},{10,6},{11,7},{20,24},{21,25... | collective-permute-start | bytes 3145736 | tf_op jit(solution)/shard_map/ppermute | solution.py:412
  42.8 3.4 %broadcast_select_fusion.1 = (bf16[128,4096]{1,0:T(8,128)(2,1)}, bf16[128,4096]{1,0:T(8,128)(2,1)}) fusion(bf16[128,4096]{1,0:T(8,128)(2,1)} %collective-permute-done.rest_0_.rest_1_, bf16[128,4096]{1,0:T(8,128)(2,1)} %collective-permute-done.2.rest_1_, pred[]{:T(512)S(6)} %eq.13, bf16[128,4096]{1,0:T(8,128)(2,1)} %collective-permute-done.1.rest_2_.rest_3_), kind=kLoop, calls=%fused_computation.1 | loop fusion | flops 1048576 | bytes 5242881 | tf_op jit(solution)/shard_map/jit(_where)/select_n | solution.py:451
  46.2 2.0 %collective-permute-start.5 = (bf16[128,4096]{1,0:T(8,128)(2,1)}, bf16[128,4096]{1,0:T(8,128)(2,1)}, u32[]{:S(2)}, u32[]{:S(2)}) collective-permute-start(bf16[128,4096]{1,0:T(8,128)(2,1)} %get-tuple-element.86), channel_id=1, source_target_pairs={{0,4},{1,5},{2,6},{3,7},{4,0},{5,1},{6,2},{7,3},{8,12},{9,13},{10,... | collective-permute-start | bytes 3145736 | tf_op jit(solution)/shard_map/ppermute | solution.py:412
  48.2 3.9 %shard_map.130 = f32[16,80,128]{2,1,0:T(8,128)S(1)} custom-call(s32[1]{0:T(128)} %bitcast.own_ref, bf16[16,80,128]{2,1,0:T(8,128)(2,1)S(1)} %all-to-all-done.got_ref, bf16[16,80,768]{2,1,0:T(8,128)(2,1)S(1)} %bitcast.25, bf16[32,768]{1,0:T(8,128)(2,1)S(1)} %bitcast.31, f32[16]{0:T(128)S(1)} %copy-done.8, s32[8,128]{1,0:T(8,128)S(1)} %bitcast.33, ...), custom_call_target="tpu_custom_call" | custom-call | flops 1000000 | bytes 10000 | tf_op jit(solution)/shard_map/pallas_call | solution.py:514
  52.3 1.6 %collective-permute-done.8 = f32[8,80,128]{2,1,0:T(8,128)S(1)} collective-permute-done((f32[8,80,128]{2,1,0:T(8,128)S(1)}, f32[8,80,128]{2,1,0:T(8,128)S(1)}, u32[]{:S(2)}, u32[]{:S(2)}) %collective-permute-start.8) | collective-permute-done | bytes 327712 | tf_op jit(solution)/shard_map/ppermute | solution.py:412
  54.6 4.1 %all-to-all-start.1 = ((bf16[8,80,128]{2,1,0:T(8,128)(2,1)}), bf16[8,80,128]{2,1,0:T(8,128)(2,1)S(1)}, u32[]{:S(2)}, u32[]{:S(2)}) async-start(bf16[8,80,128]{2,1,0:T(8,128)(2,1)} %fusion), calls=%async_computation.1 | async-start | bytes 327680 | tf_op jit(solution)/shard_map/all_to_all | solution.py:524
  59.3 9.8 %shard_map.131 = (bf16[16,80,768]{2,1,0:T(8,128)(2,1)}, bf16[5,80,768]{2,1,0:T(8,128)(2,1)}, f32[8,8,128]{2,1,0:T(8,128)}, f32[8,128]{1,0:T(8,128)}) custom-call(s32[3]{0:T(128)} %pad_add_fusion.2.place_ref, f32[16]{0:T(128)} %gate_ref.11, bf16[1,768,4096]{2,1,0:T(8,128)(2,1)} %weight_ref.7, bf16[1,768,4096]{2,1,0:T(8,128)(2,1)} %collective-permute-done.4.other_weight_ref, ...), custom_call_target="tpu_custom_call" | custom-call | flops 1000000 | bytes 10000 | tf_op jit(solution)/shard_map/pallas_call | solution.py:322
  69.1 7.0 %all-to-all-done.1 = bf16[8,80,128]{2,1,0:T(8,128)(2,1)S(1)} async-done(((bf16[8,80,128]{2,1,0:T(8,128)(2,1)}), bf16[8,80,128]{2,1,0:T(8,128)(2,1)S(1)}, u32[]{:S(2)}, u32[]{:S(2)}) %all-to-all-start.1) | async-done | bytes 163872 | tf_op jit(solution)/shard_map/all_to_all | solution.py:524
  76.1 2.3 %broadcast_select_fusion = bf16[128,4096]{1,0:T(8,128)(2,1)} fusion(bf16[128,4096]{1,0:T(8,128)(2,1)} %collective-permute-done.5.rest_4_.rest_7_, bf16[128,4096]{1,0:T(8,128)(2,1)} %collective-permute-done.6.rest_5_, pred[]{:T(512)S(6)} %eq.13), kind=kLoop, calls=%fused_computation | loop fusion | flops 524288 | bytes 3145729 | tf_op jit(solution)/shard_map/jit(_where)/select_n | solution.py:451
  78.5 1.3 collective-permute-start.9
  80.5 5.4 %all-to-all-start.2 = ((bf16[8,80,128]{2,1,0:T(8,128)(2,1)}), bf16[8,80,128]{2,1,0:T(8,128)(2,1)S(1)}, u32[]{:S(2)}, u32[]{:S(2)}) async-start(bf16[8,80,128]{2,1,0:T(8,128)(2,1)} %broadcast_in_dim.4), calls=%async_computation.2 | async-start | bytes 327680 | tf_op jit(solution)/shard_map/all_to_all | solution.py:524
  86.6 17.1 %shard_map.132 = (bf16[16,80,768]{2,1,0:T(8,128)(2,1)}, bf16[5,80,768]{2,1,0:T(8,128)(2,1)}, f32[8,8,128]{2,1,0:T(8,128)}, f32[8,128]{1,0:T(8,128)}) custom-call(s32[6]{0:T(128)} %stack.52.place_ref, f32[16]{0:T(128)} %gate_ref.11, bf16[1,768,4096]{2,1,0:T(8,128)(2,1)} %weight_ref.7, ...), custom_call_target="tpu_custom_call", output_to_operand_aliasing={{0}: (17, {}), {1}: (18, {}), {2}: (19, {})} | custom-call | flops 1000000 | bytes 10000 | tf_op jit(solution)/shard_map/pallas_call | solution.py:322
  103.6 4.0 %all-to-all-done.2 = bf16[8,80,128]{2,1,0:T(8,128)(2,1)S(1)} async-done(((bf16[8,80,128]{2,1,0:T(8,128)(2,1)}), bf16[8,80,128]{2,1,0:T(8,128)(2,1)S(1)}, u32[]{:S(2)}, u32[]{:S(2)}) %all-to-all-start.2) | async-done | bytes 163872 | tf_op jit(solution)/shard_map/all_to_all | solution.py:524
  107.7 1.0 slice.17
  109.5 1.3 collective-permute-start.12
  110.8 2.3 %collective-permute-start.11 = (bf16[64,4096]{1,0:T(8,128)(2,1)}, bf16[64,4096]{1,0:T(8,128)(2,1)}, u32[]{:S(2)}, u32[]{:S(2)}) collective-permute-start(bf16[64,4096]{1,0:T(8,128)(2,1)} %slice.17), channel_id=1, source_target_pairs={{0,2},{1,3},{2,0},{3,1},{12,14},{13,15},{14,12},{15,13},{16,18},{1... | collective-permute-start | bytes 1572872 | tf_op jit(solution)/shard_map/ppermute | solution.py:412
  113.8 11.4 %shard_map.133 = (bf16[16,80,768]{2,1,0:T(8,128)(2,1)}, bf16[2,80,768]{2,1,0:T(8,128)(2,1)}, f32[8,8,128]{2,1,0:T(8,128)}, f32[8,128]{1,0:T(8,128)}) custom-call(s32[4]{0:T(128)} %pad_add_fusion.3.place_ref, f32[16]{0:T(128)} %gate_ref.11, bf16[1,768,4096]{2,1,0:T(8,128)(2,1)} %weight_ref.7, ...), custom_call_target="tpu_custom_call", output_to_operand_aliasing={{0}: (13, {}), {2}: (14, {})} | custom-call | flops 1000000 | bytes 10000 | tf_op jit(solution)/shard_map/pallas_call | solution.py:322
  125.9 1.3 collective-permute-done.11.rest_0_
  127.2 9.9 %shard_map.134 = (bf16[16,80,768]{2,1,0:T(8,128)(2,1)}, bf16[1,80,768]{2,1,0:T(8,128)(2,1)}, f32[8,8,128]{2,1,0:T(8,128)}, f32[8,128]{1,0:T(8,128)}) custom-call(s32[3]{0:T(128)} %pad_add_fusion.place_ref, f32[16]{0:T(128)} %gate_ref.11, bf16[1,768,4096]{2,1,0:T(8,128)(2,1)} %weight_ref.7, ...), custom_call_target="tpu_custom_call", output_to_operand_aliasing={{0}: (12, {}), {2}: (13, {})} | custom-call | flops 1000000 | bytes 10000 | tf_op jit(solution)/shard_map/pallas_call | solution.py:322
  137.1 5.1 %all-to-all-start.3 = ((f32[8,8,128]{2,1,0:T(8,128)}), f32[8,8,128]{2,1,0:T(8,128)S(1)}, u32[]{:S(2)}, u32[]{:S(2)}) async-start(f32[8,8,128]{2,1,0:T(8,128)} %get-tuple-element.72), calls=%async_computation.3 | async-start | bytes 65536 | tf_op jit(solution)/shard_map/all_to_all | solution.py:524
  145.1 3.8 %all-to-all-done.3.dots_ref = f32[8,8,128]{2,1,0:T(8,128)S(1)} async-done(((f32[8,8,128]{2,1,0:T(8,128)}), f32[8,8,128]{2,1,0:T(8,128)S(1)}, u32[]{:S(2)}, u32[]{:S(2)}) %all-to-all-start.3) | async-done | bytes 32800 | tf_op jit(solution)/shard_map/all_to_all | solution.py:524
  148.9 1.3 shard_map.136
  (66 shorter events, 11.9 us)
Async XLA Ops:
  0.6 13.5 %copy-start = (bf16[1,16,80,768]{3,2,1,0:T(8,128)(2,1)S(1)}, bf16[1,16,80,768]{3,2,1,0:T(8,128)(2,1)}, u32[]{:S(2)}) copy-start(bf16[1,16,80,768]{3,2,1,0:T(8,128)(2,1)} %param.13) | copy-start | bytes 5898244
  0.6 13.5 %copy-start.3 = (bf16[768,32]{0,1:T(8,128)(2,1)S(1)}, bf16[768,32]{0,1:T(8,128)(2,1)}, u32[]{:S(2)}) copy-start(bf16[768,32]{0,1:T(8,128)(2,1)} %param.15) | copy-start | bytes 147460
  0.7 40.5 %collective-permute-start.4 = (bf16[1,768,4096]{2,1,0:T(8,128)(2,1)}, bf16[1,768,4096]{2,1,0:T(8,128)(2,1)}, u32[]{:S(2)}, u32[]{:S(2)}) collective-permute-start(bf16[1,768,4096]{2,1,0:T(8,128)(2,1)} %weight_ref.7), channel_id=1, source_target_pairs={{0,1},{1,0},{2,3},{3,2},{4,5},{5,4},{6,7},{7,6},{8,9},{9,8},{10,11... | collective-permute-start | bytes 18874376 | tf_op jit(solution)/shard_map/ppermute | solution.py:412
  1.2 12.9 %collective-permute-start.3 = (bf16[16,80,768]{2,1,0:T(8,128)(2,1)}, bf16[16,80,768]{2,1,0:T(8,128)(2,1)}, u32[]{:S(2)}, u32[]{:S(2)}) collective-permute-start(bf16[16,80,768]{2,1,0:T(8,128)(2,1)} %bitcast.19), channel_id=1, source_target_pairs={{0,1},{1,0},{2,3},{3,2},{4,5},{5,4},{6,7},{7,6},{8,9},{9,8},{10,11... | collective-permute-start | bytes 5898248 | tf_op jit(solution)/shard_map/ppermute | solution.py:412
  3.2 10.9 %copy-start.7 = (s32[128,8]{0,1:T(8,128)S(1)}, s32[128,8]{0,1:T(8,128)}, u32[]{:S(2)}) copy-start(s32[128,8]{0,1:T(8,128)} %param.11) | copy-start | bytes 12292
  3.2 10.9 %copy-start.8 = (f32[16]{0:T(128)S(1)}, f32[16]{0:T(128)}, u32[]{:S(2)}) copy-start(f32[16]{0:T(128)} %gate_ref.11) | copy-start | bytes 196
  3.2 10.9 %copy-start.10 = (bf16[128,8]{0,1:T(8,128)(2,1)S(1)}, bf16[128,8]{0,1:T(8,128)(2,1)}, u32[]{:S(2)}) copy-start(bf16[128,8]{0,1:T(8,128)(2,1)} %param.12) | copy-start | bytes 6148
  4.0 44.2 %copy-start.1 = (bf16[128,4096]{1,0:T(8,128)(2,1)}, bf16[128,4096]{1,0:T(8,128)(2,1)S(1)}, u32[]{:S(2)}) copy-start(bf16[128,4096]{1,0:T(8,128)(2,1)S(1)} %shard_map.128.rows_ref.rest_0_.rest_1_) | copy-start | bytes 3145732
  4.0 20.6 %collective-permute-start.2 = (bf16[128,4096]{1,0:T(8,128)(2,1)S(1)}, bf16[128,4096]{1,0:T(8,128)(2,1)}, u32[]{:S(2)}, u32[]{:S(2)}) collective-permute-start(bf16[128,4096]{1,0:T(8,128)(2,1)S(1)} %shard_map.128.rows_ref.rest_0_.rest_1_), channel_id=1, source_target_pairs={{4,8},{5,9},{6,10},{7,11},{8,4},{9,5},{10,6},{11,7},{20,24},{21,25... | collective-permute-start | bytes 3145736 | tf_op jit(solution)/shard_map/ppermute | solution.py:412
  5.6 26.9 %collective-permute-start.1 = (bf16[128,4096]{1,0:T(8,128)(2,1)S(1)}, bf16[128,4096]{1,0:T(8,128)(2,1)}, u32[]{:S(2)}, u32[]{:S(2)}) collective-permute-start(bf16[128,4096]{1,0:T(8,128)(2,1)S(1)} %shard_map.128.rows_ref.rest_0_.rest_1_), channel_id=1, source_target_pairs={{0,2},{1,3},{2,0},{3,1},{4,6},{5,7},{6,4},{7,5},{8,10},{9,11},{10,... | collective-permute-start | bytes 3145736 | tf_op jit(solution)/shard_map/ppermute | solution.py:412
  8.6 30.3 %collective-permute-start = (bf16[128,4096]{1,0:T(8,128)(2,1)S(1)}, bf16[128,4096]{1,0:T(8,128)(2,1)}, u32[]{:S(2)}, u32[]{:S(2)}) collective-permute-start(bf16[128,4096]{1,0:T(8,128)(2,1)S(1)} %shard_map.128.rows_ref.rest_0_.rest_1_), channel_id=1, source_target_pairs={{0,4},{1,5},{2,6},{3,7},{4,0},{5,1},{6,2},{7,3},{8,12},{9,13},{10,... | collective-permute-start | bytes 3145736 | tf_op jit(solution)/shard_map/ppermute | solution.py:412
  17.3 23.9 %all-to-all-start = ((bf16[16,80,128]{2,1,0:T(8,128)(2,1)}), bf16[16,80,128]{2,1,0:T(8,128)(2,1)S(1)}, u32[]{:S(2)}, u32[]{:S(2)}) async-start(bf16[16,80,128]{2,1,0:T(8,128)(2,1)} %copy-done.4), calls=%async_computation | async-start | bytes 655360 | tf_op jit(solution)/shard_map/all_to_all | solution.py:509
  41.2 7.0 %copy-start.2 = (bf16[16,80,128]{2,1,0:T(8,128)(2,1)}, bf16[16,80,128]{2,1,0:T(8,128)(2,1)S(1)}, u32[]{:S(2)}) copy-start(bf16[16,80,128]{2,1,0:T(8,128)(2,1)S(1)} %all-to-all-done.got_ref) | copy-start | bytes 983044
  41.2 34.9 %collective-permute-start.6 = (bf16[128,4096]{1,0:T(8,128)(2,1)}, bf16[128,4096]{1,0:T(8,128)(2,1)}, u32[]{:S(2)}, u32[]{:S(2)}) collective-permute-start(bf16[128,4096]{1,0:T(8,128)(2,1)} %collective-permute-done.rest_0_.rest_1_), channel_id=1, source_target_pairs={{4,8},{5,9},{6,10},{7,11},{8,4},{9,5},{10,6},{11,7},{20,24},{21,25... | collective-permute-start | bytes 3145736 | tf_op jit(solution)/shard_map/ppermute | solution.py:412
  46.2 29.9 %collective-permute-start.7 = (bf16[128,4096]{1,0:T(8,128)(2,1)}, bf16[128,4096]{1,0:T(8,128)(2,1)}, u32[]{:S(2)}, u32[]{:S(2)}) collective-permute-start(bf16[128,4096]{1,0:T(8,128)(2,1)} %get-tuple-element.85), channel_id=1, source_target_pairs={{0,2},{1,3},{2,0},{3,1},{4,6},{5,7},{6,4},{7,5},{8,10},{9,11},{10,... | collective-permute-start | bytes 3145736 | tf_op jit(solution)/shard_map/ppermute | solution.py:412
  46.2 29.9 %collective-permute-start.5 = (bf16[128,4096]{1,0:T(8,128)(2,1)}, bf16[128,4096]{1,0:T(8,128)(2,1)}, u32[]{:S(2)}, u32[]{:S(2)}) collective-permute-start(bf16[128,4096]{1,0:T(8,128)(2,1)} %get-tuple-element.86), channel_id=1, source_target_pairs={{0,4},{1,5},{2,6},{3,7},{4,0},{5,1},{6,2},{7,3},{8,12},{9,13},{10,... | collective-permute-start | bytes 3145736 | tf_op jit(solution)/shard_map/ppermute | solution.py:412
  52.2 1.7 %collective-permute-start.8 = (f32[8,80,128]{2,1,0:T(8,128)S(1)}, f32[8,80,128]{2,1,0:T(8,128)S(1)}, u32[]{:S(2)}, u32[]{:S(2)}) collective-permute-start(f32[8,80,128]{2,1,0:T(8,128)S(1)} %slice.21), channel_id=1, source_target_pairs={{0,1},{1,0},{2,3},{3,2},{4,5},{5,4},{6,7},{7,6},{8,9},{9,8},{10,11... | collective-permute-start | bytes 983048 | tf_op jit(solution)/shard_map/ppermute | solution.py:412
  54.6 21.5 %all-to-all-start.1 = ((bf16[8,80,128]{2,1,0:T(8,128)(2,1)}), bf16[8,80,128]{2,1,0:T(8,128)(2,1)S(1)}, u32[]{:S(2)}, u32[]{:S(2)}) async-start(bf16[8,80,128]{2,1,0:T(8,128)(2,1)} %fusion), calls=%async_computation.1 | async-start | bytes 327680 | tf_op jit(solution)/shard_map/all_to_all | solution.py:524
  78.4 29.2 %collective-permute-start.10 = (bf16[128,4096]{1,0:T(8,128)(2,1)}, bf16[128,4096]{1,0:T(8,128)(2,1)S(1)}, u32[]{:S(2)}, u32[]{:S(2)}) collective-permute-start(bf16[128,4096]{1,0:T(8,128)(2,1)} %broadcast_select_fusion), channel_id=1, source_target_pairs={{0,2},{1,3},{2,0},{3,1},{4,6},{5,7},{6,4},{7,5},{8,10},{9,11},{10,... | collective-permute-start | bytes 3145736 | tf_op jit(solution)/shard_map/ppermute | solution.py:412
  78.5 29.1 %collective-permute-start.9 = (bf16[128,4096]{1,0:T(8,128)(2,1)}, bf16[128,4096]{1,0:T(8,128)(2,1)S(1)}, u32[]{:S(2)}, u32[]{:S(2)}) collective-permute-start(bf16[128,4096]{1,0:T(8,128)(2,1)} %collective-permute-done.6.rest_5_), channel_id=1, source_target_pairs={{4,0},{5,1},{6,2},{7,3},{8,12},{9,13},{10,14},{11,15},{20,16},{21,... | collective-permute-start | bytes 3145736 | tf_op jit(solution)/shard_map/ppermute | solution.py:412
  80.5 27.1 %all-to-all-start.2 = ((bf16[8,80,128]{2,1,0:T(8,128)(2,1)}), bf16[8,80,128]{2,1,0:T(8,128)(2,1)S(1)}, u32[]{:S(2)}, u32[]{:S(2)}) async-start(bf16[8,80,128]{2,1,0:T(8,128)(2,1)} %broadcast_in_dim.4), calls=%async_computation.2 | async-start | bytes 327680 | tf_op jit(solution)/shard_map/all_to_all | solution.py:524
  107.6 6.1 %copy-start.12 = (bf16[128,4096]{1,0:T(8,128)(2,1)}, bf16[128,4096]{1,0:T(8,128)(2,1)S(1)}, u32[]{:S(2)}) copy-start(bf16[128,4096]{1,0:T(8,128)(2,1)S(1)} %collective-permute-done.10.rest_2_.rest_3_) | copy-start | bytes 3145732
  107.6 6.1 %copy-start.13 = (bf16[128,4096]{1,0:T(8,128)(2,1)}, bf16[128,4096]{1,0:T(8,128)(2,1)S(1)}, u32[]{:S(2)}) copy-start(bf16[128,4096]{1,0:T(8,128)(2,1)S(1)} %collective-permute-done.9.rest_0_) | copy-start | bytes 3145732
  107.7 6.1 %collective-permute-start.13 = (bf16[5,80,768]{2,1,0:T(8,128)(2,1)}, bf16[5,80,768]{2,1,0:T(8,128)(2,1)S(1)}, u32[]{:S(2)}, u32[]{:S(2)}) collective-permute-start(bf16[5,80,768]{2,1,0:T(8,128)(2,1)} %get-tuple-element.65), channel_id=1, source_target_pairs={{0,1},{1,0},{2,3},{3,2},{4,5},{5,4},{6,7},{7,6},{8,9},{9,8},{10,11... | collective-permute-start | bytes 1843208 | tf_op jit(solution)/shard_map/ppermute | solution.py:412
  109.5 16.4 %collective-permute-start.12 = (bf16[64,4096]{1,0:T(8,128)(2,1)}, bf16[64,4096]{1,0:T(8,128)(2,1)S(1)}, u32[]{:S(2)}, u32[]{:S(2)}) collective-permute-start(bf16[64,4096]{1,0:T(8,128)(2,1)} %slice.18), channel_id=1, source_target_pairs={{4,0},{5,1},{6,2},{7,3},{8,12},{9,13},{10,14},{11,15},{20,16},{21,... | collective-permute-start | bytes 1572872 | tf_op jit(solution)/shard_map/ppermute | solution.py:412
  110.8 16.4 %collective-permute-start.11 = (bf16[64,4096]{1,0:T(8,128)(2,1)}, bf16[64,4096]{1,0:T(8,128)(2,1)}, u32[]{:S(2)}, u32[]{:S(2)}) collective-permute-start(bf16[64,4096]{1,0:T(8,128)(2,1)} %slice.17), channel_id=1, source_target_pairs={{0,2},{1,3},{2,0},{3,1},{12,14},{13,15},{14,12},{15,13},{16,18},{1... | collective-permute-start | bytes 1572872 | tf_op jit(solution)/shard_map/ppermute | solution.py:412
  125.2 17.6 %collective-permute-start.16 = (bf16[8,80,128]{2,1,0:T(8,128)(2,1)S(1)}, bf16[8,80,128]{2,1,0:T(8,128)(2,1)S(1)}, u32[]{:S(2)}, u32[]{:S(2)}) collective-permute-start(bf16[8,80,128]{2,1,0:T(8,128)(2,1)S(1)} %all-to-all-done.2), channel_id=1, source_target_pairs={{0,1},{1,0},{2,3},{3,2},{4,5},{5,4},{6,7},{7,6},{8,9},{9,8},{10,11... | collective-permute-start | bytes 491528 | tf_op jit(solution)/shard_map/ppermute | solution.py:412
  127.2 15.2 %copy-start.15 = (bf16[2,80,768]{2,1,0:T(8,128)(2,1)S(1)}, bf16[2,80,768]{2,1,0:T(8,128)(2,1)}, u32[]{:S(2)}) copy-start(bf16[2,80,768]{2,1,0:T(8,128)(2,1)} %get-tuple-element.74) | copy-start | bytes 737284
  137.1 11.8 %all-to-all-start.3 = ((f32[8,8,128]{2,1,0:T(8,128)}), f32[8,8,128]{2,1,0:T(8,128)S(1)}, u32[]{:S(2)}, u32[]{:S(2)}) async-start(f32[8,8,128]{2,1,0:T(8,128)} %get-tuple-element.72), calls=%async_computation.3 | async-start | bytes 65536 | tf_op jit(solution)/shard_map/all_to_all | solution.py:524
  142.2 6.7 %collective-permute-start.14 = (bf16[1,80,768]{2,1,0:T(8,128)(2,1)}, bf16[1,80,768]{2,1,0:T(8,128)(2,1)S(1)}, u32[]{:S(2)}, u32[]{:S(2)}) collective-permute-start(bf16[1,80,768]{2,1,0:T(8,128)(2,1)} %get-tuple-element.73), channel_id=1, source_target_pairs={{0,1},{1,0},{2,3},{3,2},{4,5},{5,4},{6,7},{7,6},{8,9},{9,8},{10,11... | collective-permute-start | bytes 368648 | tf_op jit(solution)/shard_map/ppermute | solution.py:412
  142.4 1.8 %collective-permute-start.15 = (bf16[2,80,768]{2,1,0:T(8,128)(2,1)S(1)}, bf16[2,80,768]{2,1,0:T(8,128)(2,1)S(1)}, u32[]{:S(2)}, u32[]{:S(2)}) collective-permute-start(bf16[2,80,768]{2,1,0:T(8,128)(2,1)S(1)} %copy-done.15), channel_id=1, source_target_pairs={{0,1},{1,0},{2,3},{3,2},{4,5},{5,4},{6,7},{7,6},{8,9},{9,8},{10,11... | collective-permute-start | bytes 737288 | tf_op jit(solution)/shard_map/ppermute | solution.py:412
  144.1 4.7 %copy-start.11 = (f32[8,128]{1,0:T(8,128)S(1)}, f32[8,128]{1,0:T(8,128)}, u32[]{:S(2)}) copy-start(f32[8,128]{1,0:T(8,128)} %get-tuple-element.76.__) | copy-start | bytes 12292
  (5 other events, 4.9 us)

commit v5 on v4

--- a/solution.py
+++ b/solution.py
@@ -9,7 +9,7 @@
 
 F32, BF16 = jnp.float32, jnp.bfloat16
 VMEM_LIMIT = 16 * 1024 * 1024
-BIG_LIMIT = 59 * 1024 * 1024
+BIG_LIMIT = 50 * 1024 * 1024
 TILE, AHEAD = 384, 2
 ROWS = (((0,), (0,)), ((), ()))
 LANES = (((1,), (1,)), ((), ()))

time: 151 us -> 149 us (0.987)
  Pallas kernels: 57.4 us -> 54 us
    pallas_call x4, Pallas kernels: 48.1 us -> 44.7 us  [expert_call(): pl.pallas_call(functools.partial(expert_kernel, layout=layout, slot=slot)...]
    ppermute x17, waiting for transfers between devices: 19.3 us -> 21.8 us  [send(): return lax.ppermute(value, 'ex', pairs)]
    unnamed x32 -> x24, local copies, waits for them, and re-layouts: 3.66 us -> 5.28 us
    another operation x3, other arithmetic: 1.84 us -> 0.23 us  [experts(): place = jnp.stack([own, is_end] + [own ^ mask << 1 for mask in turns])]
  transfers between devices with their start and end apart: 21 -> 21, of which waited for: 9 -> 10; matrix products, arithmetic and copies ran while one was open for 6% -> 6% of each run, Pallas kernels for 37% -> 35%
where the time goes in v5:
time: 149 us
  Pallas kernels  54 us (36%)
  starting transfers between devices  39.5 us (27%)
  waiting for transfers between devices  37.6 us (25%)
  other arithmetic  8.57 us (6%)
  local copies, waits for them, and re-layouts  8.27 us (6%)
    pallas_call x4, Pallas kernels, expert_call(): pl.pallas_call(functools.partial(expert_kernel, layout=layout, slot=slot)...  44.7 us
    ppermute x17, waiting for transfers between devices, send(): return lax.ppermute(value, 'ex', pairs)  21.8 us
    ppermute x17, starting transfers between devices, send(): return lax.ppermute(value, 'ex', pairs)  18.1 us
    all_to_all x3, starting transfers between devices, small_body(): lax.all_to_all(value, 'ex', split_axis=0, concat_axis=0, axis_index_group...  14 us
    all_to_all x3, waiting for transfers between devices, small_body(): lax.all_to_all(value, 'ex', split_axis=0, concat_axis=0, axis_index_group...  13.4 us
    all_to_all x1, starting transfers between devices, small_body(): got = lax.all_to_all(packed, 'ex', split_axis=0, concat_axis=0, tiled=True)  7.28 us
    select_n x2, other arithmetic, small_body(): pick = lambda as_end, as_mid: jnp.where(is_end == 1, as_end, as_mid)  5.74 us
    unnamed x24, local copies, waits for them, and re-layouts  5.28 us
  transfers between devices with their start and end apart: 21, of which 10 were waited for; matrix products, arithmetic and copies ran while one was open for 6% of the time, Pallas kernels for 35%

profile of v5, /device:TPU:0, one launch (start us, length us, event | category | flops | bytes accessed | tf_op | source)
XLA Modules:
  0.0 148.7 jit_solution(6685870813954657225)
XLA Ops:
  1.3 1.2 copy-done.3
  4.0 1.7 %collective-permute-start.2 = (bf16[128,4096]{1,0:T(8,128)(2,1)S(1)}, bf16[128,4096]{1,0:T(8,128)(2,1)}, u32[]{:S(2)}, u32[]{:S(2)}) collective-permute-start(bf16[128,4096]{1,0:T(8,128)(2,1)S(1)} %shard_map.128.rows_ref.rest_0_.rest_1_), channel_id=1, source_target_pairs={{4,8},{5,9},{6,10},{7,11},{8,4},{9,5},{10,6},{11,7},{20,24},{21,25... | collective-permute-start | bytes 3145736 | tf_op jit(solution)/shard_map/ppermute | solution.py:412
  5.7 2.9 %collective-permute-start.1 = (bf16[128,4096]{1,0:T(8,128)(2,1)S(1)}, bf16[128,4096]{1,0:T(8,128)(2,1)}, u32[]{:S(2)}, u32[]{:S(2)}) collective-permute-start(bf16[128,4096]{1,0:T(8,128)(2,1)S(1)} %shard_map.128.rows_ref.rest_0_.rest_1_), channel_id=1, source_target_pairs={{0,2},{1,3},{2,0},{3,1},{4,6},{5,7},{6,4},{7,5},{8,10},{9,11},{10,... | collective-permute-start | bytes 3145736 | tf_op jit(solution)/shard_map/ppermute | solution.py:412
  8.6 3.4 %collective-permute-start = (bf16[128,4096]{1,0:T(8,128)(2,1)S(1)}, bf16[128,4096]{1,0:T(8,128)(2,1)}, u32[]{:S(2)}, u32[]{:S(2)}) collective-permute-start(bf16[128,4096]{1,0:T(8,128)(2,1)S(1)} %shard_map.128.rows_ref.rest_0_.rest_1_), channel_id=1, source_target_pairs={{0,4},{1,5},{2,6},{3,7},{4,0},{5,1},{6,2},{7,3},{8,12},{9,13},{10,... | collective-permute-start | bytes 3145736 | tf_op jit(solution)/shard_map/ppermute | solution.py:412
  12.0 2.1 %collective-permute-done.3.other_stored_ref = bf16[16,80,768]{2,1,0:T(8,128)(2,1)} collective-permute-done((bf16[16,80,768]{2,1,0:T(8,128)(2,1)}, bf16[16,80,768]{2,1,0:T(8,128)(2,1)}, u32[]{:S(2)}, u32[]{:S(2)}) %collective-permute-start.3) | collective-permute-done | bytes 1966112 | tf_op jit(solution)/shard_map/ppermute | solution.py:412
  15.1 1.4 shard_map.129
  17.3 7.3 %all-to-all-start = ((bf16[16,80,128]{2,1,0:T(8,128)(2,1)}), bf16[16,80,128]{2,1,0:T(8,128)(2,1)S(1)}, u32[]{:S(2)}, u32[]{:S(2)}) async-start(bf16[16,80,128]{2,1,0:T(8,128)(2,1)} %copy-done.2), calls=%async_computation | async-start | bytes 655360 | tf_op jit(solution)/shard_map/all_to_all | solution.py:509
  24.6 7.9 %collective-permute-done.1.rest_2_.rest_3_ = bf16[128,4096]{1,0:T(8,128)(2,1)} collective-permute-done((bf16[128,4096]{1,0:T(8,128)(2,1)S(1)}, bf16[128,4096]{1,0:T(8,128)(2,1)}, u32[]{:S(2)}, u32[]{:S(2)}) %collective-permute-start.1) | collective-permute-done | bytes 1048608 | tf_op jit(solution)/shard_map/ppermute | solution.py:412
  32.5 6.3 %collective-permute-done.rest_0_.rest_1_ = bf16[128,4096]{1,0:T(8,128)(2,1)} collective-permute-done((bf16[128,4096]{1,0:T(8,128)(2,1)S(1)}, bf16[128,4096]{1,0:T(8,128)(2,1)}, u32[]{:S(2)}, u32[]{:S(2)}) %collective-permute-start) | collective-permute-done | bytes 1048608 | tf_op jit(solution)/shard_map/ppermute | solution.py:412
  38.9 2.3 %all-to-all-done.got_ref = bf16[16,80,128]{2,1,0:T(8,128)(2,1)S(1)} async-done(((bf16[16,80,128]{2,1,0:T(8,128)(2,1)}), bf16[16,80,128]{2,1,0:T(8,128)(2,1)S(1)}, u32[]{:S(2)}, u32[]{:S(2)}) %all-to-all-start) | async-done | bytes 327712 | tf_op jit(solution)/shard_map/all_to_all | solution.py:509
  41.2 1.6 %collective-permute-start.6 = (bf16[128,4096]{1,0:T(8,128)(2,1)}, bf16[128,4096]{1,0:T(8,128)(2,1)}, u32[]{:S(2)}, u32[]{:S(2)}) collective-permute-start(bf16[128,4096]{1,0:T(8,128)(2,1)} %collective-permute-done.rest_0_.rest_1_), channel_id=1, source_target_pairs={{4,8},{5,9},{6,10},{7,11},{8,4},{9,5},{10,6},{11,7},{20,24},{21,25... | collective-permute-start | bytes 3145736 | tf_op jit(solution)/shard_map/ppermute | solution.py:412
  42.8 3.3 %broadcast_select_fusion.1 = (bf16[128,4096]{1,0:T(8,128)(2,1)}, bf16[128,4096]{1,0:T(8,128)(2,1)}) fusion(bf16[128,4096]{1,0:T(8,128)(2,1)} %collective-permute-done.rest_0_.rest_1_, bf16[128,4096]{1,0:T(8,128)(2,1)} %collective-permute-done.2.rest_1_, pred[]{:T(512)S(6)} %eq.13, bf16[128,4096]{1,0:T(8,128)(2,1)} %collective-permute-done.1.rest_2_.rest_3_), kind=kLoop, calls=%fused_computation.1 | loop fusion | flops 1048576 | bytes 5242881 | tf_op jit(solution)/shard_map/jit(_where)/select_n | solution.py:451
  46.2 2.0 %collective-permute-start.5 = (bf16[128,4096]{1,0:T(8,128)(2,1)}, bf16[128,4096]{1,0:T(8,128)(2,1)}, u32[]{:S(2)}, u32[]{:S(2)}) collective-permute-start(bf16[128,4096]{1,0:T(8,128)(2,1)} %get-tuple-element.86), channel_id=1, source_target_pairs={{0,4},{1,5},{2,6},{3,7},{4,0},{5,1},{6,2},{7,3},{8,12},{9,13},{10,... | collective-permute-start | bytes 3145736 | tf_op jit(solution)/shard_map/ppermute | solution.py:412
  48.2 3.9 %shard_map.130 = f32[16,80,128]{2,1,0:T(8,128)S(1)} custom-call(s32[1]{0:T(128)} %bitcast.own_ref, bf16[16,80,128]{2,1,0:T(8,128)(2,1)S(1)} %all-to-all-done.got_ref, bf16[16,80,768]{2,1,0:T(8,128)(2,1)S(1)} %bitcast.24, bf16[32,768]{1,0:T(8,128)(2,1)S(1)} %bitcast.27, f32[16]{0:T(128)S(1)} %copy-done.9, s32[8,128]{1,0:T(8,128)S(1)} %bitcast.33, ...), custom_call_target="tpu_custom_call" | custom-call | flops 1000000 | bytes 10000 | tf_op jit(solution)/shard_map/pallas_call | solution.py:514
  52.2 1.6 %collective-permute-done.8 = f32[8,80,128]{2,1,0:T(8,128)S(1)} collective-permute-done((f32[8,80,128]{2,1,0:T(8,128)S(1)}, f32[8,80,128]{2,1,0:T(8,128)S(1)}, u32[]{:S(2)}, u32[]{:S(2)}) %collective-permute-start.8) | collective-permute-done | bytes 327712 | tf_op jit(solution)/shard_map/ppermute | solution.py:412
  54.6 4.1 %all-to-all-start.1 = ((bf16[8,80,128]{2,1,0:T(8,128)(2,1)}), bf16[8,80,128]{2,1,0:T(8,128)(2,1)}, u32[]{:S(2)}, u32[]{:S(2)}) async-start(bf16[8,80,128]{2,1,0:T(8,128)(2,1)} %fusion), calls=%async_computation.1 | async-start | bytes 327680 | tf_op jit(solution)/shard_map/all_to_all | solution.py:524
  58.7 9.5 %shard_map.131 = (bf16[16,80,768]{2,1,0:T(8,128)(2,1)}, bf16[5,80,768]{2,1,0:T(8,128)(2,1)S(1)}, f32[8,8,128]{2,1,0:T(8,128)}, f32[8,128]{1,0:T(8,128)S(1)}) custom-call(s32[3]{0:T(128)S(1)} %pad_add_fusion.2.place_ref, f32[16]{0:T(128)S(1)} %copy-done.9, bf16[1,768,4096]{2,1,0:T(8,128)(2,1)} %weight_ref.7, ...), custom_call_target="tpu_custom_call" | custom-call | flops 1000000 | bytes 10000 | tf_op jit(solution)/shard_map/pallas_call | solution.py:322
  69.1 7.1 %all-to-all-done.1 = bf16[8,80,128]{2,1,0:T(8,128)(2,1)} async-done(((bf16[8,80,128]{2,1,0:T(8,128)(2,1)}), bf16[8,80,128]{2,1,0:T(8,128)(2,1)}, u32[]{:S(2)}, u32[]{:S(2)}) %all-to-all-start.1) | async-done | bytes 163872 | tf_op jit(solution)/shard_map/all_to_all | solution.py:524
  76.2 2.4 %broadcast_select_fusion = bf16[128,4096]{1,0:T(8,128)(2,1)} fusion(bf16[128,4096]{1,0:T(8,128)(2,1)} %collective-permute-done.5.rest_4_.rest_7_, bf16[128,4096]{1,0:T(8,128)(2,1)} %collective-permute-done.6.rest_5_, pred[]{:T(512)S(6)} %eq.13), kind=kLoop, calls=%fused_computation | loop fusion | flops 524288 | bytes 3145729 | tf_op jit(solution)/shard_map/jit(_where)/select_n | solution.py:451
  78.7 1.3 collective-permute-start.9
  81.6 5.4 %all-to-all-start.2 = ((bf16[8,80,128]{2,1,0:T(8,128)(2,1)}), bf16[8,80,128]{2,1,0:T(8,128)(2,1)}, u32[]{:S(2)}, u32[]{:S(2)}) async-start(bf16[8,80,128]{2,1,0:T(8,128)(2,1)} %broadcast_in_dim.4), calls=%async_computation.2 | async-start | bytes 327680 | tf_op jit(solution)/shard_map/all_to_all | solution.py:524
  87.1 16.5 %shard_map.132 = (bf16[16,80,768]{2,1,0:T(8,128)(2,1)}, bf16[5,80,768]{2,1,0:T(8,128)(2,1)S(1)}, f32[8,8,128]{2,1,0:T(8,128)}, f32[8,128]{1,0:T(8,128)S(1)}) custom-call(s32[6]{0:T(128)S(1)} %stack.52.place_ref, f32[16]{0:T(128)S(1)} %copy-done.9, bf16[1,768,4096]{2,1,0:T(8,128)(2,1)} %weight_ref.7, ...), custom_call_target="tpu_custom_call", output_to_operand_aliasing={{0}: (17, {}), {1}: (18, {}), {2}: (19, {})} | custom-call | flops 1000000 | bytes 10000 | tf_op jit(solution)/shard_map/pallas_call | solution.py:322
  104.4 3.5 %all-to-all-done.2 = bf16[8,80,128]{2,1,0:T(8,128)(2,1)} async-done(((bf16[8,80,128]{2,1,0:T(8,128)(2,1)}), bf16[8,80,128]{2,1,0:T(8,128)(2,1)}, u32[]{:S(2)}, u32[]{:S(2)}) %all-to-all-start.2) | async-done | bytes 163872 | tf_op jit(solution)/shard_map/all_to_all | solution.py:524
  109.6 1.3 collective-permute-start.12
  110.9 2.3 %collective-permute-start.11 = (bf16[64,4096]{1,0:T(8,128)(2,1)}, bf16[64,4096]{1,0:T(8,128)(2,1)}, u32[]{:S(2)}, u32[]{:S(2)}) collective-permute-start(bf16[64,4096]{1,0:T(8,128)(2,1)} %slice.17), channel_id=1, source_target_pairs={{0,2},{1,3},{2,0},{3,1},{12,14},{13,15},{14,12},{15,13},{16,18},{1... | collective-permute-start | bytes 1572872 | tf_op jit(solution)/shard_map/ppermute | solution.py:412
  113.3 10.0 %shard_map.133 = (bf16[16,80,768]{2,1,0:T(8,128)(2,1)}, bf16[2,80,768]{2,1,0:T(8,128)(2,1)S(1)}, f32[8,8,128]{2,1,0:T(8,128)}, f32[8,128]{1,0:T(8,128)S(1)}) custom-call(s32[4]{0:T(128)S(1)} %pad_add_fusion.3.place_ref, f32[16]{0:T(128)S(1)} %copy-done.9, bf16[1,768,4096]{2,1,0:T(8,128)(2,1)} %weight_ref.7, ...), custom_call_target="tpu_custom_call", output_to_operand_aliasing={{0}: (13, {}), {2}: (14, {})} | custom-call | flops 1000000 | bytes 10000 | tf_op jit(solution)/shard_map/pallas_call | solution.py:322
  123.6 2.5 %collective-permute-done.12.rest_1_ = bf16[64,4096]{1,0:T(8,128)(2,1)} collective-permute-done((bf16[64,4096]{1,0:T(8,128)(2,1)}, bf16[64,4096]{1,0:T(8,128)(2,1)}, u32[]{:S(2)}, u32[]{:S(2)}) %collective-permute-start.12) | collective-permute-done | bytes 524320 | tf_op jit(solution)/shard_map/ppermute | solution.py:412
  126.1 1.3 collective-permute-done.11.rest_0_
  127.4 8.8 %shard_map.134 = (bf16[16,80,768]{2,1,0:T(8,128)(2,1)}, bf16[1,80,768]{2,1,0:T(8,128)(2,1)S(1)}, f32[8,8,128]{2,1,0:T(8,128)}, f32[8,128]{1,0:T(8,128)S(1)}) custom-call(s32[3]{0:T(128)S(1)} %pad_add_fusion.place_ref, f32[16]{0:T(128)S(1)} %copy-done.9, bf16[1,768,4096]{2,1,0:T(8,128)(2,1)} %weight_ref.7, ...), custom_call_target="tpu_custom_call", output_to_operand_aliasing={{0}: (12, {}), {2}: (13, {})} | custom-call | flops 1000000 | bytes 10000 | tf_op jit(solution)/shard_map/pallas_call | solution.py:322
  136.2 4.6 %all-to-all-start.3 = ((f32[8,8,128]{2,1,0:T(8,128)}), f32[8,8,128]{2,1,0:T(8,128)S(1)}, u32[]{:S(2)}, u32[]{:S(2)}) async-start(f32[8,8,128]{2,1,0:T(8,128)} %get-tuple-element.72), calls=%async_computation.3 | async-start | bytes 65536 | tf_op jit(solution)/shard_map/all_to_all | solution.py:524
  144.6 2.9 %all-to-all-done.3.dots_ref = f32[8,8,128]{2,1,0:T(8,128)S(1)} async-done(((f32[8,8,128]{2,1,0:T(8,128)}), f32[8,8,128]{2,1,0:T(8,128)S(1)}, u32[]{:S(2)}, u32[]{:S(2)}) %all-to-all-start.3) | async-done | bytes 32800 | tf_op jit(solution)/shard_map/all_to_all | solution.py:524
  147.5 1.3 shard_map.136
  (58 shorter events, 14.1 us)
Async XLA Ops:
  0.6 13.5 %copy-start = (bf16[1,16,80,768]{3,2,1,0:T(8,128)(2,1)S(1)}, bf16[1,16,80,768]{3,2,1,0:T(8,128)(2,1)}, u32[]{:S(2)}) copy-start(bf16[1,16,80,768]{3,2,1,0:T(8,128)(2,1)} %param.13) | copy-start | bytes 5898244
  0.6 13.5 %copy-start.1 = (bf16[768,32]{0,1:T(8,128)(2,1)S(1)}, bf16[768,32]{0,1:T(8,128)(2,1)}, u32[]{:S(2)}) copy-start(bf16[768,32]{0,1:T(8,128)(2,1)} %param.15) | copy-start | bytes 147460
  0.7 40.5 %collective-permute-start.4 = (bf16[1,768,4096]{2,1,0:T(8,128)(2,1)}, bf16[1,768,4096]{2,1,0:T(8,128)(2,1)}, u32[]{:S(2)}, u32[]{:S(2)}) collective-permute-start(bf16[1,768,4096]{2,1,0:T(8,128)(2,1)} %weight_ref.7), channel_id=1, source_target_pairs={{0,1},{1,0},{2,3},{3,2},{4,5},{5,4},{6,7},{7,6},{8,9},{9,8},{10,11... | collective-permute-start | bytes 18874376 | tf_op jit(solution)/shard_map/ppermute | solution.py:412
  1.2 12.9 %collective-permute-start.3 = (bf16[16,80,768]{2,1,0:T(8,128)(2,1)}, bf16[16,80,768]{2,1,0:T(8,128)(2,1)}, u32[]{:S(2)}, u32[]{:S(2)}) collective-permute-start(bf16[16,80,768]{2,1,0:T(8,128)(2,1)} %bitcast.19), channel_id=1, source_target_pairs={{0,1},{1,0},{2,3},{3,2},{4,5},{5,4},{6,7},{7,6},{8,9},{9,8},{10,11... | collective-permute-start | bytes 5898248 | tf_op jit(solution)/shard_map/ppermute | solution.py:412
  1.3 1.2 copy-start.3
  3.2 10.9 %copy-start.8 = (s32[128,8]{0,1:T(8,128)S(1)}, s32[128,8]{0,1:T(8,128)}, u32[]{:S(2)}) copy-start(s32[128,8]{0,1:T(8,128)} %param.11) | copy-start | bytes 12292
  3.2 10.9 %copy-start.9 = (f32[16]{0:T(128)S(1)}, f32[16]{0:T(128)}, u32[]{:S(2)}) copy-start(f32[16]{0:T(128)} %gate_ref.11) | copy-start | bytes 196
  3.2 10.9 %copy-start.11 = (bf16[128,8]{0,1:T(8,128)(2,1)S(1)}, bf16[128,8]{0,1:T(8,128)(2,1)}, u32[]{:S(2)}) copy-start(bf16[128,8]{0,1:T(8,128)(2,1)} %param.12) | copy-start | bytes 6148
  4.0 20.6 %collective-permute-start.2 = (bf16[128,4096]{1,0:T(8,128)(2,1)S(1)}, bf16[128,4096]{1,0:T(8,128)(2,1)}, u32[]{:S(2)}, u32[]{:S(2)}) collective-permute-start(bf16[128,4096]{1,0:T(8,128)(2,1)S(1)} %shard_map.128.rows_ref.rest_0_.rest_1_), channel_id=1, source_target_pairs={{4,8},{5,9},{6,10},{7,11},{8,4},{9,5},{10,6},{11,7},{20,24},{21,25... | collective-permute-start | bytes 3145736 | tf_op jit(solution)/shard_map/ppermute | solution.py:412
  5.7 26.9 %collective-permute-start.1 = (bf16[128,4096]{1,0:T(8,128)(2,1)S(1)}, bf16[128,4096]{1,0:T(8,128)(2,1)}, u32[]{:S(2)}, u32[]{:S(2)}) collective-permute-start(bf16[128,4096]{1,0:T(8,128)(2,1)S(1)} %shard_map.128.rows_ref.rest_0_.rest_1_), channel_id=1, source_target_pairs={{0,2},{1,3},{2,0},{3,1},{4,6},{5,7},{6,4},{7,5},{8,10},{9,11},{10,... | collective-permute-start | bytes 3145736 | tf_op jit(solution)/shard_map/ppermute | solution.py:412
  8.6 30.3 %collective-permute-start = (bf16[128,4096]{1,0:T(8,128)(2,1)S(1)}, bf16[128,4096]{1,0:T(8,128)(2,1)}, u32[]{:S(2)}, u32[]{:S(2)}) collective-permute-start(bf16[128,4096]{1,0:T(8,128)(2,1)S(1)} %shard_map.128.rows_ref.rest_0_.rest_1_), channel_id=1, source_target_pairs={{0,4},{1,5},{2,6},{3,7},{4,0},{5,1},{6,2},{7,3},{8,12},{9,13},{10,... | collective-permute-start | bytes 3145736 | tf_op jit(solution)/shard_map/ppermute | solution.py:412
  14.1 1.0 copy-start.7
  16.5 0.7 copy-start.2
  17.3 23.9 %all-to-all-start = ((bf16[16,80,128]{2,1,0:T(8,128)(2,1)}), bf16[16,80,128]{2,1,0:T(8,128)(2,1)S(1)}, u32[]{:S(2)}, u32[]{:S(2)}) async-start(bf16[16,80,128]{2,1,0:T(8,128)(2,1)} %copy-done.2), calls=%async_computation | async-start | bytes 655360 | tf_op jit(solution)/shard_map/all_to_all | solution.py:509
  41.2 35.0 %collective-permute-start.6 = (bf16[128,4096]{1,0:T(8,128)(2,1)}, bf16[128,4096]{1,0:T(8,128)(2,1)}, u32[]{:S(2)}, u32[]{:S(2)}) collective-permute-start(bf16[128,4096]{1,0:T(8,128)(2,1)} %collective-permute-done.rest_0_.rest_1_), channel_id=1, source_target_pairs={{4,8},{5,9},{6,10},{7,11},{8,4},{9,5},{10,6},{11,7},{20,24},{21,25... | collective-permute-start | bytes 3145736 | tf_op jit(solution)/shard_map/ppermute | solution.py:412
  46.2 30.0 %collective-permute-start.7 = (bf16[128,4096]{1,0:T(8,128)(2,1)}, bf16[128,4096]{1,0:T(8,128)(2,1)}, u32[]{:S(2)}, u32[]{:S(2)}) collective-permute-start(bf16[128,4096]{1,0:T(8,128)(2,1)} %get-tuple-element.85), channel_id=1, source_target_pairs={{0,2},{1,3},{2,0},{3,1},{4,6},{5,7},{6,4},{7,5},{8,10},{9,11},{10,... | collective-permute-start | bytes 3145736 | tf_op jit(solution)/shard_map/ppermute | solution.py:412
  46.2 30.0 %collective-permute-start.5 = (bf16[128,4096]{1,0:T(8,128)(2,1)}, bf16[128,4096]{1,0:T(8,128)(2,1)}, u32[]{:S(2)}, u32[]{:S(2)}) collective-permute-start(bf16[128,4096]{1,0:T(8,128)(2,1)} %get-tuple-element.86), channel_id=1, source_target_pairs={{0,4},{1,5},{2,6},{3,7},{4,0},{5,1},{6,2},{7,3},{8,12},{9,13},{10,... | collective-permute-start | bytes 3145736 | tf_op jit(solution)/shard_map/ppermute | solution.py:412
  52.2 1.7 %collective-permute-start.8 = (f32[8,80,128]{2,1,0:T(8,128)S(1)}, f32[8,80,128]{2,1,0:T(8,128)S(1)}, u32[]{:S(2)}, u32[]{:S(2)}) collective-permute-start(f32[8,80,128]{2,1,0:T(8,128)S(1)} %slice.21), channel_id=1, source_target_pairs={{0,1},{1,0},{2,3},{3,2},{4,5},{5,4},{6,7},{7,6},{8,9},{9,8},{10,11... | collective-permute-start | bytes 983048 | tf_op jit(solution)/shard_map/ppermute | solution.py:412
  54.6 21.6 %all-to-all-start.1 = ((bf16[8,80,128]{2,1,0:T(8,128)(2,1)}), bf16[8,80,128]{2,1,0:T(8,128)(2,1)}, u32[]{:S(2)}, u32[]{:S(2)}) async-start(bf16[8,80,128]{2,1,0:T(8,128)(2,1)} %fusion), calls=%async_computation.1 | async-start | bytes 327680 | tf_op jit(solution)/shard_map/all_to_all | solution.py:524
  68.2 0.8 copy-start.4
  76.1 11.0 %copy-start.5 = (bf16[5,80,768]{2,1,0:T(8,128)(2,1)S(1)}, bf16[5,80,768]{2,1,0:T(8,128)(2,1)}, u32[]{:S(2)}) copy-start(bf16[5,80,768]{2,1,0:T(8,128)(2,1)} %copy-done.4) | copy-start | bytes 1843204
  78.6 29.3 %collective-permute-start.10 = (bf16[128,4096]{1,0:T(8,128)(2,1)}, bf16[128,4096]{1,0:T(8,128)(2,1)S(1)}, u32[]{:S(2)}, u32[]{:S(2)}) collective-permute-start(bf16[128,4096]{1,0:T(8,128)(2,1)} %broadcast_select_fusion), channel_id=1, source_target_pairs={{0,2},{1,3},{2,0},{3,1},{4,6},{5,7},{6,4},{7,5},{8,10},{9,11},{10,... | collective-permute-start | bytes 3145736 | tf_op jit(solution)/shard_map/ppermute | solution.py:412
  78.7 29.2 %collective-permute-start.9 = (bf16[128,4096]{1,0:T(8,128)(2,1)}, bf16[128,4096]{1,0:T(8,128)(2,1)S(1)}, u32[]{:S(2)}, u32[]{:S(2)}) collective-permute-start(bf16[128,4096]{1,0:T(8,128)(2,1)} %collective-permute-done.6.rest_5_), channel_id=1, source_target_pairs={{4,0},{5,1},{6,2},{7,3},{8,12},{9,13},{10,14},{11,15},{20,16},{21,... | collective-permute-start | bytes 3145736 | tf_op jit(solution)/shard_map/ppermute | solution.py:412
  81.6 26.3 %all-to-all-start.2 = ((bf16[8,80,128]{2,1,0:T(8,128)(2,1)}), bf16[8,80,128]{2,1,0:T(8,128)(2,1)}, u32[]{:S(2)}, u32[]{:S(2)}) async-start(bf16[8,80,128]{2,1,0:T(8,128)(2,1)} %broadcast_in_dim.4), calls=%async_computation.2 | async-start | bytes 327680 | tf_op jit(solution)/shard_map/all_to_all | solution.py:524
  103.6 0.8 copy-start.6
  107.9 5.4 %collective-permute-start.13 = (bf16[5,80,768]{2,1,0:T(8,128)(2,1)}, bf16[5,80,768]{2,1,0:T(8,128)(2,1)S(1)}, u32[]{:S(2)}, u32[]{:S(2)}) collective-permute-start(bf16[5,80,768]{2,1,0:T(8,128)(2,1)} %copy-done.6), channel_id=1, source_target_pairs={{0,1},{1,0},{2,3},{3,2},{4,5},{5,4},{6,7},{7,6},{8,9},{9,8},{10,11... | collective-permute-start | bytes 1843208 | tf_op jit(solution)/shard_map/ppermute | solution.py:412
  109.6 16.5 %collective-permute-start.12 = (bf16[64,4096]{1,0:T(8,128)(2,1)}, bf16[64,4096]{1,0:T(8,128)(2,1)}, u32[]{:S(2)}, u32[]{:S(2)}) collective-permute-start(bf16[64,4096]{1,0:T(8,128)(2,1)} %slice.18), channel_id=1, source_target_pairs={{4,0},{5,1},{6,2},{7,3},{8,12},{9,13},{10,14},{11,15},{20,16},{21,... | collective-permute-start | bytes 1572872 | tf_op jit(solution)/shard_map/ppermute | solution.py:412
  110.9 16.5 %collective-permute-start.11 = (bf16[64,4096]{1,0:T(8,128)(2,1)}, bf16[64,4096]{1,0:T(8,128)(2,1)}, u32[]{:S(2)}, u32[]{:S(2)}) collective-permute-start(bf16[64,4096]{1,0:T(8,128)(2,1)} %slice.17), channel_id=1, source_target_pairs={{0,2},{1,3},{2,0},{3,1},{12,14},{13,15},{14,12},{15,13},{16,18},{1... | collective-permute-start | bytes 1572872 | tf_op jit(solution)/shard_map/ppermute | solution.py:412
  123.3 18.0 %collective-permute-start.16 = (bf16[8,80,128]{2,1,0:T(8,128)(2,1)}, bf16[8,80,128]{2,1,0:T(8,128)(2,1)S(1)}, u32[]{:S(2)}, u32[]{:S(2)}) collective-permute-start(bf16[8,80,128]{2,1,0:T(8,128)(2,1)} %all-to-all-done.2), channel_id=1, source_target_pairs={{0,1},{1,0},{2,3},{3,2},{4,5},{5,4},{6,7},{7,6},{8,9},{9,8},{10,11... | collective-permute-start | bytes 491528 | tf_op jit(solution)/shard_map/ppermute | solution.py:412
  136.2 11.3 %all-to-all-start.3 = ((f32[8,8,128]{2,1,0:T(8,128)}), f32[8,8,128]{2,1,0:T(8,128)S(1)}, u32[]{:S(2)}, u32[]{:S(2)}) async-start(f32[8,8,128]{2,1,0:T(8,128)} %get-tuple-element.72), calls=%async_computation.3 | async-start | bytes 65536 | tf_op jit(solution)/shard_map/all_to_all | solution.py:524
  140.8 6.7 %collective-permute-start.14 = (bf16[1,80,768]{2,1,0:T(8,128)(2,1)S(1)}, bf16[1,80,768]{2,1,0:T(8,128)(2,1)S(1)}, u32[]{:S(2)}, u32[]{:S(2)}) collective-permute-start(bf16[1,80,768]{2,1,0:T(8,128)(2,1)S(1)} %get-tuple-element.73), channel_id=1, source_target_pairs={{0,1},{1,0},{2,3},{3,2},{4,5},{5,4},{6,7},{7,6},{8,9},{9,8},{10,11... | collective-permute-start | bytes 368648 | tf_op jit(solution)/shard_map/ppermute | solution.py:412
  140.8 2.8 %collective-permute-start.15 = (bf16[2,80,768]{2,1,0:T(8,128)(2,1)S(1)}, bf16[2,80,768]{2,1,0:T(8,128)(2,1)S(1)}, u32[]{:S(2)}, u32[]{:S(2)}) collective-permute-start(bf16[2,80,768]{2,1,0:T(8,128)(2,1)S(1)} %get-tuple-element.74), channel_id=1, source_target_pairs={{0,1},{1,0},{2,3},{3,2},{4,5},{5,4},{6,7},{7,6},{8,9},{9,8},{10,11... | collective-permute-start | bytes 737288 | tf_op jit(solution)/shard_map/ppermute | solution.py:412
  (1 other events, 0.7 us)

commit v6 on v5

--- a/solution.py
+++ b/solution.py
@@ -9,7 +9,7 @@
 
 F32, BF16 = jnp.float32, jnp.bfloat16
 VMEM_LIMIT = 16 * 1024 * 1024
-BIG_LIMIT = 50 * 1024 * 1024
+BIG_LIMIT = 48 * 1024 * 1024
 TILE, AHEAD = 384, 2
 ROWS = (((0,), (0,)), ((), ()))
 LANES = (((1,), (1,)), ((), ()))

time: 149 us -> 151 us (1.013)
  waiting for transfers between devices: 37.6 us -> 34.8 us
  Pallas kernels: 54 us -> 55.9 us
  local copies, waits for them, and re-layouts: 8.27 us -> 10 us
    all_to_all x3, waiting for transfers between devices: 13.4 us -> 11.4 us  [small_body(): lax.all_to_all(value, 'ex', split_axis=0, concat_axis=0, axis_index_group...]
    unnamed x24 -> x30, local copies, waits for them, and re-layouts: 5.28 us -> 5.99 us
  transfers between devices with their start and end apart: 21 -> 21, of which waited for: 10 -> 10; matrix products, arithmetic and copies ran while one was open for 6% -> 7% of each run, Pallas kernels for 35% -> 36%
where the time goes in v6:
time: 151 us
  Pallas kernels  55.9 us (37%)
  starting transfers between devices  40.3 us (27%)
  waiting for transfers between devices  34.8 us (23%)
  local copies, waits for them, and re-layouts  10 us (7%)
  other arithmetic  8.63 us (6%)
    pallas_call x4, Pallas kernels, expert_call(): pl.pallas_call(functools.partial(expert_kernel, layout=layout, slot=slot)...  45.6 us
    ppermute x17, waiting for transfers between devices, send(): return lax.ppermute(value, 'ex', pairs)  21.1 us
    ppermute x17, starting transfers between devices, send(): return lax.ppermute(value, 'ex', pairs)  18.1 us
    all_to_all x3, starting transfers between devices, small_body(): lax.all_to_all(value, 'ex', split_axis=0, concat_axis=0, axis_index_group...  15 us
    all_to_all x3, waiting for transfers between devices, small_body(): lax.all_to_all(value, 'ex', split_axis=0, concat_axis=0, axis_index_group...  11.4 us
    all_to_all x1, starting transfers between devices, small_body(): got = lax.all_to_all(packed, 'ex', split_axis=0, concat_axis=0, tiled=True)  7.28 us
    unnamed x30, local copies, waits for them, and re-layouts  5.99 us
    select_n x2, other arithmetic, small_body(): pick = lambda as_end, as_mid: jnp.where(is_end == 1, as_end, as_mid)  5.72 us
  transfers between devices with their start and end apart: 21, of which 10 were waited for; matrix products, arithmetic and copies ran while one was open for 7% of the time, Pallas kernels for 36%

profile of v6, /device:TPU:0, one launch (start us, length us, event | category | flops | bytes accessed | tf_op | source)
XLA Modules:
  0.0 150.6 jit_solution(13848125984464060930)
XLA Ops:
  4.0 1.7 %collective-permute-start.2 = (bf16[128,4096]{1,0:T(8,128)(2,1)S(1)}, bf16[128,4096]{1,0:T(8,128)(2,1)}, u32[]{:S(2)}, u32[]{:S(2)}) collective-permute-start(bf16[128,4096]{1,0:T(8,128)(2,1)S(1)} %shard_map.128.rows_ref.rest_0_.rest_1_), channel_id=1, source_target_pairs={{4,8},{5,9},{6,10},{7,11},{8,4},{9,5},{10,6},{11,7},{20,24},{21,25... | collective-permute-start | bytes 3145736 | tf_op jit(solution)/shard_map/ppermute | solution.py:412
  5.6 2.9 %collective-permute-start.1 = (bf16[128,4096]{1,0:T(8,128)(2,1)S(1)}, bf16[128,4096]{1,0:T(8,128)(2,1)}, u32[]{:S(2)}, u32[]{:S(2)}) collective-permute-start(bf16[128,4096]{1,0:T(8,128)(2,1)S(1)} %shard_map.128.rows_ref.rest_0_.rest_1_), channel_id=1, source_target_pairs={{0,2},{1,3},{2,0},{3,1},{4,6},{5,7},{6,4},{7,5},{8,10},{9,11},{10,... | collective-permute-start | bytes 3145736 | tf_op jit(solution)/shard_map/ppermute | solution.py:412
  8.6 3.5 %collective-permute-start = (bf16[128,4096]{1,0:T(8,128)(2,1)S(1)}, bf16[128,4096]{1,0:T(8,128)(2,1)}, u32[]{:S(2)}, u32[]{:S(2)}) collective-permute-start(bf16[128,4096]{1,0:T(8,128)(2,1)S(1)} %shard_map.128.rows_ref.rest_0_.rest_1_), channel_id=1, source_target_pairs={{0,4},{1,5},{2,6},{3,7},{4,0},{5,1},{6,2},{7,3},{8,12},{9,13},{10,... | collective-permute-start | bytes 3145736 | tf_op jit(solution)/shard_map/ppermute | solution.py:412
  12.0 2.1 %collective-permute-done.3.other_stored_ref = bf16[16,80,768]{2,1,0:T(8,128)(2,1)} collective-permute-done((bf16[16,80,768]{2,1,0:T(8,128)(2,1)}, bf16[16,80,768]{2,1,0:T(8,128)(2,1)}, u32[]{:S(2)}, u32[]{:S(2)}) %collective-permute-start.3) | collective-permute-done | bytes 1966112 | tf_op jit(solution)/shard_map/ppermute | solution.py:412
  15.1 1.4 shard_map.129
  17.3 7.3 %all-to-all-start = ((bf16[16,80,128]{2,1,0:T(8,128)(2,1)}), bf16[16,80,128]{2,1,0:T(8,128)(2,1)S(1)}, u32[]{:S(2)}, u32[]{:S(2)}) async-start(bf16[16,80,128]{2,1,0:T(8,128)(2,1)} %copy-done.3), calls=%async_computation | async-start | bytes 655360 | tf_op jit(solution)/shard_map/all_to_all | solution.py:509
  24.6 7.9 %collective-permute-done.1.rest_2_.rest_3_ = bf16[128,4096]{1,0:T(8,128)(2,1)} collective-permute-done((bf16[128,4096]{1,0:T(8,128)(2,1)S(1)}, bf16[128,4096]{1,0:T(8,128)(2,1)}, u32[]{:S(2)}, u32[]{:S(2)}) %collective-permute-start.1) | collective-permute-done | bytes 1048608 | tf_op jit(solution)/shard_map/ppermute | solution.py:412
  32.5 6.4 %collective-permute-done.rest_0_.rest_1_ = bf16[128,4096]{1,0:T(8,128)(2,1)} collective-permute-done((bf16[128,4096]{1,0:T(8,128)(2,1)S(1)}, bf16[128,4096]{1,0:T(8,128)(2,1)}, u32[]{:S(2)}, u32[]{:S(2)}) %collective-permute-start) | collective-permute-done | bytes 1048608 | tf_op jit(solution)/shard_map/ppermute | solution.py:412
  38.9 2.3 %all-to-all-done.got_ref = bf16[16,80,128]{2,1,0:T(8,128)(2,1)S(1)} async-done(((bf16[16,80,128]{2,1,0:T(8,128)(2,1)}), bf16[16,80,128]{2,1,0:T(8,128)(2,1)S(1)}, u32[]{:S(2)}, u32[]{:S(2)}) %all-to-all-start) | async-done | bytes 327712 | tf_op jit(solution)/shard_map/all_to_all | solution.py:509
  41.2 1.6 %collective-permute-start.6 = (bf16[128,4096]{1,0:T(8,128)(2,1)}, bf16[128,4096]{1,0:T(8,128)(2,1)}, u32[]{:S(2)}, u32[]{:S(2)}) collective-permute-start(bf16[128,4096]{1,0:T(8,128)(2,1)} %collective-permute-done.rest_0_.rest_1_), channel_id=1, source_target_pairs={{4,8},{5,9},{6,10},{7,11},{8,4},{9,5},{10,6},{11,7},{20,24},{21,25... | collective-permute-start | bytes 3145736 | tf_op jit(solution)/shard_map/ppermute | solution.py:412
  42.8 3.3 %broadcast_select_fusion.1 = (bf16[128,4096]{1,0:T(8,128)(2,1)}, bf16[128,4096]{1,0:T(8,128)(2,1)}) fusion(bf16[128,4096]{1,0:T(8,128)(2,1)} %collective-permute-done.rest_0_.rest_1_, bf16[128,4096]{1,0:T(8,128)(2,1)} %collective-permute-done.2.rest_1_, pred[]{:T(512)S(6)} %eq.13, bf16[128,4096]{1,0:T(8,128)(2,1)} %collective-permute-done.1.rest_2_.rest_3_), kind=kLoop, calls=%fused_computation.1 | loop fusion | flops 1048576 | bytes 5242881 | tf_op jit(solution)/shard_map/jit(_where)/select_n | solution.py:451
  46.2 2.0 %collective-permute-start.5 = (bf16[128,4096]{1,0:T(8,128)(2,1)}, bf16[128,4096]{1,0:T(8,128)(2,1)}, u32[]{:S(2)}, u32[]{:S(2)}) collective-permute-start(bf16[128,4096]{1,0:T(8,128)(2,1)} %get-tuple-element.86), channel_id=1, source_target_pairs={{0,4},{1,5},{2,6},{3,7},{4,0},{5,1},{6,2},{7,3},{8,12},{9,13},{10,... | collective-permute-start | bytes 3145736 | tf_op jit(solution)/shard_map/ppermute | solution.py:412
  48.2 3.9 %shard_map.130 = f32[16,80,128]{2,1,0:T(8,128)S(1)} custom-call(s32[1]{0:T(128)} %bitcast.own_ref, bf16[16,80,128]{2,1,0:T(8,128)(2,1)S(1)} %all-to-all-done.got_ref, bf16[16,80,768]{2,1,0:T(8,128)(2,1)S(1)} %bitcast.22, bf16[32,768]{1,0:T(8,128)(2,1)S(1)} %bitcast.27, f32[16]{0:T(128)S(1)} %copy-done.10, s32[8,128]{1,0:T(8,128)S(1)} %bitcast.33, ...), custom_call_target="tpu_custom_call" | custom-call | flops 1000000 | bytes 10000 | tf_op jit(solution)/shard_map/pallas_call | solution.py:514
  52.2 1.6 %collective-permute-done.8 = f32[8,80,128]{2,1,0:T(8,128)S(1)} collective-permute-done((f32[8,80,128]{2,1,0:T(8,128)S(1)}, f32[8,80,128]{2,1,0:T(8,128)S(1)}, u32[]{:S(2)}, u32[]{:S(2)}) %collective-permute-start.8) | collective-permute-done | bytes 327712 | tf_op jit(solution)/shard_map/ppermute | solution.py:412
  54.6 4.1 %all-to-all-start.1 = ((bf16[8,80,128]{2,1,0:T(8,128)(2,1)}), bf16[8,80,128]{2,1,0:T(8,128)(2,1)}, u32[]{:S(2)}, u32[]{:S(2)}) async-start(bf16[8,80,128]{2,1,0:T(8,128)(2,1)} %fusion), calls=%async_computation.1 | async-start | bytes 327680 | tf_op jit(solution)/shard_map/all_to_all | solution.py:524
  58.7 9.5 %shard_map.131 = (bf16[16,80,768]{2,1,0:T(8,128)(2,1)}, bf16[5,80,768]{2,1,0:T(8,128)(2,1)S(1)}, f32[8,8,128]{2,1,0:T(8,128)}, f32[8,128]{1,0:T(8,128)S(1)}) custom-call(s32[3]{0:T(128)S(1)} %pad_add_fusion.2.place_ref, f32[16]{0:T(128)S(1)} %copy-done.10, bf16[1,768,4096]{2,1,0:T(8,128)(2,1)} %weight_ref.7, ...), custom_call_target="tpu_custom_call" | custom-call | flops 1000000 | bytes 10000 | tf_op jit(solution)/shard_map/pallas_call | solution.py:322
  69.0 7.1 %all-to-all-done.1 = bf16[8,80,128]{2,1,0:T(8,128)(2,1)} async-done(((bf16[8,80,128]{2,1,0:T(8,128)(2,1)}), bf16[8,80,128]{2,1,0:T(8,128)(2,1)}, u32[]{:S(2)}, u32[]{:S(2)}) %all-to-all-start.1) | async-done | bytes 163872 | tf_op jit(solution)/shard_map/all_to_all | solution.py:524
  76.2 2.4 %broadcast_select_fusion = bf16[128,4096]{1,0:T(8,128)(2,1)} fusion(bf16[128,4096]{1,0:T(8,128)(2,1)} %collective-permute-done.5.rest_4_.rest_7_, bf16[128,4096]{1,0:T(8,128)(2,1)} %collective-permute-done.6.rest_5_, pred[]{:T(512)S(6)} %eq.13), kind=kLoop, calls=%fused_computation | loop fusion | flops 524288 | bytes 3145729 | tf_op jit(solution)/shard_map/jit(_where)/select_n | solution.py:451
  78.7 1.3 collective-permute-start.9
  81.6 6.3 %all-to-all-start.2 = ((bf16[8,80,128]{2,1,0:T(8,128)(2,1)}), bf16[8,80,128]{2,1,0:T(8,128)(2,1)}, u32[]{:S(2)}, u32[]{:S(2)}) async-start(bf16[8,80,128]{2,1,0:T(8,128)(2,1)} %broadcast_in_dim.4), calls=%async_computation.2 | async-start | bytes 327680 | tf_op jit(solution)/shard_map/all_to_all | solution.py:524
  88.0 16.5 %shard_map.132 = (bf16[16,80,768]{2,1,0:T(8,128)(2,1)}, bf16[5,80,768]{2,1,0:T(8,128)(2,1)S(1)}, f32[8,8,128]{2,1,0:T(8,128)}, f32[8,128]{1,0:T(8,128)S(1)}) custom-call(s32[6]{0:T(128)S(1)} %stack.52.place_ref, f32[16]{0:T(128)S(1)} %copy-done.10, bf16[1,768,4096]{2,1,0:T(8,128)(2,1)} %weight_ref.7, ...), custom_call_target="tpu_custom_call", output_to_operand_aliasing={{0}: (17, {}), {1}: (18, {}), {2}: (19, {})} | custom-call | flops 1000000 | bytes 10000 | tf_op jit(solution)/shard_map/pallas_call | solution.py:322
  105.3 2.6 %all-to-all-done.2 = bf16[8,80,128]{2,1,0:T(8,128)(2,1)} async-done(((bf16[8,80,128]{2,1,0:T(8,128)(2,1)}), bf16[8,80,128]{2,1,0:T(8,128)(2,1)}, u32[]{:S(2)}, u32[]{:S(2)}) %all-to-all-start.2) | async-done | bytes 163872 | tf_op jit(solution)/shard_map/all_to_all | solution.py:524
  107.9 1.9 %slice.17 = bf16[64,4096]{1,0:T(8,128)(2,1)} slice(bf16[128,4096]{1,0:T(8,128)(2,1)} %collective-permute-done.9.rest_0_), slice={[0:64], [0:4096]} | slice | bytes 1048576 | tf_op jit(solution)/shard_map/slice | solution.py:537
  110.6 1.3 collective-permute-start.12
  111.9 2.3 %collective-permute-start.11 = (bf16[64,4096]{1,0:T(8,128)(2,1)}, bf16[64,4096]{1,0:T(8,128)(2,1)}, u32[]{:S(2)}, u32[]{:S(2)}) collective-permute-start(bf16[64,4096]{1,0:T(8,128)(2,1)} %slice.17), channel_id=1, source_target_pairs={{0,2},{1,3},{2,0},{3,1},{12,14},{13,15},{14,12},{15,13},{16,18},{1... | collective-permute-start | bytes 1572872 | tf_op jit(solution)/shard_map/ppermute | solution.py:412
  114.3 10.0 %shard_map.133 = (bf16[16,80,768]{2,1,0:T(8,128)(2,1)}, bf16[2,80,768]{2,1,0:T(8,128)(2,1)S(1)}, f32[8,8,128]{2,1,0:T(8,128)}, f32[8,128]{1,0:T(8,128)S(1)}) custom-call(s32[4]{0:T(128)S(1)} %pad_add_fusion.3.place_ref, f32[16]{0:T(128)S(1)} %copy-done.10, bf16[1,768,4096]{2,1,0:T(8,128)(2,1)} %weight_ref.7, ...), custom_call_target="tpu_custom_call", output_to_operand_aliasing={{0}: (13, {}), {2}: (14, {})} | custom-call | flops 1000000 | bytes 10000 | tf_op jit(solution)/shard_map/pallas_call | solution.py:322
  125.3 1.8 %collective-permute-done.12.rest_1_ = bf16[64,4096]{1,0:T(8,128)(2,1)} collective-permute-done((bf16[64,4096]{1,0:T(8,128)(2,1)}, bf16[64,4096]{1,0:T(8,128)(2,1)}, u32[]{:S(2)}, u32[]{:S(2)}) %collective-permute-start.12) | collective-permute-done | bytes 524320 | tf_op jit(solution)/shard_map/ppermute | solution.py:412
  127.2 1.3 collective-permute-done.11.rest_0_
  128.5 9.6 %shard_map.134 = (bf16[16,80,768]{2,1,0:T(8,128)(2,1)}, bf16[1,80,768]{2,1,0:T(8,128)(2,1)S(1)}, f32[8,8,128]{2,1,0:T(8,128)}, f32[8,128]{1,0:T(8,128)S(1)}) custom-call(s32[3]{0:T(128)S(1)} %pad_add_fusion.place_ref, f32[16]{0:T(128)S(1)} %copy-done.10, bf16[1,768,4096]{2,1,0:T(8,128)(2,1)} %weight_ref.7, ...), custom_call_target="tpu_custom_call", output_to_operand_aliasing={{0}: (12, {}), {2}: (13, {})} | custom-call | flops 1000000 | bytes 10000 | tf_op jit(solution)/shard_map/pallas_call | solution.py:322
  138.1 4.6 %all-to-all-start.3 = ((f32[8,8,128]{2,1,0:T(8,128)}), f32[8,8,128]{2,1,0:T(8,128)S(1)}, u32[]{:S(2)}, u32[]{:S(2)}) async-start(f32[8,8,128]{2,1,0:T(8,128)} %get-tuple-element.72), calls=%async_computation.3 | async-start | bytes 65536 | tf_op jit(solution)/shard_map/all_to_all | solution.py:524
  145.6 2.0 %shard_map.135._ = bf16[16,80,768]{2,1,0:T(8,128)(2,1)} custom-call(s32[1]{0:T(128)} %bitcast.own_ref, bf16[5,80,768]{2,1,0:T(8,128)(2,1)} %collective-permute-done.13.refs_0_, bf16[2,80,768]{2,1,0:T(8,128)(2,1)S(1)} %collective-permute-done.15.refs_1_, bf16[16,80,768]{2,1,0:T(8,128)(2,1)} %get-tuple-element.75.refs_2_), custom_call_target="tpu_custom_call", output_to_operand_aliasing={{}: (3, {})} | custom-call | flops 1000000 | bytes 10000 | tf_op jit(solution)/shard_map/pallas_call | solution.py:368
  147.6 1.7 %all-to-all-done.3.dots_ref = f32[8,8,128]{2,1,0:T(8,128)S(1)} async-done(((f32[8,8,128]{2,1,0:T(8,128)}), f32[8,8,128]{2,1,0:T(8,128)S(1)}, u32[]{:S(2)}, u32[]{:S(2)}) %all-to-all-start.3) | async-done | bytes 32800 | tf_op jit(solution)/shard_map/all_to_all | solution.py:524
  (64 shorter events, 15.5 us)
Async XLA Ops:
  0.6 13.5 %copy-start = (bf16[1,16,80,768]{3,2,1,0:T(8,128)(2,1)S(1)}, bf16[1,16,80,768]{3,2,1,0:T(8,128)(2,1)}, u32[]{:S(2)}) copy-start(bf16[1,16,80,768]{3,2,1,0:T(8,128)(2,1)} %param.13) | copy-start | bytes 5898244
  0.6 13.5 %copy-start.2 = (bf16[768,32]{0,1:T(8,128)(2,1)S(1)}, bf16[768,32]{0,1:T(8,128)(2,1)}, u32[]{:S(2)}) copy-start(bf16[768,32]{0,1:T(8,128)(2,1)} %param.15) | copy-start | bytes 147460
  0.7 40.5 %collective-permute-start.4 = (bf16[1,768,4096]{2,1,0:T(8,128)(2,1)}, bf16[1,768,4096]{2,1,0:T(8,128)(2,1)}, u32[]{:S(2)}, u32[]{:S(2)}) collective-permute-start(bf16[1,768,4096]{2,1,0:T(8,128)(2,1)} %weight_ref.7), channel_id=1, source_target_pairs={{0,1},{1,0},{2,3},{3,2},{4,5},{5,4},{6,7},{7,6},{8,9},{9,8},{10,11... | collective-permute-start | bytes 18874376 | tf_op jit(solution)/shard_map/ppermute | solution.py:412
  1.2 12.9 %collective-permute-start.3 = (bf16[16,80,768]{2,1,0:T(8,128)(2,1)}, bf16[16,80,768]{2,1,0:T(8,128)(2,1)}, u32[]{:S(2)}, u32[]{:S(2)}) collective-permute-start(bf16[16,80,768]{2,1,0:T(8,128)(2,1)} %bitcast.19), channel_id=1, source_target_pairs={{0,1},{1,0},{2,3},{3,2},{4,5},{5,4},{6,7},{7,6},{8,9},{9,8},{10,11... | collective-permute-start | bytes 5898248 | tf_op jit(solution)/shard_map/ppermute | solution.py:412
  1.3 1.2 copy-start.4
  3.2 10.9 %copy-start.9 = (s32[128,8]{0,1:T(8,128)S(1)}, s32[128,8]{0,1:T(8,128)}, u32[]{:S(2)}) copy-start(s32[128,8]{0,1:T(8,128)} %param.11) | copy-start | bytes 12292
  3.2 10.9 %copy-start.10 = (f32[16]{0:T(128)S(1)}, f32[16]{0:T(128)}, u32[]{:S(2)}) copy-start(f32[16]{0:T(128)} %gate_ref.11) | copy-start | bytes 196
  3.2 10.9 %copy-start.12 = (bf16[128,8]{0,1:T(8,128)(2,1)S(1)}, bf16[128,8]{0,1:T(8,128)(2,1)}, u32[]{:S(2)}) copy-start(bf16[128,8]{0,1:T(8,128)(2,1)} %param.12) | copy-start | bytes 6148
  4.0 20.6 %collective-permute-start.2 = (bf16[128,4096]{1,0:T(8,128)(2,1)S(1)}, bf16[128,4096]{1,0:T(8,128)(2,1)}, u32[]{:S(2)}, u32[]{:S(2)}) collective-permute-start(bf16[128,4096]{1,0:T(8,128)(2,1)S(1)} %shard_map.128.rows_ref.rest_0_.rest_1_), channel_id=1, source_target_pairs={{4,8},{5,9},{6,10},{7,11},{8,4},{9,5},{10,6},{11,7},{20,24},{21,25... | collective-permute-start | bytes 3145736 | tf_op jit(solution)/shard_map/ppermute | solution.py:412
  5.6 26.9 %collective-permute-start.1 = (bf16[128,4096]{1,0:T(8,128)(2,1)S(1)}, bf16[128,4096]{1,0:T(8,128)(2,1)}, u32[]{:S(2)}, u32[]{:S(2)}) collective-permute-start(bf16[128,4096]{1,0:T(8,128)(2,1)S(1)} %shard_map.128.rows_ref.rest_0_.rest_1_), channel_id=1, source_target_pairs={{0,2},{1,3},{2,0},{3,1},{4,6},{5,7},{6,4},{7,5},{8,10},{9,11},{10,... | collective-permute-start | bytes 3145736 | tf_op jit(solution)/shard_map/ppermute | solution.py:412
  8.6 30.3 %collective-permute-start = (bf16[128,4096]{1,0:T(8,128)(2,1)S(1)}, bf16[128,4096]{1,0:T(8,128)(2,1)}, u32[]{:S(2)}, u32[]{:S(2)}) collective-permute-start(bf16[128,4096]{1,0:T(8,128)(2,1)S(1)} %shard_map.128.rows_ref.rest_0_.rest_1_), channel_id=1, source_target_pairs={{0,4},{1,5},{2,6},{3,7},{4,0},{5,1},{6,2},{7,3},{8,12},{9,13},{10,... | collective-permute-start | bytes 3145736 | tf_op jit(solution)/shard_map/ppermute | solution.py:412
  14.1 1.0 copy-start.8
  17.3 23.9 %all-to-all-start = ((bf16[16,80,128]{2,1,0:T(8,128)(2,1)}), bf16[16,80,128]{2,1,0:T(8,128)(2,1)S(1)}, u32[]{:S(2)}, u32[]{:S(2)}) async-start(bf16[16,80,128]{2,1,0:T(8,128)(2,1)} %copy-done.3), calls=%async_computation | async-start | bytes 655360 | tf_op jit(solution)/shard_map/all_to_all | solution.py:509
  41.2 35.0 %collective-permute-start.6 = (bf16[128,4096]{1,0:T(8,128)(2,1)}, bf16[128,4096]{1,0:T(8,128)(2,1)}, u32[]{:S(2)}, u32[]{:S(2)}) collective-permute-start(bf16[128,4096]{1,0:T(8,128)(2,1)} %collective-permute-done.rest_0_.rest_1_), channel_id=1, source_target_pairs={{4,8},{5,9},{6,10},{7,11},{8,4},{9,5},{10,6},{11,7},{20,24},{21,25... | collective-permute-start | bytes 3145736 | tf_op jit(solution)/shard_map/ppermute | solution.py:412
  46.2 30.0 %collective-permute-start.7 = (bf16[128,4096]{1,0:T(8,128)(2,1)}, bf16[128,4096]{1,0:T(8,128)(2,1)}, u32[]{:S(2)}, u32[]{:S(2)}) collective-permute-start(bf16[128,4096]{1,0:T(8,128)(2,1)} %get-tuple-element.85), channel_id=1, source_target_pairs={{0,2},{1,3},{2,0},{3,1},{4,6},{5,7},{6,4},{7,5},{8,10},{9,11},{10,... | collective-permute-start | bytes 3145736 | tf_op jit(solution)/shard_map/ppermute | solution.py:412
  46.2 30.0 %collective-permute-start.5 = (bf16[128,4096]{1,0:T(8,128)(2,1)}, bf16[128,4096]{1,0:T(8,128)(2,1)}, u32[]{:S(2)}, u32[]{:S(2)}) collective-permute-start(bf16[128,4096]{1,0:T(8,128)(2,1)} %get-tuple-element.86), channel_id=1, source_target_pairs={{0,4},{1,5},{2,6},{3,7},{4,0},{5,1},{6,2},{7,3},{8,12},{9,13},{10,... | collective-permute-start | bytes 3145736 | tf_op jit(solution)/shard_map/ppermute | solution.py:412
  52.2 1.7 %collective-permute-start.8 = (f32[8,80,128]{2,1,0:T(8,128)S(1)}, f32[8,80,128]{2,1,0:T(8,128)S(1)}, u32[]{:S(2)}, u32[]{:S(2)}) collective-permute-start(f32[8,80,128]{2,1,0:T(8,128)S(1)} %slice.21), channel_id=1, source_target_pairs={{0,1},{1,0},{2,3},{3,2},{4,5},{5,4},{6,7},{7,6},{8,9},{9,8},{10,11... | collective-permute-start | bytes 983048 | tf_op jit(solution)/shard_map/ppermute | solution.py:412
  54.6 21.6 %all-to-all-start.1 = ((bf16[8,80,128]{2,1,0:T(8,128)(2,1)}), bf16[8,80,128]{2,1,0:T(8,128)(2,1)}, u32[]{:S(2)}, u32[]{:S(2)}) async-start(bf16[8,80,128]{2,1,0:T(8,128)(2,1)} %fusion), calls=%async_computation.1 | async-start | bytes 327680 | tf_op jit(solution)/shard_map/all_to_all | solution.py:524
  76.1 11.9 %copy-start.6 = (bf16[5,80,768]{2,1,0:T(8,128)(2,1)S(1)}, bf16[5,80,768]{2,1,0:T(8,128)(2,1)}, u32[]{:S(2)}) copy-start(bf16[5,80,768]{2,1,0:T(8,128)(2,1)} %copy-done.5) | copy-start | bytes 1843204
  78.5 29.4 %collective-permute-start.10 = (bf16[128,4096]{1,0:T(8,128)(2,1)}, bf16[128,4096]{1,0:T(8,128)(2,1)S(1)}, u32[]{:S(2)}, u32[]{:S(2)}) collective-permute-start(bf16[128,4096]{1,0:T(8,128)(2,1)} %broadcast_select_fusion), channel_id=1, source_target_pairs={{0,2},{1,3},{2,0},{3,1},{4,6},{5,7},{6,4},{7,5},{8,10},{9,11},{10,... | collective-permute-start | bytes 3145736 | tf_op jit(solution)/shard_map/ppermute | solution.py:412
  78.7 29.2 %collective-permute-start.9 = (bf16[128,4096]{1,0:T(8,128)(2,1)}, bf16[128,4096]{1,0:T(8,128)(2,1)}, u32[]{:S(2)}, u32[]{:S(2)}) collective-permute-start(bf16[128,4096]{1,0:T(8,128)(2,1)} %collective-permute-done.6.rest_5_), channel_id=1, source_target_pairs={{4,0},{5,1},{6,2},{7,3},{8,12},{9,13},{10,14},{11,15},{20,16},{21,... | collective-permute-start | bytes 3145736 | tf_op jit(solution)/shard_map/ppermute | solution.py:412
  81.6 26.3 %all-to-all-start.2 = ((bf16[8,80,128]{2,1,0:T(8,128)(2,1)}), bf16[8,80,128]{2,1,0:T(8,128)(2,1)}, u32[]{:S(2)}, u32[]{:S(2)}) async-start(bf16[8,80,128]{2,1,0:T(8,128)(2,1)} %broadcast_in_dim.4), calls=%async_computation.2 | async-start | bytes 327680 | tf_op jit(solution)/shard_map/all_to_all | solution.py:524
  104.5 0.8 copy-start.7
  105.3 9.0 %copy-start.1 = (bf16[1,16,80,768]{3,2,1,0:T(8,128)(2,1)S(1)}, bf16[1,16,80,768]{3,2,1,0:T(8,128)(2,1)}, u32[]{:S(2)}) copy-start(bf16[1,16,80,768]{3,2,1,0:T(8,128)(2,1)} %param.13) | copy-start | bytes 5898244
  107.9 6.4 %collective-permute-start.13 = (bf16[5,80,768]{2,1,0:T(8,128)(2,1)}, bf16[5,80,768]{2,1,0:T(8,128)(2,1)}, u32[]{:S(2)}, u32[]{:S(2)}) collective-permute-start(bf16[5,80,768]{2,1,0:T(8,128)(2,1)} %copy-done.7), channel_id=1, source_target_pairs={{0,1},{1,0},{2,3},{3,2},{4,5},{5,4},{6,7},{7,6},{8,9},{9,8},{10,11... | collective-permute-start | bytes 1843208 | tf_op jit(solution)/shard_map/ppermute | solution.py:412
  110.6 16.5 %collective-permute-start.12 = (bf16[64,4096]{1,0:T(8,128)(2,1)}, bf16[64,4096]{1,0:T(8,128)(2,1)}, u32[]{:S(2)}, u32[]{:S(2)}) collective-permute-start(bf16[64,4096]{1,0:T(8,128)(2,1)} %slice.18), channel_id=1, source_target_pairs={{4,0},{5,1},{6,2},{7,3},{8,12},{9,13},{10,14},{11,15},{20,16},{21,... | collective-permute-start | bytes 1572872 | tf_op jit(solution)/shard_map/ppermute | solution.py:412
  111.9 16.5 %collective-permute-start.11 = (bf16[64,4096]{1,0:T(8,128)(2,1)}, bf16[64,4096]{1,0:T(8,128)(2,1)}, u32[]{:S(2)}, u32[]{:S(2)}) collective-permute-start(bf16[64,4096]{1,0:T(8,128)(2,1)} %slice.17), channel_id=1, source_target_pairs={{0,2},{1,3},{2,0},{3,1},{12,14},{13,15},{14,12},{15,13},{16,18},{1... | collective-permute-start | bytes 1572872 | tf_op jit(solution)/shard_map/ppermute | solution.py:412
  125.0 18.1 %collective-permute-start.16 = (bf16[8,80,128]{2,1,0:T(8,128)(2,1)}, bf16[8,80,128]{2,1,0:T(8,128)(2,1)}, u32[]{:S(2)}, u32[]{:S(2)}) collective-permute-start(bf16[8,80,128]{2,1,0:T(8,128)(2,1)} %all-to-all-done.2), channel_id=1, source_target_pairs={{0,1},{1,0},{2,3},{3,2},{4,5},{5,4},{6,7},{7,6},{8,9},{9,8},{10,11... | collective-permute-start | bytes 491528 | tf_op jit(solution)/shard_map/ppermute | solution.py:412
  128.5 14.2 %copy-start.14 = (bf16[2,80,768]{2,1,0:T(8,128)(2,1)S(1)}, bf16[2,80,768]{2,1,0:T(8,128)(2,1)}, u32[]{:S(2)}) copy-start(bf16[2,80,768]{2,1,0:T(8,128)(2,1)} %copy-done.13) | copy-start | bytes 737284
  138.1 11.3 %all-to-all-start.3 = ((f32[8,8,128]{2,1,0:T(8,128)}), f32[8,8,128]{2,1,0:T(8,128)S(1)}, u32[]{:S(2)}, u32[]{:S(2)}) async-start(f32[8,8,128]{2,1,0:T(8,128)} %get-tuple-element.72), calls=%async_computation.3 | async-start | bytes 65536 | tf_op jit(solution)/shard_map/all_to_all | solution.py:524
  142.6 6.7 %collective-permute-start.14 = (bf16[1,80,768]{2,1,0:T(8,128)(2,1)S(1)}, bf16[1,80,768]{2,1,0:T(8,128)(2,1)S(1)}, u32[]{:S(2)}, u32[]{:S(2)}) collective-permute-start(bf16[1,80,768]{2,1,0:T(8,128)(2,1)S(1)} %get-tuple-element.73), channel_id=1, source_target_pairs={{0,1},{1,0},{2,3},{3,2},{4,5},{5,4},{6,7},{7,6},{8,9},{9,8},{10,11... | collective-permute-start | bytes 368648 | tf_op jit(solution)/shard_map/ppermute | solution.py:412
  142.7 2.9 %collective-permute-start.15 = (bf16[2,80,768]{2,1,0:T(8,128)(2,1)S(1)}, bf16[2,80,768]{2,1,0:T(8,128)(2,1)S(1)}, u32[]{:S(2)}, u32[]{:S(2)}) collective-permute-start(bf16[2,80,768]{2,1,0:T(8,128)(2,1)S(1)} %copy-done.14), channel_id=1, source_target_pairs={{0,1},{1,0},{2,3},{3,2},{4,5},{5,4},{6,7},{7,6},{8,9},{9,8},{10,11... | collective-permute-start | bytes 737288 | tf_op jit(solution)/shard_map/ppermute | solution.py:412
  (4 other events, 3.0 us)
